TPU v7x, 256 devices: a whole 4x4x8 slice. The times are simulated.
256 devices in a mesh: group: 8 (over z_lo, core), tensor: 32 (over y, x, z_hi).
Axes of the slice: x: 4, y: 4, z: 8 (z_hi: 2, z_lo: 4; z = z_hi * 4 + z_lo), core: 2. Of those that a mesh axis runs over, the one named last changes fastest.
Arguments:
- grad_a: float32 [8, 16, 64, 4096], P('group', None, None, 'tensor'), may hold values from -6 to 6
- grad_b: float32 [8, 16, 1536, 64], P('group', None, 'tensor'), may hold values from -6 to 6
- factor_a: float32 [16, 64, 4096], P('group', None, 'tensor'), may hold values from -6 to 6
- factor_b: float32 [16, 1536, 64], P('group', 'tensor'), may hold values from -6 to 6
- moment_a: float32 [16, 64, 4096], P('group', None, 'tensor'), may hold values from -6 to 6
- second_a: float32 [16, 64, 4096], P('group', None, 'tensor'), may hold values from 0.01 to 1
- moment_b: float32 [16, 1536, 64], P('group', 'tensor'), may hold values from -6 to 6
- second_b: float32 [16, 1536, 64], P('group', 'tensor'), may hold values from 0.01 to 1
- base_rows: bfloat16 [16, 1536, 4096], P(None, 'tensor'), may hold values from -6 to 6
Outputs:
- new_factor_a: float32 [16, 64, 4096], P('group', None, 'tensor')
- new_factor_b: float32 [16, 1536, 64], P('group', 'tensor')
- new_moment_a: float32 [16, 64, 4096], P('group', None, 'tensor')
- new_second_a: float32 [16, 64, 4096], P('group', None, 'tensor')
- new_moment_b: float32 [16, 1536, 64], P('group', 'tensor')
- new_second_b: float32 [16, 1536, 64], P('group', 'tensor')
- merged: bfloat16 [16, 1536, 4096], P(None, 'tensor')
All inputs are finite; a program needn't handle non-finite values.
Results may differ from a plain program's by a relative error of at most 0.011.
Values may be sent and summed in bfloat16 or wider, within the bound.
No kernel may reach another device: no remote copies, remote signals or barrier semaphores. Data moves between devices by JAX's collectives and lax.ppermute only.
A program may use at most 64 MiB of HBM per device.

v0:
```python
import jax
import jax.numpy as jnp
from jax import lax
from jax.sharding import PartitionSpec as P

STEP = 100


def adam_update(param, grad, first, second):
    new_first = 0.9 * first + 0.1 * grad
    new_second = 0.999 * second + 0.001 * grad * grad
    corr_first = new_first / (1.0 - 0.9**STEP)
    corr_second = new_second / (1.0 - 0.999**STEP)
    new_param = param - 0.1 * corr_first / (jnp.sqrt(corr_second) + 1e-08)
    return (new_param, new_first, new_second)


def per_device(
    grad_a, grad_b, factor_a, factor_b, moment_a, second_a, moment_b, second_b, base_rows
):
    summed_a, summed_b = (
        lax.psum_scatter(
            grad_a.astype(jnp.bfloat16), "group", scatter_dimension=1, tiled=True
        ).astype(jnp.float32),
        lax.psum_scatter(
            grad_b.astype(jnp.bfloat16), "group", scatter_dimension=1, tiled=True
        ).astype(jnp.float32),
    )
    summed_a = summed_a[0]
    summed_b = summed_b[0]
    new_a, new_ma, new_va = adam_update(factor_a, summed_a, moment_a, second_a)
    new_b, new_mb, new_vb = adam_update(factor_b, summed_b, moment_b, second_b)
    a_half = new_a.astype(jnp.bfloat16)
    b_half = new_b.astype(jnp.bfloat16)
    b_every = lax.all_gather(b_half, "group", axis=0, tiled=True)
    a_wide = lax.all_gather(a_half, "tensor", axis=2, tiled=True)
    delta = jnp.einsum(
        "efr,erd->efd",
        b_every,
        lax.all_gather(a_wide, "group", axis=0, tiled=True),
        preferred_element_type=jnp.float32,
    )
    merged = (base_rows.astype(jnp.float32) + 0.125 * delta).astype(jnp.bfloat16)
    return (new_a, new_b, new_ma, new_va, new_mb, new_vb, merged)


def solution(mesh):
    in_specs = (
        P("group", None, None, "tensor"),
        P("group", None, "tensor", None),
        P("group", None, "tensor"),
        P("group", "tensor", None),
        P("group", None, "tensor"),
        P("group", None, "tensor"),
        P("group", "tensor", None),
        P("group", "tensor", None),
        P(None, "tensor", None),
    )
    out_specs = (
        P("group", None, "tensor"),
        P("group", "tensor", None),
        P("group", None, "tensor"),
        P("group", None, "tensor"),
        P("group", "tensor", None),
        P("group", "tensor", None),
        P(None, "tensor", None),
    )
    return jax.shard_map(
        per_device, mesh=mesh, in_specs=in_specs, out_specs=out_specs, check_vma=False
    )
```

profile of v0, /device:TPU:1, one launch (start us, length us, event | category | flops | bytes accessed | tf_op | source)
XLA Modules:
  0.0 280.4 jit_solution(4845870289357603683)
XLA Ops:
  7.2 0.0 reduce-scatter.3.cloned.1.call-start
  7.2 1.8 convert_element_type.20
  9.0 0.0 reduce-scatter.3.cloned.1.call-update
  9.0 0.0 all-gather.3.cloned.1.call-start
  9.1 38.3 %reduce-scatter.3.cloned.1.call-done = bf16[1,2,64,128]{3,2,1,0:T(8,128)(2,1)} async-done(((bf16[1,16,64,128]{3,2,1,0:T(8,128)(2,1)}), bf16[1,2,64,128]{3,2,1,0:T(8,128)(2,1)}) %reduce-scatter.3.cloned.1.call-update) | async-done | bytes 32784 | tf_op jit(solution)/shard_map/reduce_scatter | solution.py:22
  47.4 1.6 fusion.4
  49.0 0.0 all-gather.3.cloned.1.call-update
  49.0 0.0 reduce-scatter.5.cloned.1.call-start
  49.1 1.7 convert_element_type.21
  50.8 0.0 reduce-scatter.5.cloned.1.call-update
  50.8 0.0 all-gather.5.cloned.1.call-start
  50.9 84.9 %all-gather.3.cloned.1.call-done = bf16[2,64,4096]{2,1,0:T(8,128)(2,1)} async-done(((bf16[2,64,128]{2,1,0:T(8,128)(2,1)}), bf16[2,64,4096]{2,1,0:T(8,128)(2,1)}) %all-gather.3.cloned.1.call-update) | async-done | bytes 1048592 | tf_op jit(solution)/shard_map/all_gather | solution.py:36
  135.7 0.0 all-gather.5.cloned.1.call-update
  135.8 32.8 %reduce-scatter.5.cloned.1.call-done = bf16[1,2,48,64]{3,2,1,0:T(8,128)(2,1)} async-done(((bf16[1,16,48,64]{3,2,1,0:T(8,128)(2,1)}), bf16[1,2,48,64]{3,2,1,0:T(8,128)(2,1)}) %reduce-scatter.5.cloned.1.call-update) | async-done | bytes 12304 | tf_op jit(solution)/shard_map/reduce_scatter | solution.py:25
  168.5 1.5 fusion.7
  170.1 17.7 %all_gather.9 = bf16[16,48,64]{2,1,0:T(8,128)(2,1)S(1)} all-gather(bf16[2,48,64]{2,1,0:T(8,128)(2,1)S(1)} %get-tuple-element.11), channel_id=1, replica_groups=mesh['group'=8,'tensor'=32] {'group'}, dimensions={0}, use_global_device_ids=true | all-gather | bytes 110592 | tf_op jit(solution)/shard_map/all_gather | solution.py:35
  187.8 76.1 %all-gather.5.cloned.1.call-done = bf16[16,64,4096]{2,1,0:T(8,128)(2,1)} async-done(((bf16[2,64,4096]{2,1,0:T(8,128)(2,1)}), bf16[16,64,4096]{2,1,0:T(8,128)(2,1)}) %all-gather.5.cloned.1.call-update) | async-done | bytes 8388624 | tf_op jit(solution)/shard_map/all_gather | solution.py:40
  263.8 10.0 %add_convert_fusion = bf16[16,48,4096]{2,1,0:T(8,128)(2,1)} fusion(bf16[16,48,4096]{2,1,0:T(8,128)(2,1)} %param.17, bf16[16,48,64]{2,1,0:T(8,128)(2,1)S(1)} %all_gather.9, bf16[16,64,4096]{2,1,0:T(8,128)(2,1)} %all-gather.5.cloned.1.call-done), kind=kOutput, calls=%fused_computation | convolution fusion | flops 415236096 | bytes 21069824 | tf_op jit(solution)/shard_map/efr,erd->efd/dot_general | solution.py:37
Async XLA Ops:
  7.2 40.2 %reduce-scatter.3.cloned.1.call-start = ((), (), s32[]{:S(2)}) async-start(), calls=%async_computation.2 | async-start | bytes 294912 | tf_op jit(solution)/shard_map/reduce_scatter | solution.py:22
  9.0 126.7 %all-gather.3.cloned.1.call-start = ((), (), s32[]{:S(2)}) async-start(), calls=%async_computation.4 | async-start | bytes 1081344 | tf_op jit(solution)/shard_map/all_gather | solution.py:36
  49.0 119.5 %reduce-scatter.5.cloned.1.call-start = ((), (), s32[]{:S(2)}) async-start(), calls=%async_computation.3 | async-start | bytes 221184 | tf_op jit(solution)/shard_map/reduce_scatter | solution.py:25
  50.8 213.0 %all-gather.5.cloned.1.call-start = ((), (), s32[]{:S(2)}) async-start(), calls=%async_computation.5 | async-start | bytes 9437184 | tf_op jit(solution)/shard_map/all_gather | solution.py:40
Sparse Core Ops, SparseCore 0:
  11.1 36.2 reduce-scatter.2
  51.7 84.0 all-gather.2
  139.0 29.5 reduce-scatter.4
  170.2 93.6 all-gather.4
where the time goes:
time: 282 us; the launch traced here: 280 us
  waiting for transfers between devices  232 us (82%)
  blocking collectives  17.7 us (6%)
  between operations  13.8 us (5%)
  matrix products  10 us (4%)
  other arithmetic  6.64 us (2%)
    all_gather x1, waiting for transfers between devices, per_device(): a_wide = lax.all_gather(a_half, 'tensor', axis=2, tiled=True)  84.9 us
    all_gather x1, waiting for transfers between devices, per_device(): lax.all_gather(a_wide, 'group', axis=0, tiled=True)  76.1 us
    reduce_scatter x1, waiting for transfers between devices, per_device(): lax.psum_scatter(grad_a.astype(jnp.bfloat16), 'group', scatter_dimension=...  38.3 us
    reduce_scatter x1, waiting for transfers between devices, per_device(): lax.psum_scatter(grad_b.astype(jnp.bfloat16), 'group', scatter_dimension=...  32.8 us
    all_gather x1, blocking collectives, per_device(): b_every = lax.all_gather(b_half, 'group', axis=0, tiled=True)  17.7 us
    dot_general x1, matrix products, per_device(): jnp.einsum('efr,erd->efd', b_every, lax.all_gather(a_wide, 'group', axis=...  10 us
  transfers between devices with their start and end apart: 4, of which 4 were waited for; matrix products, arithmetic and copies ran while one was open for 1% of the time, Pallas kernels for 0%

commit v1 on v0

v1 whole, which is shorter than its diff:
```python
import jax
import jax.numpy as jnp
from jax import lax
from jax.experimental import pallas as pl
from jax.experimental.pallas import tpu as pltpu
from jax.sharding import Mesh, PartitionSpec as P

STEP = 100
HALF = jnp.bfloat16
VMEM = pl.BlockSpec(memory_space=pltpu.VMEM)


def adam_update(param, grad, first, second):
    new_first = 0.9 * first + 0.1 * grad
    new_second = 0.999 * second + 0.001 * grad * grad
    corr_first = new_first / (1.0 - 0.9**STEP)
    corr_second = new_second / (1.0 - 0.999**STEP)
    new_param = param - 0.1 * corr_first / (jnp.sqrt(corr_second) + 1e-08)
    return (new_param, new_first, new_second)


def pack_kernel(grad_a, grad_b, out):
    out[:, 0:128, :] = grad_a[0].reshape(8, 128, 128).astype(HALF)
    for owner in range(8):
        pair = jnp.concatenate([grad_b[0, 2 * owner], grad_b[0, 2 * owner + 1]], axis=-1)
        out[owner, 128:176, :] = pair.astype(HALF)


def update_kernel(
    got, factor_a, factor_b, moment_a, second_a, moment_b, second_b,
    new_a, new_b, new_ma, new_va, new_mb, new_vb, send,
):
    total = got[0].astype(jnp.float32)
    for learner in range(1, 8):
        total = total + got[learner].astype(jnp.float32)
    grad_a = total[0:128].reshape(2, 64, 128)
    a, ma, va = adam_update(factor_a[...], grad_a, moment_a[...], second_a[...])
    new_a[...] = a
    new_ma[...] = ma
    new_va[...] = va
    halves = []
    for expert in range(2):
        grad_b = total[128:176, 64 * expert : 64 * expert + 64]
        b, mb, vb = adam_update(factor_b[expert], grad_b, moment_b[expert], second_b[expert])
        new_b[expert] = b
        new_mb[expert] = mb
        new_vb[expert] = vb
        halves.append(b)
    a_half = a.astype(HALF).reshape(128, 128)
    b_half = jnp.concatenate(halves, axis=-1).astype(HALF)
    for peer in range(8):
        send[peer, 0:128, :] = a_half
        send[peer, 128:176, :] = b_half


def merge_kernel(place, b_own, b_sibling, base, *rest):
    pieces = rest[:16]
    out, blocks = rest[16:]
    x, core = place[0], place[2]
    ky = pl.program_id(0)

    @pl.when(ky == 0)
    def _():
        blocks[...] = jnp.zeros_like(blocks)
        for side, rows in ((0, b_own), (1, b_sibling)):
            for h in range(2):
                for zl in range(4):
                    blocks[side, h, 48 * zl : 48 * zl + 48, 64 * zl : 64 * zl + 64] = rows[
                        zl, :, 64 * h : 64 * h + 64
                    ]

    def one(step):
        for kx in range(4):
            column = pl.multiple_of(lax.rem(x + 4 - kx, 4) * 256, 256)
            for side in range(2):
                for h in range(2):
                    if h == 0:
                        piece = pieces[8 * side + step][kx]
                    else:
                        piece = pieces[8 * side + 4 + kx][step]
                    wide = jnp.concatenate(
                        [piece[:, 0].reshape(256, 128), piece[:, 1].reshape(256, 128)], axis=-1
                    )
                    delta = jnp.dot(
                        blocks[side, h], wide, preferred_element_type=jnp.float32
                    ).reshape(4, 48, 256)
                    which = (core if side == 0 else 1 - core) * 2 + h
                    old = base[:, which, :, pl.ds(column, 256)].astype(jnp.float32)
                    out[:, which, :, pl.ds(column, 256)] = (old + 0.125 * delta).astype(HALF)

    for step in range(4):
        pl.when(ky == step)(lambda step=step: one(step))


def per_device(
    grad_a, grad_b, factor_a, factor_b, moment_a, second_a, moment_b, second_b, base_rows
):
    f32 = jnp.float32
    shape = jax.ShapeDtypeStruct
    packed = pl.pallas_call(
        pack_kernel,
        out_shape=shape((8, 176, 128), HALF),
        in_specs=[VMEM] * 2,
        out_specs=VMEM,
    )(grad_a, grad_b)
    got = lax.all_to_all(packed, ("zl", "core"), 0, 0, tiled=True)
    sa, sb = shape((2, 64, 128), f32), shape((2, 48, 64), f32)
    new_a, new_b, new_ma, new_va, new_mb, new_vb, send = pl.pallas_call(
        update_kernel,
        out_shape=(sa, sb, sa, sa, sb, sb, shape((8, 176, 128), HALF)),
        in_specs=[VMEM] * 7,
        out_specs=[VMEM] * 7,
    )(got, factor_a, factor_b, moment_a, second_a, moment_b, second_b)
    line = lax.all_to_all(send, ("zl", "zh"), 0, 0, tiled=True)

    def hop(value, axis, k):
        n = lax.axis_size(axis)
        return lax.ppermute(value, axis, [(i, (i + k) % n) for i in range(n)])

    def spread(value, axis):
        return [value] + [hop(value, axis, k) for k in (1, 2, 3)]

    x, y, core, zh = (lax.axis_index(a) for a in ("x", "y", "core", "zh"))
    one = jnp.stack(spread(line[:, 0:64], "x"))
    two = jnp.stack(spread(line[:, 64:128], "y"))
    b_own = lax.dynamic_index_in_dim(
        line.reshape(4, 2, 176, 128)[:, :, 128:176], zh, axis=1, keepdims=False
    )
    pieces = spread(one, "y") + spread(two, "x")
    pieces = pieces + [hop(p, "core", 1) for p in pieces]
    b_sibling = hop(b_own, "core", 1)
    pieces = [p.reshape(4, 4, 2, 64, 128) for p in pieces]
    place = jnp.stack([x, y, core]).astype(jnp.int32)
    block = pl.BlockSpec(
        (4, 4, 48, 1024), lambda ky, place: (0, 0, 0, lax.rem(place[1] + 4 - ky, 4))
    )
    merged = pl.pallas_call(
        merge_kernel,
        out_shape=shape((4, 4, 48, 4096), HALF),
        grid_spec=pltpu.PrefetchScalarGridSpec(
            num_scalar_prefetch=1,
            grid=(4,),
            in_specs=[VMEM, VMEM, block] + [VMEM] * 16,
            out_specs=block,
            scratch_shapes=[pltpu.VMEM((2, 2, 192, 256), HALF)],
        ),
        compiler_params=pltpu.CompilerParams(vmem_limit_bytes=40 * 1024 * 1024),
    )(place, b_own, b_sibling, base_rows.reshape(4, 4, 48, 4096), *pieces)
    return (new_a, new_b, new_ma, new_va, new_mb, new_vb, merged.reshape(16, 48, 4096))


def solution(mesh):
    fine = Mesh(mesh.devices.reshape(4, 2, 4, 4, 2), ("zl", "core", "y", "x", "zh"))
    group, tensor = ("zl", "core"), ("y", "x", "zh")
    in_specs = (
        P(group, None, None, tensor),
        P(group, None, tensor, None),
        P(group, None, tensor),
        P(group, tensor, None),
        P(group, None, tensor),
        P(group, None, tensor),
        P(group, tensor, None),
        P(group, tensor, None),
        P(None, tensor, None),
    )
    out_specs = (
        P(group, None, tensor),
        P(group, tensor, None),
        P(group, None, tensor),
        P(group, None, tensor),
        P(group, tensor, None),
        P(group, tensor, None),
        P(None, tensor, None),
    )
    return jax.shard_map(
        per_device, mesh=fine, in_specs=in_specs, out_specs=out_specs, check_vma=False
    )
```

time: 282 us -> 140 us (0.50)
  waiting for transfers between devices: 232 us -> 56.3 us
  starting transfers between devices: 0.16 us -> 27.9 us
  blocking collectives: 17.7 us -> 35.1 us
  between operations: 13.8 us -> 0.77 us
  Pallas kernels: 0 us -> 12.8 us
  matrix products: 10 us -> 0 us
    all_gather x2 -> x0, waiting for transfers between devices: 161 us -> none  [the longest x1 84.9 us: per_device(): a_wide = lax.all_gather(a_half, 'tensor', axis=2, tiled=True)]
    reduce_scatter x2 -> x0, waiting for transfers between devices: 71.1 us -> none  [the longest x1 38.3 us: per_device(): lax.psum_scatter(grad_a.astype(jnp.bfloat16), 'group', scatter_dimension=...]
    ppermute x0 -> x21, waiting for transfers between devices: none -> 56.3 us  [hop(): return lax.ppermute(value, axis, [(i, (i + k) % n) for i in range(n)])]
    all_to_all x0 -> x2, blocking collectives: none -> 35.1 us  [the longest x1 18.5 us: per_device(): got = lax.all_to_all(packed, ('zl', 'core'), 0, 0, tiled=True)]
    ppermute x0 -> x21, starting transfers between devices: none -> 27.9 us  [hop(): return lax.ppermute(value, axis, [(i, (i + k) % n) for i in range(n)])]
    all_gather x1 -> x0, blocking collectives: 17.7 us -> none  [per_device(): b_every = lax.all_gather(b_half, 'group', axis=0, tiled=True)]
    pallas_call x0 -> x3, Pallas kernels: none -> 12.8 us  [the longest x1 8.76 us: per_device(): pl.pallas_call(merge_kernel, out_shape=shape((4, 4, 48, 4096), HALF), gri...]
    dot_general x1 -> x0, matrix products: 10 us -> none  [per_device(): jnp.einsum('efr,erd->efd', b_every, lax.all_gather(a_wide, 'group', axis=...]
  transfers between devices with their start and end apart: 4 -> 21, of which waited for: 4 -> 8; matrix products, arithmetic and copies ran while one was open for 1% -> 2% of each run, Pallas kernels for 0% -> 0%
where the time goes in v1:
time: 140 us; the launch traced here: 139 us
  waiting for transfers between devices  56.3 us (40%)
  blocking collectives  35.1 us (25%)
  starting transfers between devices  27.9 us (20%)
  Pallas kernels  12.8 us (9%)
  other arithmetic  4.11 us (3%)
  local copies, waits for them, and re-layouts  1.97 us (1%)
    ppermute x21, waiting for transfers between devices, hop(): return lax.ppermute(value, axis, [(i, (i + k) % n) for i in range(n)])  56.3 us
    ppermute x21, starting transfers between devices, hop(): return lax.ppermute(value, axis, [(i, (i + k) % n) for i in range(n)])  27.9 us
    all_to_all x1, blocking collectives, per_device(): got = lax.all_to_all(packed, ('zl', 'core'), 0, 0, tiled=True)  18.5 us
    all_to_all x1, blocking collectives, per_device(): line = lax.all_to_all(send, ('zl', 'zh'), 0, 0, tiled=True)  16.5 us
    pallas_call x1, Pallas kernels, per_device(): pl.pallas_call(merge_kernel, out_shape=shape((4, 4, 48, 4096), HALF), gri...  8.76 us
  transfers between devices with their start and end apart: 21, of which 8 were waited for; matrix products, arithmetic and copies ran while one was open for 2% of the time, Pallas kernels for 0%

profile of v1, /device:TPU:1, one launch (start us, length us, event | category | flops | bytes accessed | tf_op | source)
XLA Modules:
  0.0 138.9 jit_solution(347413894866041960)
XLA Ops:
  0.6 2.0 %shard_map.144 = bf16[8,176,128]{2,1,0:T(8,128)(2,1)} custom-call(f32[1,16,64,128]{3,2,1,0:T(8,128)} %grad_a.1, f32[1,16,48,64]{3,2,1,0:T(8,128)} %grad_b.1), custom_call_target="tpu_custom_call" | custom-call | tf_op jit(solution)/shard_map/pallas_call | solution.py:100
  2.6 18.5 %all_to_all.10.got = bf16[8,176,128]{2,1,0:T(8,128)(2,1)} all-to-all(bf16[8,176,128]{2,1,0:T(8,128)(2,1)} %shard_map.144), channel_id=1, replica_groups=mesh['zl'=4,'core'=2,'y'=4,'x'=4,'zh'=2] {'zl','core'}, dimensions={0} | all-to-all | bytes 720896 | tf_op jit(solution)/shard_map/all_to_all | solution.py:106
  21.2 2.1 %shard_map.145 = (f32[2,64,128]{2,1,0:T(8,128)}, f32[2,48,64]{2,1,0:T(8,128)}, f32[2,64,128]{2,1,0:T(8,128)}, f32[2,64,128]{2,1,0:T(8,128)}, f32[2,48,64]{2,1,0:...) custom-call(bf16[8,176,128]{2,1,0:T(8,128)(2,1)} %all_to_all.10.got, f32[2,64,128]{2,1,0:T(8,128)} %factor_a.1, ...), custom_call_target="tpu_custom_call" | custom-call | tf_op jit(solution)/shard_map/pallas_call | solution.py:108
  23.2 16.5 %all_to_all.11 = bf16[8,176,128]{2,1,0:T(8,128)(2,1)S(1)} all-to-all(bf16[8,176,128]{2,1,0:T(8,128)(2,1)} %get-tuple-element.20), channel_id=1, replica_groups=mesh['zl'=4,'core'=2,'y'=4,'x'=4,'zh'=2] {'zl','zh'}, dimensions={0} | all-to-all | bytes 720896 | tf_op jit(solution)/shard_map/all_to_all | solution.py:114
  39.7 0.1 slice_bitcast_fusion
  39.8 2.8 %collective-permute-start.9 = (bf16[8,64,128]{2,1,0:T(8,128)(2,1)S(1)}, bf16[8,64,128]{2,1,0:T(8,128)(2,1)S(1)}, u32[]{:S(2)}, u32[]{:S(2)}) collective-permute-start(bf16[8,64,128]{2,1,0:T(8,128)(2,1)S(1)} %get-tuple-element.23), channel_id=1, source_target_pairs={{0,24},{8,0},{16,8},{24,16},{1,25},{9,1},{17,9},{25,17},{2,26},{10... | collective-permute-start | bytes 393224 | tf_op jit(solution)/shard_map/ppermute | solution.py:118
  42.7 0.3 collective-permute-start.8
  43.0 0.7 collective-permute-start.7
  43.7 2.3 %collective-permute-done.9 = bf16[8,64,128]{2,1,0:T(8,128)(2,1)S(1)} collective-permute-done((bf16[8,64,128]{2,1,0:T(8,128)(2,1)S(1)}, bf16[8,64,128]{2,1,0:T(8,128)(2,1)S(1)}, u32[]{:S(2)}, u32[]{:S(2)}) %collective-permute-start.9) | collective-permute-done | bytes 131104 | tf_op jit(solution)/shard_map/ppermute | solution.py:118
  46.0 0.0 copy-start.2
  46.0 2.1 %collective-permute-done.8 = bf16[8,64,128]{2,1,0:T(8,128)(2,1)S(1)} collective-permute-done((bf16[8,64,128]{2,1,0:T(8,128)(2,1)S(1)}, bf16[8,64,128]{2,1,0:T(8,128)(2,1)S(1)}, u32[]{:S(2)}, u32[]{:S(2)}) %collective-permute-start.8) | collective-permute-done | bytes 131104 | tf_op jit(solution)/shard_map/ppermute | solution.py:118
  48.1 0.0 copy-start.3
  48.1 1.3 collective-permute-done.7
  49.4 0.0 copy-start.4
  49.4 0.9 pad_maximum_fusion.3
  50.2 4.6 %collective-permute-start.17 = (bf16[4,8,64,128]{3,2,1,0:T(8,128)(2,1)}, bf16[4,8,64,128]{3,2,1,0:T(8,128)(2,1)S(1)}, u32[]{:S(2)}, u32[]{:S(2)}) collective-permute-start(bf16[4,8,64,128]{3,2,1,0:T(8,128)(2,1)} %pad_maximum_fusion.3), channel_id=1, source_target_pairs={{0,32},{32,0},{1,33},{33,1},{2,34},{34,2},{3,35},{35,3},{4,36},{36... | collective-permute-start | bytes 1572872 | tf_op jit(solution)/shard_map/ppermute | solution.py:118
  54.9 2.5 %collective-permute-start.12 = (bf16[4,8,64,128]{3,2,1,0:T(8,128)(2,1)}, bf16[4,8,64,128]{3,2,1,0:T(8,128)(2,1)S(1)}, u32[]{:S(2)}, u32[]{:S(2)}) collective-permute-start(bf16[4,8,64,128]{3,2,1,0:T(8,128)(2,1)} %pad_maximum_fusion.3), channel_id=1, source_target_pairs={{0,6},{2,0},{4,2},{6,4},{1,7},{3,1},{5,3},{7,5},{8,14},{10,8},{12,... | collective-permute-start | bytes 1572872 | tf_op jit(solution)/shard_map/ppermute | solution.py:118
  57.4 0.5 collective-permute-start.11
  57.9 0.6 collective-permute-start.10
  58.5 2.1 %collective-permute-start.3 = (bf16[8,64,128]{2,1,0:T(8,128)(2,1)S(1)}, bf16[8,64,128]{2,1,0:T(8,128)(2,1)S(1)}, u32[]{:S(2)}, u32[]{:S(2)}) collective-permute-start(bf16[8,64,128]{2,1,0:T(8,128)(2,1)S(1)} %get-tuple-element.24), channel_id=1, source_target_pairs={{0,6},{2,0},{4,2},{6,4},{1,7},{3,1},{5,3},{7,5},{8,14},{10,8},{12,... | collective-permute-start | bytes 393224 | tf_op jit(solution)/shard_map/ppermute | solution.py:118
  60.6 22.4 %collective-permute-done.3 = bf16[8,64,128]{2,1,0:T(8,128)(2,1)S(1)} collective-permute-done((bf16[8,64,128]{2,1,0:T(8,128)(2,1)S(1)}, bf16[8,64,128]{2,1,0:T(8,128)(2,1)S(1)}, u32[]{:S(2)}, u32[]{:S(2)}) %collective-permute-start.3) | collective-permute-done | bytes 131104 | tf_op jit(solution)/shard_map/ppermute | solution.py:118
  83.0 2.5 %collective-permute-start.2 = (bf16[8,64,128]{2,1,0:T(8,128)(2,1)S(1)}, bf16[8,64,128]{2,1,0:T(8,128)(2,1)S(1)}, u32[]{:S(2)}, u32[]{:S(2)}) collective-permute-start(bf16[8,64,128]{2,1,0:T(8,128)(2,1)S(1)} %get-tuple-element.24), channel_id=1, source_target_pairs={{0,4},{2,6},{4,0},{6,2},{1,5},{3,7},{5,1},{7,3},{8,12},{10,14},{12... | collective-permute-start | bytes 393224 | tf_op jit(solution)/shard_map/ppermute | solution.py:118
  85.5 3.2 %collective-permute-done.2 = bf16[8,64,128]{2,1,0:T(8,128)(2,1)S(1)} collective-permute-done((bf16[8,64,128]{2,1,0:T(8,128)(2,1)S(1)}, bf16[8,64,128]{2,1,0:T(8,128)(2,1)S(1)}, u32[]{:S(2)}, u32[]{:S(2)}) %collective-permute-start.2) | collective-permute-done | bytes 131104 | tf_op jit(solution)/shard_map/ppermute | solution.py:118
  88.7 1.1 collective-permute-start.1
  89.9 4.7 %collective-permute-done.1 = bf16[8,64,128]{2,1,0:T(8,128)(2,1)} collective-permute-done((bf16[8,64,128]{2,1,0:T(8,128)(2,1)S(1)}, bf16[8,64,128]{2,1,0:T(8,128)(2,1)}, u32[]{:S(2)}, u32[]{:S(2)}) %collective-permute-start.1) | collective-permute-done | bytes 131104 | tf_op jit(solution)/shard_map/ppermute | solution.py:118
  94.6 2.5 %collective-permute-start = (bf16[4,48,128]{2,1,0:T(8,128)(2,1)S(1)}, bf16[4,48,128]{2,1,0:T(8,128)(2,1)S(1)}, u32[]{:S(2)}, u32[]{:S(2)}) collective-permute-start(bf16[4,48,128]{2,1,0:T(8,128)(2,1)S(1)} %dynamic-slice_bitcast_fusion.b_own), channel_id=1, source_target_pairs={{0,32},{32,0},{1,33},{33,1},{2,34},{34,2},{3,35},{35,3},{4,36},{36... | collective-permute-start | bytes 147464 | tf_op jit(solution)/shard_map/ppermute | solution.py:118
  97.1 1.0 pad_maximum_fusion.1
  98.1 0.0 copy-done.3
  98.1 0.0 copy-done.4
  98.1 0.0 copy-done.5
  98.1 0.0 collective-permute-done.b_sibling
  98.1 0.2 collective-permute-start.13
  98.4 0.0 copy-done.2
  98.4 0.0 copy-done.6
  98.4 0.0 collective-permute-done.17
  98.4 0.4 collective-permute-start.6
  98.7 0.0 collective-permute-done.12
  98.7 0.3 collective-permute-start.5
  99.1 0.0 collective-permute-done.11
  99.1 0.9 collective-permute-start.4
  100.0 0.0 collective-permute-done.10
  100.0 0.9 collective-permute-start.20
  100.9 0.0 collective-permute-done.13
  101.0 0.1 collective-permute-start.19
  101.0 10.6 %collective-permute-done.6 = bf16[4,8,64,128]{3,2,1,0:T(8,128)(2,1)S(1)} collective-permute-done((bf16[4,8,64,128]{3,2,1,0:T(8,128)(2,1)S(1)}, bf16[4,8,64,128]{3,2,1,0:T(8,128)(2,1)S(1)}, u32[]{:S(2)}, u32[]{:S(2)}) %collective-permute-start.6) | collective-permute-done | bytes 524320 | tf_op jit(solution)/shard_map/ppermute | solution.py:118
  111.7 1.9 %collective-permute-start.18 = (bf16[4,8,64,128]{3,2,1,0:T(8,128)(2,1)S(1)}, bf16[4,8,64,128]{3,2,1,0:T(8,128)(2,1)}, u32[]{:S(2)}, u32[]{:S(2)}) collective-permute-start(bf16[4,8,64,128]{3,2,1,0:T(8,128)(2,1)S(1)} %collective-permute-done.10), channel_id=1, source_target_pairs={{0,32},{32,0},{1,33},{33,1},{2,34},{34,2},{3,35},{35,3},{4,36},{36... | collective-permute-start | bytes 1572872 | tf_op jit(solution)/shard_map/ppermute | solution.py:118
  113.6 0.0 collective-permute-done.5
  113.6 2.3 %collective-permute-start.16 = (bf16[4,8,64,128]{3,2,1,0:T(8,128)(2,1)S(1)}, bf16[4,8,64,128]{3,2,1,0:T(8,128)(2,1)}, u32[]{:S(2)}, u32[]{:S(2)}) collective-permute-start(bf16[4,8,64,128]{3,2,1,0:T(8,128)(2,1)S(1)} %collective-permute-done.6), channel_id=1, source_target_pairs={{0,32},{32,0},{1,33},{33,1},{2,34},{34,2},{3,35},{35,3},{4,36},{36... | collective-permute-start | bytes 1572872 | tf_op jit(solution)/shard_map/ppermute | solution.py:118
  115.9 9.6 %collective-permute-done.4 = bf16[4,8,64,128]{3,2,1,0:T(8,128)(2,1)} collective-permute-done((bf16[4,8,64,128]{3,2,1,0:T(8,128)(2,1)S(1)}, bf16[4,8,64,128]{3,2,1,0:T(8,128)(2,1)}, u32[]{:S(2)}, u32[]{:S(2)}) %collective-permute-start.4) | collective-permute-done | bytes 524320 | tf_op jit(solution)/shard_map/ppermute | solution.py:118
  125.4 0.5 collective-permute-start.15
  125.9 0.0 collective-permute-done.20
  125.9 0.8 copy-done
  126.7 0.0 collective-permute-start.14
  126.7 0.1 pad_add_fusion.place
  126.8 1.1 pad_maximum_fusion.rest_0_
  127.9 1.1 pad_maximum_fusion.2.rest_4_
  129.0 0.0 collective-permute-done.19
  129.0 0.0 collective-permute-done.18
  129.0 0.0 collective-permute-done.16
  129.0 0.0 collective-permute-done.15
  129.1 0.0 collective-permute-done.14
  129.1 0.0 copy-start.1
  129.1 1.0 copy-done.1
  130.1 8.8 %shard_map.146 = bf16[4,4,48,4096]{3,2,1,0:T(8,128)(2,1)} custom-call(s32[3]{0:T(128)S(1)} %pad_add_fusion.place, bf16[4,48,128]{2,1,0:T(8,128)(2,1)S(1)} %dynamic-slice_bitcast_fusion.b_own, bf16[4,48,128]{2,1,0:T(8,128)(2,1)S(1)} %collective-permute-done.b_sibling, bf16[4,4,48,4096]{3,2,1,0:T(8,128)(2,1)} %bitcast.49, ...), custom_call_target="tpu_custom_call" | custom-call | tf_op jit(solution)/shard_map/pallas_call | solution.py:137
  (5 shorter events, 0.0 us)
Async XLA Ops:
  39.8 6.1 %collective-permute-start.9 = (bf16[8,64,128]{2,1,0:T(8,128)(2,1)S(1)}, bf16[8,64,128]{2,1,0:T(8,128)(2,1)S(1)}, u32[]{:S(2)}, u32[]{:S(2)}) collective-permute-start(bf16[8,64,128]{2,1,0:T(8,128)(2,1)S(1)} %get-tuple-element.23), channel_id=1, source_target_pairs={{0,24},{8,0},{16,8},{24,16},{1,25},{9,1},{17,9},{25,17},{2,26},{10... | collective-permute-start | bytes 393224 | tf_op jit(solution)/shard_map/ppermute | solution.py:118
  42.7 5.4 %collective-permute-start.8 = (bf16[8,64,128]{2,1,0:T(8,128)(2,1)S(1)}, bf16[8,64,128]{2,1,0:T(8,128)(2,1)S(1)}, u32[]{:S(2)}, u32[]{:S(2)}) collective-permute-start(bf16[8,64,128]{2,1,0:T(8,128)(2,1)S(1)} %get-tuple-element.23), channel_id=1, source_target_pairs={{0,16},{8,24},{16,0},{24,8},{1,17},{9,25},{17,1},{25,9},{2,18},{10... | collective-permute-start | bytes 393224 | tf_op jit(solution)/shard_map/ppermute | solution.py:118
  43.0 6.4 %collective-permute-start.7 = (bf16[8,64,128]{2,1,0:T(8,128)(2,1)S(1)}, bf16[8,64,128]{2,1,0:T(8,128)(2,1)S(1)}, u32[]{:S(2)}, u32[]{:S(2)}) collective-permute-start(bf16[8,64,128]{2,1,0:T(8,128)(2,1)S(1)} %get-tuple-element.23), channel_id=1, source_target_pairs={{0,8},{8,16},{16,24},{24,0},{1,9},{9,17},{17,25},{25,1},{2,10},{10... | collective-permute-start | bytes 393224 | tf_op jit(solution)/shard_map/ppermute | solution.py:118
  46.0 52.4 %copy-start.2 = (bf16[8,64,128]{2,1,0:T(8,128)(2,1)}, bf16[8,64,128]{2,1,0:T(8,128)(2,1)S(1)}, u32[]{:S(2)}) copy-start(bf16[8,64,128]{2,1,0:T(8,128)(2,1)S(1)} %collective-permute-done.9) | copy-start | bytes 393220
  48.1 50.0 %copy-start.3 = (bf16[8,64,128]{2,1,0:T(8,128)(2,1)}, bf16[8,64,128]{2,1,0:T(8,128)(2,1)S(1)}, u32[]{:S(2)}) copy-start(bf16[8,64,128]{2,1,0:T(8,128)(2,1)S(1)} %collective-permute-done.8) | copy-start | bytes 393220
  49.4 48.7 %copy-start.4 = (bf16[8,64,128]{2,1,0:T(8,128)(2,1)}, bf16[8,64,128]{2,1,0:T(8,128)(2,1)S(1)}, u32[]{:S(2)}) copy-start(bf16[8,64,128]{2,1,0:T(8,128)(2,1)S(1)} %collective-permute-done.7) | copy-start | bytes 393220
  50.2 48.1 %collective-permute-start.17 = (bf16[4,8,64,128]{3,2,1,0:T(8,128)(2,1)}, bf16[4,8,64,128]{3,2,1,0:T(8,128)(2,1)S(1)}, u32[]{:S(2)}, u32[]{:S(2)}) collective-permute-start(bf16[4,8,64,128]{3,2,1,0:T(8,128)(2,1)} %pad_maximum_fusion.3), channel_id=1, source_target_pairs={{0,32},{32,0},{1,33},{33,1},{2,34},{34,2},{3,35},{35,3},{4,36},{36... | collective-permute-start | bytes 1572872 | tf_op jit(solution)/shard_map/ppermute | solution.py:118
  54.9 43.9 %collective-permute-start.12 = (bf16[4,8,64,128]{3,2,1,0:T(8,128)(2,1)}, bf16[4,8,64,128]{3,2,1,0:T(8,128)(2,1)S(1)}, u32[]{:S(2)}, u32[]{:S(2)}) collective-permute-start(bf16[4,8,64,128]{3,2,1,0:T(8,128)(2,1)} %pad_maximum_fusion.3), channel_id=1, source_target_pairs={{0,6},{2,0},{4,2},{6,4},{1,7},{3,1},{5,3},{7,5},{8,14},{10,8},{12,... | collective-permute-start | bytes 1572872 | tf_op jit(solution)/shard_map/ppermute | solution.py:118
  57.4 41.7 %collective-permute-start.11 = (bf16[4,8,64,128]{3,2,1,0:T(8,128)(2,1)}, bf16[4,8,64,128]{3,2,1,0:T(8,128)(2,1)S(1)}, u32[]{:S(2)}, u32[]{:S(2)}) collective-permute-start(bf16[4,8,64,128]{3,2,1,0:T(8,128)(2,1)} %pad_maximum_fusion.3), channel_id=1, source_target_pairs={{0,4},{2,6},{4,0},{6,2},{1,5},{3,7},{5,1},{7,3},{8,12},{10,14},{12... | collective-permute-start | bytes 1572872 | tf_op jit(solution)/shard_map/ppermute | solution.py:118
  57.9 42.1 %collective-permute-start.10 = (bf16[4,8,64,128]{3,2,1,0:T(8,128)(2,1)}, bf16[4,8,64,128]{3,2,1,0:T(8,128)(2,1)S(1)}, u32[]{:S(2)}, u32[]{:S(2)}) collective-permute-start(bf16[4,8,64,128]{3,2,1,0:T(8,128)(2,1)} %pad_maximum_fusion.3), channel_id=1, source_target_pairs={{0,2},{2,4},{4,6},{6,0},{1,3},{3,5},{5,7},{7,1},{8,10},{10,12},{12... | collective-permute-start | bytes 1572872 | tf_op jit(solution)/shard_map/ppermute | solution.py:118
  58.5 24.5 %collective-permute-start.3 = (bf16[8,64,128]{2,1,0:T(8,128)(2,1)S(1)}, bf16[8,64,128]{2,1,0:T(8,128)(2,1)S(1)}, u32[]{:S(2)}, u32[]{:S(2)}) collective-permute-start(bf16[8,64,128]{2,1,0:T(8,128)(2,1)S(1)} %get-tuple-element.24), channel_id=1, source_target_pairs={{0,6},{2,0},{4,2},{6,4},{1,7},{3,1},{5,3},{7,5},{8,14},{10,8},{12,... | collective-permute-start | bytes 393224 | tf_op jit(solution)/shard_map/ppermute | solution.py:118
  83.0 15.2 %copy-start.5 = (bf16[8,64,128]{2,1,0:T(8,128)(2,1)}, bf16[8,64,128]{2,1,0:T(8,128)(2,1)S(1)}, u32[]{:S(2)}) copy-start(bf16[8,64,128]{2,1,0:T(8,128)(2,1)S(1)} %collective-permute-done.3) | copy-start | bytes 393220
  83.0 5.7 %collective-permute-start.2 = (bf16[8,64,128]{2,1,0:T(8,128)(2,1)S(1)}, bf16[8,64,128]{2,1,0:T(8,128)(2,1)S(1)}, u32[]{:S(2)}, u32[]{:S(2)}) collective-permute-start(bf16[8,64,128]{2,1,0:T(8,128)(2,1)S(1)} %get-tuple-element.24), channel_id=1, source_target_pairs={{0,4},{2,6},{4,0},{6,2},{1,5},{3,7},{5,1},{7,3},{8,12},{10,14},{12... | collective-permute-start | bytes 393224 | tf_op jit(solution)/shard_map/ppermute | solution.py:118
  88.7 9.7 %copy-start.6 = (bf16[8,64,128]{2,1,0:T(8,128)(2,1)}, bf16[8,64,128]{2,1,0:T(8,128)(2,1)S(1)}, u32[]{:S(2)}) copy-start(bf16[8,64,128]{2,1,0:T(8,128)(2,1)S(1)} %collective-permute-done.2) | copy-start | bytes 393220
  88.7 5.9 %collective-permute-start.1 = (bf16[8,64,128]{2,1,0:T(8,128)(2,1)S(1)}, bf16[8,64,128]{2,1,0:T(8,128)(2,1)}, u32[]{:S(2)}, u32[]{:S(2)}) collective-permute-start(bf16[8,64,128]{2,1,0:T(8,128)(2,1)S(1)} %get-tuple-element.24), channel_id=1, source_target_pairs={{0,2},{2,4},{4,6},{6,0},{1,3},{3,5},{5,7},{7,1},{8,10},{10,12},{12... | collective-permute-start | bytes 393224 | tf_op jit(solution)/shard_map/ppermute | solution.py:118
  94.6 3.5 %collective-permute-start = (bf16[4,48,128]{2,1,0:T(8,128)(2,1)S(1)}, bf16[4,48,128]{2,1,0:T(8,128)(2,1)S(1)}, u32[]{:S(2)}, u32[]{:S(2)}) collective-permute-start(bf16[4,48,128]{2,1,0:T(8,128)(2,1)S(1)} %dynamic-slice_bitcast_fusion.b_own), channel_id=1, source_target_pairs={{0,32},{32,0},{1,33},{33,1},{2,34},{34,2},{3,35},{35,3},{4,36},{36... | collective-permute-start | bytes 147464 | tf_op jit(solution)/shard_map/ppermute | solution.py:118
  98.1 2.8 %collective-permute-start.13 = (bf16[4,8,64,128]{3,2,1,0:T(8,128)(2,1)S(1)}, bf16[4,8,64,128]{3,2,1,0:T(8,128)(2,1)S(1)}, u32[]{:S(2)}, u32[]{:S(2)}) collective-permute-start(bf16[4,8,64,128]{3,2,1,0:T(8,128)(2,1)S(1)} %pad_maximum_fusion.1), channel_id=1, source_target_pairs={{0,32},{32,0},{1,33},{33,1},{2,34},{34,2},{3,35},{35,3},{4,36},{36... | collective-permute-start | bytes 1572872 | tf_op jit(solution)/shard_map/ppermute | solution.py:118
  98.4 13.3 %collective-permute-start.6 = (bf16[4,8,64,128]{3,2,1,0:T(8,128)(2,1)S(1)}, bf16[4,8,64,128]{3,2,1,0:T(8,128)(2,1)S(1)}, u32[]{:S(2)}, u32[]{:S(2)}) collective-permute-start(bf16[4,8,64,128]{3,2,1,0:T(8,128)(2,1)S(1)} %pad_maximum_fusion.1), channel_id=1, source_target_pairs={{0,24},{8,0},{16,8},{24,16},{1,25},{9,1},{17,9},{25,17},{2,26},{10... | collective-permute-start | bytes 1572872 | tf_op jit(solution)/shard_map/ppermute | solution.py:118
  98.7 14.9 %collective-permute-start.5 = (bf16[4,8,64,128]{3,2,1,0:T(8,128)(2,1)S(1)}, bf16[4,8,64,128]{3,2,1,0:T(8,128)(2,1)}, u32[]{:S(2)}, u32[]{:S(2)}) collective-permute-start(bf16[4,8,64,128]{3,2,1,0:T(8,128)(2,1)S(1)} %pad_maximum_fusion.1), channel_id=1, source_target_pairs={{0,16},{8,24},{16,0},{24,8},{1,17},{9,25},{17,1},{25,9},{2,18},{10... | collective-permute-start | bytes 1572872 | tf_op jit(solution)/shard_map/ppermute | solution.py:118
  99.1 26.3 %collective-permute-start.4 = (bf16[4,8,64,128]{3,2,1,0:T(8,128)(2,1)S(1)}, bf16[4,8,64,128]{3,2,1,0:T(8,128)(2,1)}, u32[]{:S(2)}, u32[]{:S(2)}) collective-permute-start(bf16[4,8,64,128]{3,2,1,0:T(8,128)(2,1)S(1)} %pad_maximum_fusion.1), channel_id=1, source_target_pairs={{0,8},{8,16},{16,24},{24,0},{1,9},{9,17},{17,25},{25,1},{2,10},{10... | collective-permute-start | bytes 1572872 | tf_op jit(solution)/shard_map/ppermute | solution.py:118
  100.0 25.9 %collective-permute-start.20 = (bf16[4,8,64,128]{3,2,1,0:T(8,128)(2,1)S(1)}, bf16[4,8,64,128]{3,2,1,0:T(8,128)(2,1)S(1)}, u32[]{:S(2)}, u32[]{:S(2)}) collective-permute-start(bf16[4,8,64,128]{3,2,1,0:T(8,128)(2,1)S(1)} %collective-permute-done.12), channel_id=1, source_target_pairs={{0,32},{32,0},{1,33},{33,1},{2,34},{34,2},{3,35},{35,3},{4,36},{36... | collective-permute-start | bytes 1572872 | tf_op jit(solution)/shard_map/ppermute | solution.py:118
  101.0 28.1 %collective-permute-start.19 = (bf16[4,8,64,128]{3,2,1,0:T(8,128)(2,1)S(1)}, bf16[4,8,64,128]{3,2,1,0:T(8,128)(2,1)}, u32[]{:S(2)}, u32[]{:S(2)}) collective-permute-start(bf16[4,8,64,128]{3,2,1,0:T(8,128)(2,1)S(1)} %collective-permute-done.11), channel_id=1, source_target_pairs={{0,32},{32,0},{1,33},{33,1},{2,34},{34,2},{3,35},{35,3},{4,36},{36... | collective-permute-start | bytes 1572872 | tf_op jit(solution)/shard_map/ppermute | solution.py:118
  111.7 17.4 %collective-permute-start.18 = (bf16[4,8,64,128]{3,2,1,0:T(8,128)(2,1)S(1)}, bf16[4,8,64,128]{3,2,1,0:T(8,128)(2,1)}, u32[]{:S(2)}, u32[]{:S(2)}) collective-permute-start(bf16[4,8,64,128]{3,2,1,0:T(8,128)(2,1)S(1)} %collective-permute-done.10), channel_id=1, source_target_pairs={{0,32},{32,0},{1,33},{33,1},{2,34},{34,2},{3,35},{35,3},{4,36},{36... | collective-permute-start | bytes 1572872 | tf_op jit(solution)/shard_map/ppermute | solution.py:118
  113.6 15.4 %collective-permute-start.16 = (bf16[4,8,64,128]{3,2,1,0:T(8,128)(2,1)S(1)}, bf16[4,8,64,128]{3,2,1,0:T(8,128)(2,1)}, u32[]{:S(2)}, u32[]{:S(2)}) collective-permute-start(bf16[4,8,64,128]{3,2,1,0:T(8,128)(2,1)S(1)} %collective-permute-done.6), channel_id=1, source_target_pairs={{0,32},{32,0},{1,33},{33,1},{2,34},{34,2},{3,35},{35,3},{4,36},{36... | collective-permute-start | bytes 1572872 | tf_op jit(solution)/shard_map/ppermute | solution.py:118
  125.4 3.6 %collective-permute-start.15 = (bf16[4,8,64,128]{3,2,1,0:T(8,128)(2,1)}, bf16[4,8,64,128]{3,2,1,0:T(8,128)(2,1)}, u32[]{:S(2)}, u32[]{:S(2)}) collective-permute-start(bf16[4,8,64,128]{3,2,1,0:T(8,128)(2,1)} %collective-permute-done.5), channel_id=1, source_target_pairs={{0,32},{32,0},{1,33},{33,1},{2,34},{34,2},{3,35},{35,3},{4,36},{36... | collective-permute-start | bytes 1572872 | tf_op jit(solution)/shard_map/ppermute | solution.py:118
  125.9 0.8 copy-start
  126.7 2.3 %collective-permute-start.14 = (bf16[4,8,64,128]{3,2,1,0:T(8,128)(2,1)}, bf16[4,8,64,128]{3,2,1,0:T(8,128)(2,1)}, u32[]{:S(2)}, u32[]{:S(2)}) collective-permute-start(bf16[4,8,64,128]{3,2,1,0:T(8,128)(2,1)} %collective-permute-done.4), channel_id=1, source_target_pairs={{0,32},{32,0},{1,33},{33,1},{2,34},{34,2},{3,35},{35,3},{4,36},{36... | collective-permute-start | bytes 1572872 | tf_op jit(solution)/shard_map/ppermute | solution.py:118
  129.1 1.0 copy-start.1

commit v2 on v1

v2 whole, which is shorter than its diff:
```python
import functools

import jax
import jax.numpy as jnp
from jax import lax
from jax.experimental import pallas as pl
from jax.experimental.pallas import tpu as pltpu
from jax.sharding import Mesh, PartitionSpec as P

STEP = 100
HALF = jnp.bfloat16
VMEM = pl.BlockSpec(memory_space=pltpu.VMEM)
SMEM = pl.BlockSpec(memory_space=pltpu.SMEM)
HBM = pl.BlockSpec(memory_space=pltpu.HBM)


def cost(size):
    return pl.CostEstimate(flops=0, bytes_accessed=size, transcendentals=0)


def inside(value):
    return pltpu.with_memory_space_constraint(value, pltpu.VMEM)


def adam_update(param, grad, first, second):
    new_first = 0.9 * first + 0.1 * grad
    new_second = 0.999 * second + 0.001 * grad * grad
    corr_first = new_first / (1.0 - 0.9**STEP)
    corr_second = new_second / (1.0 - 0.999**STEP)
    new_param = param - 0.1 * corr_first / (jnp.sqrt(corr_second) + 1e-08)
    return (new_param, new_first, new_second)


def pack_kernel(grad_a, grad_b, out):
    out[:, 0:128, :] = grad_a[0].reshape(8, 128, 128).astype(HALF)
    for owner in range(8):
        pair = jnp.concatenate([grad_b[0, 2 * owner], grad_b[0, 2 * owner + 1]], axis=-1)
        out[owner, 128:176, :] = pair.astype(HALF)


def summed(got):
    total = got[0].astype(jnp.float32)
    for learner in range(1, 8):
        total = total + got[learner].astype(jnp.float32)
    return total


def apart(total):
    return total[0:128].reshape(2, 64, 128), [total[128:176, 64 * e : 64 * e + 64] for e in range(2)]


def send_kernel(got, factor_a, factor_b, moment_a, second_a, moment_b, second_b, send, total):
    total[...] = summed(got)
    grad_a, grad_b = apart(total)
    a = adam_update(factor_a[...], grad_a, moment_a[...], second_a[...])[0]
    b = [adam_update(factor_b[e], grad_b[e], moment_b[e], second_b[e])[0] for e in range(2)]
    a_half = a.astype(HALF).reshape(128, 128)
    b_half = jnp.concatenate(b, axis=-1).astype(HALF)
    for peer in range(8):
        send[peer, 0:128, :] = a_half
        send[peer, 128:176, :] = b_half


def state_kernel(
    total, factor_a, factor_b, moment_a, second_a, moment_b, second_b,
    new_a, new_b, new_ma, new_va, new_mb, new_vb,
):
    grad_a, grad_b = apart(total)
    new_a[...], new_ma[...], new_va[...] = adam_update(
        factor_a[...], grad_a, moment_a[...], second_a[...]
    )
    for e in range(2):
        new_b[e], new_mb[e], new_vb[e] = adam_update(
            factor_b[e], grad_b[e], moment_b[e], second_b[e]
        )


def split_kernel(place, line, half_0, half_1, rows):
    half_0[...] = line[:, 0:64].reshape(512, 128)
    half_1[...] = line[:, 64:128].reshape(512, 128)
    zh = place[0]
    for zl in range(4):
        rows[zl] = line[2 * zl + zh, 128:176]


def join_kernel(*refs):
    rows, mine_0, mine_1, everything = refs[8:]
    for h, mine in ((0, mine_0), (1, mine_1)):
        for k in range(4):
            value = refs[4 * h + k][...]
            mine[512 * k : 512 * k + 512] = value
            everything[2048 * h + 512 * k : 2048 * h + 512 * k + 512] = value
    everything[4096:4288] = rows[...].reshape(192, 128)


def blocks_kernel(rows_own, other, blocks):
    rows_sibling = other[4096:4288].reshape(4, 48, 128)
    for side, rows in ((0, rows_own[...]), (1, rows_sibling)):
        for h in range(2):
            for zl in range(4):
                parts = []
                if zl:
                    parts.append(jnp.zeros((48, 64 * zl), HALF))
                parts.append(rows[zl, :, 64 * h : 64 * h + 64])
                if zl < 3:
                    parts.append(jnp.zeros((48, 192 - 64 * zl), HALF))
                blocks[side, h, 48 * zl : 48 * zl + 48, :] = jnp.concatenate(parts, axis=-1)


def relay_kernel(up_0, up_1, down_0, down_1, half_0, half_1, half_2, half_3, everything):
    half_0[...] = up_0[0:1024]
    half_1[...] = up_1[0:1024]
    half_2[...] = down_0[1024:2048]
    half_3[...] = down_1[1024:2048]
    for k, piece in enumerate((up_0, up_1, down_0, down_1)):
        everything[2048 * k : 2048 * k + 2048] = piece[...]


def merge_kernel(place, blocks, *refs, distances, pick):
    n = len(distances)
    pieces = pick(refs)
    base, out, held, read, write = refs[-5:]
    x, y, core = place[0], place[1], place[2]

    def unit(h, d, inner):
        ky, kx = (distances[d], inner) if h == 0 else (inner, distances[d])
        column = lax.rem(y + 4 - ky, 4) * 1024 + lax.rem(x + 4 - kx, 4) * 256
        return pl.ds(pl.multiple_of(column, 256), 256), (h * n + d) * 4 + inner

    def copy_in(h, d, inner):
        where, u = unit(h, d, inner)
        return pltpu.make_async_copy(base.at[:, :, h, :, where], held.at[u], read.at[u])

    def copy_out(h, d, inner):
        where, u = unit(h, d, inner)
        return pltpu.make_async_copy(held.at[u], out.at[:, :, h, :, where], write.at[u])

    units = [(h, d, inner) for d in range(n) for h in range(2) for inner in range(4)]
    for t in units:
        copy_in(*t).start()
    for d in range(n):
        for h in range(2):
            for inner in range(4):
                copy_in(h, d, inner).wait()
            for side in range(2):
                piece = jnp.concatenate([p[...] for p in pieces[side][h]]).reshape(4, 4, 2, 64, 128)
                wide = jnp.concatenate(
                    [piece[i, :, zh].reshape(256, 128) for i in range(4) for zh in range(2)], axis=-1
                )
                delta = jnp.dot(blocks[side, h], wide, preferred_element_type=jnp.float32)
                owner = core if side == 0 else 1 - core
                for inner in range(4):
                    u = (h * n + d) * 4 + inner
                    old = held[u, :, owner].astype(jnp.float32)
                    part = delta[:, 256 * inner : 256 * inner + 256].reshape(4, 48, 256)
                    held[u, :, owner] = (old + 0.125 * part).astype(HALF)
            for inner in range(4):
                copy_out(h, d, inner).start()
    for t in units:
        copy_out(*t).wait()


def next_merge_kernel(place, blocks, *refs, distances, pick):
    merge_kernel(place, blocks, *refs[:-5], *refs[-4:], distances=distances, pick=pick)


def pick_first(refs):
    return [[[refs[side].at[2048 * h : 2048 * h + 2048]] for h in range(2)] for side in range(2)]


def pick_near(refs, start):
    other = [[refs[2].at[start + 2048 * h : start + 2048 * h + 2048]] for h in range(2)]
    return [[[refs[0]], [refs[1]]], other]


def pick_far(refs):
    return [[[refs[4 * side + h], refs[4 * side + 2 + h]] for h in range(2)] for side in range(2)]


def hop(value, axis, k):
    n = lax.axis_size(axis)
    return lax.ppermute(value, axis, [(i, (i + k) % n) for i in range(n)])


def swap(value, axis, mask):
    n = lax.axis_size(axis)
    return lax.ppermute(value, axis, [(i, i ^ mask) for i in range(n)])


def per_device(
    grad_a, grad_b, factor_a, factor_b, moment_a, second_a, moment_b, second_b, base_rows
):
    f32 = jnp.float32
    shape = jax.ShapeDtypeStruct
    packed = pl.pallas_call(
        pack_kernel,
        out_shape=pltpu.VMEM((8, 176, 128), HALF),
        in_specs=[VMEM] * 2,
        out_specs=VMEM,
    )(grad_a, grad_b)
    got = lax.all_to_all(packed, ("zl", "core"), 0, 0, tiled=True)
    sa, sb = shape((2, 64, 128), f32), shape((2, 48, 64), f32)
    state = (factor_a, factor_b, moment_a, second_a, moment_b, second_b)
    send, total = pl.pallas_call(
        send_kernel,
        out_shape=(pltpu.VMEM((8, 176, 128), HALF), shape((176, 128), f32)),
        in_specs=[VMEM] * 7,
        out_specs=(VMEM,) * 2,
    )(inside(got), *state)
    line = lax.all_to_all(send, ("zl", "zh"), 0, 0, tiled=True)

    x, y, core, zh = (lax.axis_index(a).astype(jnp.int32) for a in ("x", "y", "core", "zh"))
    half_0, half_1, rows_own = pl.pallas_call(
        split_kernel,
        out_shape=(pltpu.VMEM((512, 128), HALF), pltpu.VMEM((512, 128), HALF), pltpu.VMEM((4, 48, 128), HALF)),
        in_specs=[SMEM, VMEM],
        out_specs=(VMEM,) * 3,
    )(zh.reshape(1), inside(line))
    halves = half_0, half_1

    first, second = ("x", "y"), ("y", "x")
    parts = [[halves[h]] + [hop(halves[h], first[h], k) for k in (1, 2, 3)] for h in range(2)]
    parts = lax.optimization_barrier(parts)
    mine_0, mine_1, everything = pl.pallas_call(
        join_kernel,
        out_shape=(shape((2048, 128), HALF),) * 2 + (shape((4288, 128), HALF),),
        in_specs=[VMEM] * 9,
        out_specs=(VMEM,) * 3,
    )(*[inside(p) for p in parts[0] + parts[1]], inside(rows_own))
    mine = mine_0, mine_1
    near = [hop(mine[h], second[h], k) for k in (1, 3) for h in range(2)]
    other = hop(everything, "core", 1)
    blocks = pl.pallas_call(
        blocks_kernel,
        out_shape=pltpu.VMEM((2, 2, 192, 256), HALF),
        in_specs=[VMEM] * 2,
        out_specs=VMEM,
    )(inside(rows_own), inside(other))
    states = pl.pallas_call(
        state_kernel,
        out_shape=(sa, sb, sa, sa, sb, sb),
        in_specs=[VMEM] * 7,
        out_specs=[VMEM] * 6,
        cost_estimate=cost(1024),
    )(total, *state)

    place = jnp.stack([x, y, core])
    base = pltpu.with_memory_space_constraint(base_rows.reshape(4, 2, 2, 48, 4096), pltpu.HBM)

    def merge(distances, pick, pieces, before):
        n = len(distances)
        before = [] if before is None else [before]
        return pl.pallas_call(
            functools.partial(next_merge_kernel if before else merge_kernel, distances=distances, pick=pick),
            out_shape=shape((4, 2, 2, 48, 4096), HALF),
            in_specs=[SMEM, VMEM] + [VMEM] * len(pieces) + [HBM] + [HBM] * len(before),
            out_specs=HBM,
            input_output_aliases={3 + len(pieces): 0} if before else {},
            scratch_shapes=[
                pltpu.VMEM((8 * n, 4, 2, 48, 256), HALF),
                pltpu.SemaphoreType.DMA((8 * n,)),
                pltpu.SemaphoreType.DMA((8 * n,)),
            ],
            compiler_params=pltpu.CompilerParams(vmem_limit_bytes=(6 + 4 * n) * 1024 * 1024),
            cost_estimate=cost(1024),
        )(place, inside(blocks), *pieces, base, *before)

    merged = merge((0,), pick_first, [everything, other], None)
    near, merged, states = lax.optimization_barrier((near, merged, states))
    half = shape((1024, 128), HALF)
    *relayed, everything = pl.pallas_call(
        relay_kernel,
        out_shape=(half,) * 4 + (shape((8192, 128), HALF),),
        in_specs=[VMEM] * 4,
        out_specs=(VMEM,) * 5,
    )(*near)
    far = [hop(relayed[2 * s + h], second[h], 1 + 2 * s) for s in range(2) for h in range(2)]
    near_other = hop(everything, "core", 1)
    merged = merge((1,), functools.partial(pick_near, start=0), near[:2] + [near_other], merged)
    far, merged = lax.optimization_barrier((far, merged))
    far_other = [hop(v, "core", 1) for v in far]
    merged = merge((3,), functools.partial(pick_near, start=4096), near[2:] + [near_other], merged)
    merged = merge((2,), pick_far, far + far_other, merged)
    new_a, new_b, new_ma, new_va, new_mb, new_vb = states
    return (new_a, new_b, new_ma, new_va, new_mb, new_vb, merged.reshape(16, 48, 4096))


def solution(mesh):
    fine = Mesh(mesh.devices.reshape(4, 2, 4, 4, 2), ("zl", "core", "y", "x", "zh"))
    group, tensor = ("zl", "core"), ("y", "x", "zh")
    in_specs = (
        P(group, None, None, tensor),
        P(group, None, tensor, None),
        P(group, None, tensor),
        P(group, tensor, None),
        P(group, None, tensor),
        P(group, None, tensor),
        P(group, tensor, None),
        P(group, tensor, None),
        P(None, tensor, None),
    )
    out_specs = (
        P(group, None, tensor),
        P(group, tensor, None),
        P(group, None, tensor),
        P(group, None, tensor),
        P(group, tensor, None),
        P(group, tensor, None),
        P(None, tensor, None),
    )
    return jax.shard_map(
        per_device, mesh=fine, in_specs=in_specs, out_specs=out_specs, check_vma=False
    )
```

time: 140 us -> 103 us (0.74)
  the two profiles are of different devices: /device:TPU:1 before, /device:TPU:39 now
where the time goes in v2:
time: 103 us; the launch traced here: 102 us
  waiting for transfers between devices  29.2 us (28%)
  starting transfers between devices  28.1 us (27%)
  Pallas kernels  24.8 us (24%)
  blocking collectives  15.8 us (15%)
  local copies, waits for them, and re-layouts  3.15 us (3%)
    ppermute x20, starting transfers between devices, hop(): return lax.ppermute(value, axis, [(i, (i + k) % n) for i in range(n)])  21.1 us
    ppermute x20, waiting for transfers between devices, hop(): return lax.ppermute(value, axis, [(i, (i + k) % n) for i in range(n)])  16.4 us
    all_to_all x1, blocking collectives, per_device(): got = lax.all_to_all(packed, ('zl', 'core'), 0, 0, tiled=True)  15.8 us
    pallas_call x4, Pallas kernels, merge(): pl.pallas_call(functools.partial(next_merge_kernel if before else merge_k...  14.9 us
    all_to_all x1, waiting for transfers between devices, per_device(): line = lax.all_to_all(send, ('zl', 'zh'), 0, 0, tiled=True)  12.8 us
    all_to_all x1, starting transfers between devices, per_device(): line = lax.all_to_all(send, ('zl', 'zh'), 0, 0, tiled=True)  6.93 us
    pallas_call x1, Pallas kernels, per_device(): pl.pallas_call(relay_kernel, out_shape=(half,) * 4 + (shape((8192, 128),...  3.21 us
    unnamed x14, local copies, waits for them, and re-layouts  3.15 us
  transfers between devices with their start and end apart: 21, of which 9 were waited for; matrix products, arithmetic and copies ran while one was open for 0% of the time, Pallas kernels for 13%

profile of v2, /device:TPU:39, one launch (start us, length us, event | category | flops | bytes accessed | tf_op | source)
XLA Modules:
  0.0 102.0 jit_solution(9476664246041605441)
XLA Ops:
  0.6 1.3 %shard_map.144 = bf16[8,176,128]{2,1,0:T(8,128)(2,1)S(1)} custom-call(f32[1,16,64,128]{3,2,1,0:T(8,128)} %grad_a.1, f32[1,16,48,64]{3,2,1,0:T(8,128)} %grad_b.1), custom_call_target="tpu_custom_call" | custom-call | tf_op jit(solution)/shard_map/pallas_call | solution.py:195
  1.9 15.8 %all_to_all.10.got = bf16[8,176,128]{2,1,0:T(8,128)(2,1)S(1)} all-to-all(bf16[8,176,128]{2,1,0:T(8,128)(2,1)S(1)} %shard_map.144), channel_id=1, replica_groups=mesh['zl'=4,'core'=2,'y'=4,'x'=4,'zh'=2] {'zl','core'}, dimensions={0} | all-to-all | bytes 720896 | tf_op jit(solution)/shard_map/all_to_all | solution.py:201
  17.7 1.9 %shard_map.145 = (bf16[8,176,128]{2,1,0:T(8,128)(2,1)}, f32[176,128]{1,0:T(8,128)}) custom-call(bf16[8,176,128]{2,1,0:T(8,128)(2,1)S(1)} %all_to_all.10.got, f32[2,64,128]{2,1,0:T(8,128)} %factor_a.3, f32[2,48,64]{2,1,0:T(8,128)} %factor_b.3, f32[2,64,128]{2,1,0:T(8,128)} %moment_a.3, f32[2,64,128]{2,1,0:T(8,128)} %second_a.3, f32[2,48,64]{2,1,0:T(8,128)} %moment_b.3, ...), custom_call_target="tpu_custom_call" | custom-call | tf_op jit(solution)/shard_map/pallas_call | solution.py:204
  19.6 6.9 %all-to-all-start.1 = ((bf16[8,176,128]{2,1,0:T(8,128)(2,1)}), bf16[8,176,128]{2,1,0:T(8,128)(2,1)S(1)}, u32[]{:S(2)}, u32[]{:S(2)}) async-start(bf16[8,176,128]{2,1,0:T(8,128)(2,1)} %get-tuple-element.50), calls=%async_computation.1 | async-start | bytes 720896 | tf_op jit(solution)/shard_map/all_to_all | solution.py:210
  26.5 12.8 %all-to-all-done.1.line = bf16[8,176,128]{2,1,0:T(8,128)(2,1)S(1)} async-done(((bf16[8,176,128]{2,1,0:T(8,128)(2,1)}), bf16[8,176,128]{2,1,0:T(8,128)(2,1)S(1)}, u32[]{:S(2)}, u32[]{:S(2)}) %all-to-all-start.1) | async-done | bytes 360480 | tf_op jit(solution)/shard_map/all_to_all | solution.py:210
  39.3 0.6 collective-permute-start.2
  39.9 0.8 collective-permute-start.1
  40.8 1.8 %collective-permute-start = (bf16[512,128]{1,0:T(8,128)(2,1)S(1)}, bf16[512,128]{1,0:T(8,128)(2,1)S(1)}, u32[]{:S(2)}, u32[]{:S(2)}) collective-permute-start(bf16[512,128]{1,0:T(8,128)(2,1)S(1)} %get-tuple-element.53.refs_0_), channel_id=1, source_target_pairs={{0,2},{2,4},{4,6},{6,0},{1,3},{3,5},{5,7},{7,1},{8,10},{10,12},{12... | collective-permute-start | bytes 393224 | tf_op jit(solution)/shard_map/ppermute | solution.py:182
  42.6 2.7 %collective-permute-start.5 = (bf16[512,128]{1,0:T(8,128)(2,1)S(1)}, bf16[512,128]{1,0:T(8,128)(2,1)S(1)}, u32[]{:S(2)}, u32[]{:S(2)}) collective-permute-start(bf16[512,128]{1,0:T(8,128)(2,1)S(1)} %get-tuple-element.57.refs_4_), channel_id=1, source_target_pairs={{0,24},{8,0},{16,8},{24,16},{1,25},{9,1},{17,9},{25,17},{2,26},{10... | collective-permute-start | bytes 393224 | tf_op jit(solution)/shard_map/ppermute | solution.py:182
  45.3 0.3 collective-permute-start.4
  45.7 2.3 %collective-permute-done.2.refs_3_ = bf16[512,128]{1,0:T(8,128)(2,1)S(1)} collective-permute-done((bf16[512,128]{1,0:T(8,128)(2,1)S(1)}, bf16[512,128]{1,0:T(8,128)(2,1)S(1)}, u32[]{:S(2)}, u32[]{:S(2)}) %collective-permute-start.2) | collective-permute-done | bytes 131104 | tf_op jit(solution)/shard_map/ppermute | solution.py:182
  47.9 1.3 %collective-permute-start.3 = (bf16[512,128]{1,0:T(8,128)(2,1)S(1)}, bf16[512,128]{1,0:T(8,128)(2,1)S(1)}, u32[]{:S(2)}, u32[]{:S(2)}) collective-permute-start(bf16[512,128]{1,0:T(8,128)(2,1)S(1)} %get-tuple-element.57.refs_4_), channel_id=1, source_target_pairs={{0,8},{8,16},{16,24},{24,0},{1,9},{9,17},{17,25},{25,1},{2,10},{10... | collective-permute-start | bytes 393224 | tf_op jit(solution)/shard_map/ppermute | solution.py:182
  49.2 0.0 collective-permute-done.1.refs_2_
  49.2 0.0 collective-permute-done.refs_1_
  49.2 0.0 collective-permute-done.5.refs_7_
  49.2 1.4 %collective-permute-done.4.refs_6_ = bf16[512,128]{1,0:T(8,128)(2,1)S(1)} collective-permute-done((bf16[512,128]{1,0:T(8,128)(2,1)S(1)}, bf16[512,128]{1,0:T(8,128)(2,1)S(1)}, u32[]{:S(2)}, u32[]{:S(2)}) %collective-permute-start.4) | collective-permute-done | bytes 131104 | tf_op jit(solution)/shard_map/ppermute | solution.py:182
  50.6 4.7 %collective-permute-done.3.refs_5_ = bf16[512,128]{1,0:T(8,128)(2,1)S(1)} collective-permute-done((bf16[512,128]{1,0:T(8,128)(2,1)S(1)}, bf16[512,128]{1,0:T(8,128)(2,1)S(1)}, u32[]{:S(2)}, u32[]{:S(2)}) %collective-permute-start.3) | collective-permute-done | bytes 131104 | tf_op jit(solution)/shard_map/ppermute | solution.py:182
  55.4 1.6 %shard_map.147 = (bf16[2048,128]{1,0:T(8,128)(2,1)}, bf16[2048,128]{1,0:T(8,128)(2,1)}, bf16[4288,128]{1,0:T(8,128)(2,1)}) custom-call(bf16[512,128]{1,0:T(8,128)(2,1)S(1)} %get-tuple-element.53.refs_0_, bf16[512,128]{1,0:T(8,128)(2,1)S(1)} %collective-permute-done.refs_1_, bf16[512,128]{1,0:T(8,128)(2,1)S(1)} %collective-permute-done.1.refs_2_, ...), custom_call_target="tpu_custom_call" | custom-call | tf_op jit(solution)/shard_map/pallas_call | solution.py:224
  57.0 1.0 collective-permute-start.10
  58.0 0.6 collective-permute-start.8
  58.6 0.8 collective-permute-start.6
  59.4 0.0 collective-permute-start.9
  59.4 2.7 %collective-permute-start.7 = (bf16[2048,128]{1,0:T(8,128)(2,1)}, bf16[2048,128]{1,0:T(8,128)(2,1)}, u32[]{:S(2)}, u32[]{:S(2)}) collective-permute-start(bf16[2048,128]{1,0:T(8,128)(2,1)} %get-tuple-element.63), channel_id=1, source_target_pairs={{0,2},{2,4},{4,6},{6,0},{1,3},{3,5},{5,7},{7,1},{8,10},{10,12},{12... | collective-permute-start | bytes 1572872 | tf_op jit(solution)/shard_map/ppermute | solution.py:182
  62.1 0.1 pad_add_fusion.place
  62.2 1.8 %shard_map.150 = (f32[2,64,128]{2,1,0:T(8,128)}, f32[2,48,64]{2,1,0:T(8,128)}, f32[2,64,128]{2,1,0:T(8,128)}, f32[2,64,128]{2,1,0:T(8,128)}, f32[2,48,64]{2,1,0:T(8,128)}, /*index=5*/f32[2,48,64]{2,1,0:T(8,128)}) custom-call(f32[176,128]{1,0:T(8,128)} %get-tuple-element.65.total, f32[2,64,128]{2,1,0:T(8,128)} %factor_a.3, f32[2,48,64]{2,1,0:T(8,128)} %factor_b.3, ...), custom_call_target="tpu_custom_call" | custom-call | bytes 1024 | tf_op jit(solution)/shard_map/pallas_call | solution.py:239
  64.0 0.0 collective-permute-done.10.other.refs_1_
  64.0 0.1 shard_map.148.blocks
  64.1 0.0 copy-start.6
  64.1 1.2 %copy-done.6 = bf16[4288,128]{1,0:T(8,128)(2,1)S(1)} copy-done((bf16[4288,128]{1,0:T(8,128)(2,1)S(1)}, bf16[4288,128]{1,0:T(8,128)(2,1)}, u32[]{:S(2)}) %copy-start.6) | copy-done | bytes 1097752
  65.3 3.6 %shard_map.149.refs_4_ = bf16[4,2,2,48,4096]{4,3,2,1,0:T(8,128)(2,1)} custom-call(s32[3]{0:T(128)S(1)} %pad_add_fusion.place, bf16[2,2,192,256]{3,2,1,0:T(8,128)(2,1)S(1)} %shard_map.148.blocks, bf16[4288,128]{1,0:T(8,128)(2,1)S(1)} %copy-done.6, bf16[4288,128]{1,0:T(8,128)(2,1)S(1)} %collective-permute-done.10.other.refs_1_, ...), custom_call_target="tpu_custom_call" | custom-call | bytes 1024 | tf_op jit(solution)/shard_map/pallas_call | solution.py:253
  68.9 2.9 %collective-permute-done.8.down_0.refs_0_ = bf16[2048,128]{1,0:T(8,128)(2,1)S(1)} collective-permute-done((bf16[2048,128]{1,0:T(8,128)(2,1)}, bf16[2048,128]{1,0:T(8,128)(2,1)S(1)}, u32[]{:S(2)}, u32[]{:S(2)}) %collective-permute-start.8) | collective-permute-done | bytes 524320 | tf_op jit(solution)/shard_map/ppermute | solution.py:182
  71.8 0.0 copy-start
  71.8 1.4 %collective-permute-done.6.up_0.refs_0_ = bf16[2048,128]{1,0:T(8,128)(2,1)S(1)} collective-permute-done((bf16[2048,128]{1,0:T(8,128)(2,1)}, bf16[2048,128]{1,0:T(8,128)(2,1)S(1)}, u32[]{:S(2)}, u32[]{:S(2)}) %collective-permute-start.6) | collective-permute-done | bytes 524320 | tf_op jit(solution)/shard_map/ppermute | solution.py:182
  73.3 0.5 collective-permute-done.9.down_1.refs_1_
  73.8 0.0 collective-permute-done.7.up_1.refs_1_
  73.8 0.0 copy-done
  73.8 0.3 copy-done.4
  74.1 0.5 copy-done.2
  74.6 3.2 %shard_map.151 = (bf16[1024,128]{1,0:T(8,128)(2,1)}, bf16[1024,128]{1,0:T(8,128)(2,1)}, bf16[1024,128]{1,0:T(8,128)(2,1)}, bf16[1024,128]{1,0:T(8,128)(2,1)}, bf16[8192,128]{1,0:T(8,128)(2,1)}) custom-call(bf16[2048,128]{1,0:T(8,128)(2,1)} %copy-done.4, bf16[2048,128]{1,0:T(8,128)(2,1)} %collective-permute-done.7.up_1.refs_1_, bf16[2048,128]{1,0:T(8,128)(2,1)} %copy-done, ...), custom_call_target="tpu_custom_call" | custom-call | tf_op jit(solution)/shard_map/pallas_call | solution.py:271
  77.8 1.4 %collective-permute-start.15 = (bf16[8192,128]{1,0:T(8,128)(2,1)}, bf16[8192,128]{1,0:T(8,128)(2,1)S(1)}, u32[]{:S(2)}, u32[]{:S(2)}) collective-permute-start(bf16[8192,128]{1,0:T(8,128)(2,1)} %get-tuple-element.86), channel_id=1, source_target_pairs={{0,32},{32,0},{1,33},{33,1},{2,34},{34,2},{3,35},{35,3},{4,36},{36... | collective-permute-start | bytes 6291464 | tf_op jit(solution)/shard_map/ppermute | solution.py:182
  79.2 0.0 collective-permute-start.11
  79.2 2.0 %collective-permute-start.12 = (bf16[1024,128]{1,0:T(8,128)(2,1)}, bf16[1024,128]{1,0:T(8,128)(2,1)S(1)}, u32[]{:S(2)}, u32[]{:S(2)}) collective-permute-start(bf16[1024,128]{1,0:T(8,128)(2,1)} %get-tuple-element.83), channel_id=1, source_target_pairs={{0,2},{2,4},{4,6},{6,0},{1,3},{3,5},{5,7},{7,1},{8,10},{10,12},{12... | collective-permute-start | bytes 786440 | tf_op jit(solution)/shard_map/ppermute | solution.py:182
  81.2 2.7 %collective-permute-start.13 = (bf16[1024,128]{1,0:T(8,128)(2,1)}, bf16[1024,128]{1,0:T(8,128)(2,1)S(1)}, u32[]{:S(2)}, u32[]{:S(2)}) collective-permute-start(bf16[1024,128]{1,0:T(8,128)(2,1)} %get-tuple-element.84), channel_id=1, source_target_pairs={{0,24},{8,0},{16,8},{24,16},{1,25},{9,1},{17,9},{25,17},{2,26},{10... | collective-permute-start | bytes 786440 | tf_op jit(solution)/shard_map/ppermute | solution.py:182
  83.9 0.0 collective-permute-start.14
  83.9 0.0 collective-permute-done.15.refs_2_
  83.9 0.0 copy-start.5
  83.9 1.1 %copy-done.5 = bf16[2048,128]{1,0:T(8,128)(2,1)S(1)} copy-done((bf16[2048,128]{1,0:T(8,128)(2,1)S(1)}, bf16[2048,128]{1,0:T(8,128)(2,1)}, u32[]{:S(2)}) %copy-start.5) | copy-done | bytes 524312
  85.0 4.1 %shard_map.152.refs_4_ = bf16[4,2,2,48,4096]{4,3,2,1,0:T(8,128)(2,1)} custom-call(s32[3]{0:T(128)S(1)} %pad_add_fusion.place, bf16[2,2,192,256]{3,2,1,0:T(8,128)(2,1)S(1)} %shard_map.148.blocks, bf16[2048,128]{1,0:T(8,128)(2,1)S(1)} %copy-done.5, bf16[2048,128]{1,0:T(8,128)(2,1)} %collective-permute-done.7.up_1.refs_1_, ...), custom_call_target="tpu_custom_call", output_to_operand_aliasing={{}: (6, {})} | custom-call | bytes 1024 | tf_op jit(solution)/shard_map/pallas_call | solution.py:253
  89.2 0.0 collective-permute-done.11.refs_0_
  89.2 0.0 collective-permute-done.12.refs_1_
  89.2 0.1 collective-permute-done.13.refs_2_
  89.3 3.0 %collective-permute-done.14.refs_3_ = bf16[1024,128]{1,0:T(8,128)(2,1)S(1)} collective-permute-done((bf16[1024,128]{1,0:T(8,128)(2,1)}, bf16[1024,128]{1,0:T(8,128)(2,1)S(1)}, u32[]{:S(2)}, u32[]{:S(2)}) %collective-permute-start.14) | collective-permute-done | bytes 262176 | tf_op jit(solution)/shard_map/ppermute | solution.py:182
  92.3 1.7 %collective-permute-start.16 = (bf16[1024,128]{1,0:T(8,128)(2,1)S(1)}, bf16[1024,128]{1,0:T(8,128)(2,1)S(1)}, u32[]{:S(2)}, u32[]{:S(2)}) collective-permute-start(bf16[1024,128]{1,0:T(8,128)(2,1)S(1)} %collective-permute-done.11.refs_0_), channel_id=1, source_target_pairs={{0,32},{32,0},{1,33},{33,1},{2,34},{34,2},{3,35},{35,3},{4,36},{36... | collective-permute-start | bytes 786440 | tf_op jit(solution)/shard_map/ppermute | solution.py:182
  94.0 0.0 collective-permute-start.17
  94.0 0.5 collective-permute-start.18
  94.5 0.0 collective-permute-start.19
  94.6 0.0 copy-done.1
  94.6 0.0 copy-done.3
  94.6 3.6 %shard_map.153.refs_9_ = bf16[4,2,2,48,4096]{4,3,2,1,0:T(8,128)(2,1)} custom-call(s32[3]{0:T(128)S(1)} %pad_add_fusion.place, bf16[2,2,192,256]{3,2,1,0:T(8,128)(2,1)S(1)} %shard_map.148.blocks, bf16[2048,128]{1,0:T(8,128)(2,1)S(1)} %copy-done.1, bf16[2048,128]{1,0:T(8,128)(2,1)S(1)} %copy-done.3, ...), custom_call_target="tpu_custom_call", output_to_operand_aliasing={{}: (6, {})} | custom-call | bytes 1024 | tf_op jit(solution)/shard_map/pallas_call | solution.py:253
  98.2 0.0 collective-permute-done.16.refs_4_
  98.2 0.0 collective-permute-done.17.refs_5_
  98.2 0.0 collective-permute-done.18.refs_6_
  98.2 0.0 collective-permute-done.19.refs_7_
  98.2 3.6 %shard_map.154 = bf16[4,2,2,48,4096]{4,3,2,1,0:T(8,128)(2,1)} custom-call(s32[3]{0:T(128)S(1)} %pad_add_fusion.place, bf16[2,2,192,256]{3,2,1,0:T(8,128)(2,1)S(1)} %shard_map.148.blocks, bf16[1024,128]{1,0:T(8,128)(2,1)S(1)} %collective-permute-done.11.refs_0_, ...), custom_call_target="tpu_custom_call", output_to_operand_aliasing={{}: (11, {})} | custom-call | bytes 1024 | tf_op jit(solution)/shard_map/pallas_call | solution.py:253
  (5 shorter events, 0.0 us)
Async XLA Ops:
  19.6 19.7 %all-to-all-start.1 = ((bf16[8,176,128]{2,1,0:T(8,128)(2,1)}), bf16[8,176,128]{2,1,0:T(8,128)(2,1)S(1)}, u32[]{:S(2)}, u32[]{:S(2)}) async-start(bf16[8,176,128]{2,1,0:T(8,128)(2,1)} %get-tuple-element.50), calls=%async_computation.1 | async-start | bytes 720896 | tf_op jit(solution)/shard_map/all_to_all | solution.py:210
  39.3 8.6 %collective-permute-start.2 = (bf16[512,128]{1,0:T(8,128)(2,1)S(1)}, bf16[512,128]{1,0:T(8,128)(2,1)S(1)}, u32[]{:S(2)}, u32[]{:S(2)}) collective-permute-start(bf16[512,128]{1,0:T(8,128)(2,1)S(1)} %get-tuple-element.53.refs_0_), channel_id=1, source_target_pairs={{0,6},{2,0},{4,2},{6,4},{1,7},{3,1},{5,3},{7,5},{8,14},{10,8},{12,... | collective-permute-start | bytes 393224 | tf_op jit(solution)/shard_map/ppermute | solution.py:182
  39.9 9.3 %collective-permute-start.1 = (bf16[512,128]{1,0:T(8,128)(2,1)S(1)}, bf16[512,128]{1,0:T(8,128)(2,1)S(1)}, u32[]{:S(2)}, u32[]{:S(2)}) collective-permute-start(bf16[512,128]{1,0:T(8,128)(2,1)S(1)} %get-tuple-element.53.refs_0_), channel_id=1, source_target_pairs={{0,4},{2,6},{4,0},{6,2},{1,5},{3,7},{5,1},{7,3},{8,12},{10,14},{12... | collective-permute-start | bytes 393224 | tf_op jit(solution)/shard_map/ppermute | solution.py:182
  40.8 8.5 %collective-permute-start = (bf16[512,128]{1,0:T(8,128)(2,1)S(1)}, bf16[512,128]{1,0:T(8,128)(2,1)S(1)}, u32[]{:S(2)}, u32[]{:S(2)}) collective-permute-start(bf16[512,128]{1,0:T(8,128)(2,1)S(1)} %get-tuple-element.53.refs_0_), channel_id=1, source_target_pairs={{0,2},{2,4},{4,6},{6,0},{1,3},{3,5},{5,7},{7,1},{8,10},{10,12},{12... | collective-permute-start | bytes 393224 | tf_op jit(solution)/shard_map/ppermute | solution.py:182
  42.6 6.7 %collective-permute-start.5 = (bf16[512,128]{1,0:T(8,128)(2,1)S(1)}, bf16[512,128]{1,0:T(8,128)(2,1)S(1)}, u32[]{:S(2)}, u32[]{:S(2)}) collective-permute-start(bf16[512,128]{1,0:T(8,128)(2,1)S(1)} %get-tuple-element.57.refs_4_), channel_id=1, source_target_pairs={{0,24},{8,0},{16,8},{24,16},{1,25},{9,1},{17,9},{25,17},{2,26},{10... | collective-permute-start | bytes 393224 | tf_op jit(solution)/shard_map/ppermute | solution.py:182
  45.3 5.3 %collective-permute-start.4 = (bf16[512,128]{1,0:T(8,128)(2,1)S(1)}, bf16[512,128]{1,0:T(8,128)(2,1)S(1)}, u32[]{:S(2)}, u32[]{:S(2)}) collective-permute-start(bf16[512,128]{1,0:T(8,128)(2,1)S(1)} %get-tuple-element.57.refs_4_), channel_id=1, source_target_pairs={{0,16},{8,24},{16,0},{24,8},{1,17},{9,25},{17,1},{25,9},{2,18},{10... | collective-permute-start | bytes 393224 | tf_op jit(solution)/shard_map/ppermute | solution.py:182
  47.9 7.4 %collective-permute-start.3 = (bf16[512,128]{1,0:T(8,128)(2,1)S(1)}, bf16[512,128]{1,0:T(8,128)(2,1)S(1)}, u32[]{:S(2)}, u32[]{:S(2)}) collective-permute-start(bf16[512,128]{1,0:T(8,128)(2,1)S(1)} %get-tuple-element.57.refs_4_), channel_id=1, source_target_pairs={{0,8},{8,16},{16,24},{24,0},{1,9},{9,17},{17,25},{25,1},{2,10},{10... | collective-permute-start | bytes 393224 | tf_op jit(solution)/shard_map/ppermute | solution.py:182
  57.0 7.0 %collective-permute-start.10 = (bf16[4288,128]{1,0:T(8,128)(2,1)}, bf16[4288,128]{1,0:T(8,128)(2,1)S(1)}, u32[]{:S(2)}, u32[]{:S(2)}) collective-permute-start(bf16[4288,128]{1,0:T(8,128)(2,1)} %get-tuple-element.64.refs_0_), channel_id=1, source_target_pairs={{0,32},{32,0},{1,33},{33,1},{2,34},{34,2},{3,35},{35,3},{4,36},{36... | collective-permute-start | bytes 3293192 | tf_op jit(solution)/shard_map/ppermute | solution.py:182
  58.0 13.9 %collective-permute-start.8 = (bf16[2048,128]{1,0:T(8,128)(2,1)}, bf16[2048,128]{1,0:T(8,128)(2,1)S(1)}, u32[]{:S(2)}, u32[]{:S(2)}) collective-permute-start(bf16[2048,128]{1,0:T(8,128)(2,1)} %get-tuple-element.62), channel_id=1, source_target_pairs={{0,24},{8,0},{16,8},{24,16},{1,25},{9,1},{17,9},{25,17},{2,26},{10... | collective-permute-start | bytes 1572872 | tf_op jit(solution)/shard_map/ppermute | solution.py:182
  58.6 14.7 %collective-permute-start.6 = (bf16[2048,128]{1,0:T(8,128)(2,1)}, bf16[2048,128]{1,0:T(8,128)(2,1)S(1)}, u32[]{:S(2)}, u32[]{:S(2)}) collective-permute-start(bf16[2048,128]{1,0:T(8,128)(2,1)} %get-tuple-element.62), channel_id=1, source_target_pairs={{0,8},{8,16},{16,24},{24,0},{1,9},{9,17},{17,25},{25,1},{2,10},{10... | collective-permute-start | bytes 1572872 | tf_op jit(solution)/shard_map/ppermute | solution.py:182
  59.4 14.3 %collective-permute-start.9 = (bf16[2048,128]{1,0:T(8,128)(2,1)}, bf16[2048,128]{1,0:T(8,128)(2,1)S(1)}, u32[]{:S(2)}, u32[]{:S(2)}) collective-permute-start(bf16[2048,128]{1,0:T(8,128)(2,1)} %get-tuple-element.63), channel_id=1, source_target_pairs={{0,6},{2,0},{4,2},{6,4},{1,7},{3,1},{5,3},{7,5},{8,14},{10,8},{12,... | collective-permute-start | bytes 1572872 | tf_op jit(solution)/shard_map/ppermute | solution.py:182
  59.4 14.3 %collective-permute-start.7 = (bf16[2048,128]{1,0:T(8,128)(2,1)}, bf16[2048,128]{1,0:T(8,128)(2,1)}, u32[]{:S(2)}, u32[]{:S(2)}) collective-permute-start(bf16[2048,128]{1,0:T(8,128)(2,1)} %get-tuple-element.63), channel_id=1, source_target_pairs={{0,2},{2,4},{4,6},{6,0},{1,3},{3,5},{5,7},{7,1},{8,10},{10,12},{12... | collective-permute-start | bytes 1572872 | tf_op jit(solution)/shard_map/ppermute | solution.py:182
  64.1 1.2 %copy-start.6 = (bf16[4288,128]{1,0:T(8,128)(2,1)S(1)}, bf16[4288,128]{1,0:T(8,128)(2,1)}, u32[]{:S(2)}) copy-start(bf16[4288,128]{1,0:T(8,128)(2,1)} %get-tuple-element.64.refs_0_) | copy-start | bytes 3293188
  71.8 1.9 %copy-start = (bf16[2048,128]{1,0:T(8,128)(2,1)}, bf16[2048,128]{1,0:T(8,128)(2,1)S(1)}, u32[]{:S(2)}) copy-start(bf16[2048,128]{1,0:T(8,128)(2,1)S(1)} %collective-permute-done.8.down_0.refs_0_) | copy-start | bytes 1572868
  73.3 0.8 copy-start.4
  73.8 0.8 copy-start.2
  77.8 6.1 %collective-permute-start.15 = (bf16[8192,128]{1,0:T(8,128)(2,1)}, bf16[8192,128]{1,0:T(8,128)(2,1)S(1)}, u32[]{:S(2)}, u32[]{:S(2)}) collective-permute-start(bf16[8192,128]{1,0:T(8,128)(2,1)} %get-tuple-element.86), channel_id=1, source_target_pairs={{0,32},{32,0},{1,33},{33,1},{2,34},{34,2},{3,35},{35,3},{4,36},{36... | collective-permute-start | bytes 6291464 | tf_op jit(solution)/shard_map/ppermute | solution.py:182
  79.2 10.0 %collective-permute-start.11 = (bf16[1024,128]{1,0:T(8,128)(2,1)}, bf16[1024,128]{1,0:T(8,128)(2,1)S(1)}, u32[]{:S(2)}, u32[]{:S(2)}) collective-permute-start(bf16[1024,128]{1,0:T(8,128)(2,1)} %get-tuple-element.82), channel_id=1, source_target_pairs={{0,8},{8,16},{16,24},{24,0},{1,9},{9,17},{17,25},{25,1},{2,10},{10... | collective-permute-start | bytes 786440 | tf_op jit(solution)/shard_map/ppermute | solution.py:182
  79.2 10.0 %collective-permute-start.12 = (bf16[1024,128]{1,0:T(8,128)(2,1)}, bf16[1024,128]{1,0:T(8,128)(2,1)S(1)}, u32[]{:S(2)}, u32[]{:S(2)}) collective-permute-start(bf16[1024,128]{1,0:T(8,128)(2,1)} %get-tuple-element.83), channel_id=1, source_target_pairs={{0,2},{2,4},{4,6},{6,0},{1,3},{3,5},{5,7},{7,1},{8,10},{10,12},{12... | collective-permute-start | bytes 786440 | tf_op jit(solution)/shard_map/ppermute | solution.py:182
  81.2 8.1 %collective-permute-start.13 = (bf16[1024,128]{1,0:T(8,128)(2,1)}, bf16[1024,128]{1,0:T(8,128)(2,1)S(1)}, u32[]{:S(2)}, u32[]{:S(2)}) collective-permute-start(bf16[1024,128]{1,0:T(8,128)(2,1)} %get-tuple-element.84), channel_id=1, source_target_pairs={{0,24},{8,0},{16,8},{24,16},{1,25},{9,1},{17,9},{25,17},{2,26},{10... | collective-permute-start | bytes 786440 | tf_op jit(solution)/shard_map/ppermute | solution.py:182
  83.9 10.7 %copy-start.1 = (bf16[2048,128]{1,0:T(8,128)(2,1)S(1)}, bf16[2048,128]{1,0:T(8,128)(2,1)}, u32[]{:S(2)}) copy-start(bf16[2048,128]{1,0:T(8,128)(2,1)} %copy-done) | copy-start | bytes 1572868
  83.9 10.7 %copy-start.3 = (bf16[2048,128]{1,0:T(8,128)(2,1)S(1)}, bf16[2048,128]{1,0:T(8,128)(2,1)}, u32[]{:S(2)}) copy-start(bf16[2048,128]{1,0:T(8,128)(2,1)} %copy-done.2) | copy-start | bytes 1572868
  83.9 8.4 %collective-permute-start.14 = (bf16[1024,128]{1,0:T(8,128)(2,1)}, bf16[1024,128]{1,0:T(8,128)(2,1)S(1)}, u32[]{:S(2)}, u32[]{:S(2)}) collective-permute-start(bf16[1024,128]{1,0:T(8,128)(2,1)} %get-tuple-element.85), channel_id=1, source_target_pairs={{0,6},{2,0},{4,2},{6,4},{1,7},{3,1},{5,3},{7,5},{8,14},{10,8},{12,... | collective-permute-start | bytes 786440 | tf_op jit(solution)/shard_map/ppermute | solution.py:182
  83.9 1.1 %copy-start.5 = (bf16[2048,128]{1,0:T(8,128)(2,1)S(1)}, bf16[2048,128]{1,0:T(8,128)(2,1)}, u32[]{:S(2)}) copy-start(bf16[2048,128]{1,0:T(8,128)(2,1)} %copy-done.4) | copy-start | bytes 1572868
  92.3 5.9 %collective-permute-start.16 = (bf16[1024,128]{1,0:T(8,128)(2,1)S(1)}, bf16[1024,128]{1,0:T(8,128)(2,1)S(1)}, u32[]{:S(2)}, u32[]{:S(2)}) collective-permute-start(bf16[1024,128]{1,0:T(8,128)(2,1)S(1)} %collective-permute-done.11.refs_0_), channel_id=1, source_target_pairs={{0,32},{32,0},{1,33},{33,1},{2,34},{34,2},{3,35},{35,3},{4,36},{36... | collective-permute-start | bytes 786440 | tf_op jit(solution)/shard_map/ppermute | solution.py:182
  94.0 4.2 %collective-permute-start.17 = (bf16[1024,128]{1,0:T(8,128)(2,1)S(1)}, bf16[1024,128]{1,0:T(8,128)(2,1)S(1)}, u32[]{:S(2)}, u32[]{:S(2)}) collective-permute-start(bf16[1024,128]{1,0:T(8,128)(2,1)S(1)} %collective-permute-done.12.refs_1_), channel_id=1, source_target_pairs={{0,32},{32,0},{1,33},{33,1},{2,34},{34,2},{3,35},{35,3},{4,36},{36... | collective-permute-start | bytes 786440 | tf_op jit(solution)/shard_map/ppermute | solution.py:182
  94.0 4.2 %collective-permute-start.18 = (bf16[1024,128]{1,0:T(8,128)(2,1)S(1)}, bf16[1024,128]{1,0:T(8,128)(2,1)S(1)}, u32[]{:S(2)}, u32[]{:S(2)}) collective-permute-start(bf16[1024,128]{1,0:T(8,128)(2,1)S(1)} %collective-permute-done.13.refs_2_), channel_id=1, source_target_pairs={{0,32},{32,0},{1,33},{33,1},{2,34},{34,2},{3,35},{35,3},{4,36},{36... | collective-permute-start | bytes 786440 | tf_op jit(solution)/shard_map/ppermute | solution.py:182
  94.5 3.7 %collective-permute-start.19 = (bf16[1024,128]{1,0:T(8,128)(2,1)S(1)}, bf16[1024,128]{1,0:T(8,128)(2,1)S(1)}, u32[]{:S(2)}, u32[]{:S(2)}) collective-permute-start(bf16[1024,128]{1,0:T(8,128)(2,1)S(1)} %collective-permute-done.14.refs_3_), channel_id=1, source_target_pairs={{0,32},{32,0},{1,33},{33,1},{2,34},{34,2},{3,35},{35,3},{4,36},{36... | collective-permute-start | bytes 786440 | tf_op jit(solution)/shard_map/ppermute | solution.py:182

commit v3 on v2

--- a/solution.py
+++ b/solution.py
@@ -16,6 +16,10 @@
 
 def cost(size):
     return pl.CostEstimate(flops=0, bytes_accessed=size, transcendentals=0)
+
+
+def limit(size):
+    return pltpu.CompilerParams(vmem_limit_bytes=size * 2**20)
 
 
 def inside(value):
@@ -31,11 +35,25 @@
     return (new_param, new_first, new_second)
 
 
-def pack_kernel(grad_a, grad_b, out):
+def fetched(there, here, sems):
+    copies = [pltpu.make_async_copy(t, h, sems.at[i]) for i, (t, h) in enumerate(zip(there, here))]
+    for copy in copies:
+        copy.start()
+    return copies
+
+
+def pack_kernel(*refs):
+    there, out, here = refs[:8], refs[8], refs[9:15]
+    grad_a, grad_b, sems = refs[15:]
+    copies = fetched(there, (grad_a, grad_b, *here), sems)
+    copies[0].wait()
+    copies[1].wait()
     out[:, 0:128, :] = grad_a[0].reshape(8, 128, 128).astype(HALF)
     for owner in range(8):
         pair = jnp.concatenate([grad_b[0, 2 * owner], grad_b[0, 2 * owner + 1]], axis=-1)
         out[owner, 128:176, :] = pair.astype(HALF)
+    for copy in copies[2:]:
+        copy.wait()
 
 
 def summed(got):
@@ -116,65 +134,57 @@
         everything[2048 * k : 2048 * k + 2048] = piece[...]
 
 
-def merge_kernel(place, blocks, *refs, distances, pick):
+def stash_kernel(base, kept, sems):
+    for copy in fetched([base.at[zl] for zl in range(4)], [kept.at[zl] for zl in range(4)], sems):
+        copy.wait()
+
+
+def merge_kernel(place, blocks, base, *refs, distances, pick):
     n = len(distances)
-    pieces = pick(refs)
-    base, out, held, read, write = refs[-5:]
+    out, held, write = refs[-3:]
     x, y, core = place[0], place[1], place[2]
 
-    def unit(h, d, inner):
+    def unit(d, h, inner):
         ky, kx = (distances[d], inner) if h == 0 else (inner, distances[d])
         column = lax.rem(y + 4 - ky, 4) * 1024 + lax.rem(x + 4 - kx, 4) * 256
-        return pl.ds(pl.multiple_of(column, 256), 256), (h * n + d) * 4 + inner
-
-    def copy_in(h, d, inner):
-        where, u = unit(h, d, inner)
-        return pltpu.make_async_copy(base.at[:, :, h, :, where], held.at[u], read.at[u])
-
-    def copy_out(h, d, inner):
-        where, u = unit(h, d, inner)
+        return pl.ds(pl.multiple_of(column, 256), 256), (d * 2 + h) * 4 + inner
+
+    def copy_out(d, h, inner):
+        where, u = unit(d, h, inner)
         return pltpu.make_async_copy(held.at[u], out.at[:, :, h, :, where], write.at[u])
 
-    units = [(h, d, inner) for d in range(n) for h in range(2) for inner in range(4)]
-    for t in units:
-        copy_in(*t).start()
-    for d in range(n):
-        for h in range(2):
-            for inner in range(4):
-                copy_in(h, d, inner).wait()
-            for side in range(2):
-                piece = jnp.concatenate([p[...] for p in pieces[side][h]]).reshape(4, 4, 2, 64, 128)
-                wide = jnp.concatenate(
-                    [piece[i, :, zh].reshape(256, 128) for i in range(4) for zh in range(2)], axis=-1
-                )
-                delta = jnp.dot(blocks[side, h], wide, preferred_element_type=jnp.float32)
-                owner = core if side == 0 else 1 - core
-                for inner in range(4):
-                    u = (h * n + d) * 4 + inner
-                    old = held[u, :, owner].astype(jnp.float32)
-                    part = delta[:, 256 * inner : 256 * inner + 256].reshape(4, 48, 256)
-                    held[u, :, owner] = (old + 0.125 * part).astype(HALF)
-            for inner in range(4):
-                copy_out(h, d, inner).start()
+    units = [(d, h, inner) for d in range(n) for h in range(2) for inner in range(4)]
+    for d, h, inner in units:
+        where, u = unit(d, h, inner)
+        for side in range(2):
+            ref, row = pick(refs, side, d, h, inner)
+            piece = ref[row : row + 512].reshape(4, 2, 64, 128)
+            wide = jnp.concatenate([piece[:, zh].reshape(256, 128) for zh in range(2)], axis=-1)
+            delta = jnp.dot(blocks[side, h], wide, preferred_element_type=jnp.float32)
+            owner = core if side == 0 else 1 - core
+            old = base[:, owner, h, :, where].astype(jnp.float32)
+            held[u, :, owner] = (old + 0.125 * delta.reshape(4, 48, 256)).astype(HALF)
+        copy_out(d, h, inner).start()
     for t in units:
         copy_out(*t).wait()
 
 
-def next_merge_kernel(place, blocks, *refs, distances, pick):
-    merge_kernel(place, blocks, *refs[:-5], *refs[-4:], distances=distances, pick=pick)
-
-
-def pick_first(refs):
-    return [[[refs[side].at[2048 * h : 2048 * h + 2048]] for h in range(2)] for side in range(2)]
-
-
-def pick_near(refs, start):
-    other = [[refs[2].at[start + 2048 * h : start + 2048 * h + 2048]] for h in range(2)]
-    return [[[refs[0]], [refs[1]]], other]
-
-
-def pick_far(refs):
-    return [[[refs[4 * side + h], refs[4 * side + 2 + h]] for h in range(2)] for side in range(2)]
+def next_merge_kernel(place, blocks, base, *refs, **how):
+    merge_kernel(place, blocks, base, *refs[:-4], *refs[-3:], **how)
+
+
+def pick_first(refs, side, d, h, inner):
+    return refs[side], 2048 * h + 512 * inner
+
+
+def pick_near(refs, side, d, h, inner):
+    if side == 0:
+        return refs[2 * d + h], 512 * inner
+    return refs[4], 2048 * (2 * d + h) + 512 * inner
+
+
+def pick_far(refs, side, d, h, inner):
+    return refs[4 * side + 2 * (inner // 2) + h], 512 * (inner % 2)
 
 
 def hop(value, axis, k):
@@ -192,20 +202,24 @@
 ):
     f32 = jnp.float32
     shape = jax.ShapeDtypeStruct
-    packed = pl.pallas_call(
+    sa, sb = shape((2, 64, 128), f32), shape((2, 48, 64), f32)
+    needed = (grad_a, grad_b, factor_a, factor_b, moment_a, second_a, moment_b, second_b)
+    packed, *state = pl.pallas_call(
         pack_kernel,
-        out_shape=pltpu.VMEM((8, 176, 128), HALF),
-        in_specs=[VMEM] * 2,
-        out_specs=VMEM,
-    )(grad_a, grad_b)
+        out_shape=[pltpu.VMEM((8, 176, 128), HALF)] + [pltpu.VMEM(v.shape, f32) for v in needed[2:]],
+        in_specs=[HBM] * 8,
+        out_specs=[VMEM] * 7,
+        scratch_shapes=[pltpu.VMEM(v.shape, f32) for v in needed[:2]] + [pltpu.SemaphoreType.DMA((8,))],
+        compiler_params=limit(4),
+    )(*[pltpu.with_memory_space_constraint(v, pltpu.HBM) for v in needed])
     got = lax.all_to_all(packed, ("zl", "core"), 0, 0, tiled=True)
-    sa, sb = shape((2, 64, 128), f32), shape((2, 48, 64), f32)
-    state = (factor_a, factor_b, moment_a, second_a, moment_b, second_b)
+    state = [inside(v) for v in state]
     send, total = pl.pallas_call(
         send_kernel,
-        out_shape=(pltpu.VMEM((8, 176, 128), HALF), shape((176, 128), f32)),
+        out_shape=(pltpu.VMEM((8, 176, 128), HALF), pltpu.VMEM((176, 128), f32)),
         in_specs=[VMEM] * 7,
         out_specs=(VMEM,) * 2,
+        compiler_params=limit(4),
     )(inside(got), *state)
     line = lax.all_to_all(send, ("zl", "zh"), 0, 0, tiled=True)
 
@@ -215,6 +229,7 @@
         out_shape=(pltpu.VMEM((512, 128), HALF), pltpu.VMEM((512, 128), HALF), pltpu.VMEM((4, 48, 128), HALF)),
         in_specs=[SMEM, VMEM],
         out_specs=(VMEM,) * 3,
+        compiler_params=limit(4),
     )(zh.reshape(1), inside(line))
     halves = half_0, half_1
 
@@ -223,29 +238,41 @@
     parts = lax.optimization_barrier(parts)
     mine_0, mine_1, everything = pl.pallas_call(
         join_kernel,
-        out_shape=(shape((2048, 128), HALF),) * 2 + (shape((4288, 128), HALF),),
+        out_shape=(pltpu.VMEM((2048, 128), HALF),) * 2 + (pltpu.VMEM((4288, 128), HALF),),
         in_specs=[VMEM] * 9,
         out_specs=(VMEM,) * 3,
+        compiler_params=limit(6),
     )(*[inside(p) for p in parts[0] + parts[1]], inside(rows_own))
     mine = mine_0, mine_1
     near = [hop(mine[h], second[h], k) for k in (1, 3) for h in range(2)]
     other = hop(everything, "core", 1)
+    base, mine_0 = lax.optimization_barrier((base_rows, mine_0))
+    base = pl.pallas_call(
+        stash_kernel,
+        out_shape=pltpu.VMEM((4, 2, 2, 48, 4096), HALF),
+        in_specs=[HBM],
+        out_specs=VMEM,
+        scratch_shapes=[pltpu.SemaphoreType.DMA((4,))],
+        compiler_params=limit(2),
+        cost_estimate=cost(1024),
+    )(pltpu.with_memory_space_constraint(base.reshape(4, 2, 2, 48, 4096), pltpu.HBM))
     blocks = pl.pallas_call(
         blocks_kernel,
         out_shape=pltpu.VMEM((2, 2, 192, 256), HALF),
         in_specs=[VMEM] * 2,
         out_specs=VMEM,
+        compiler_params=limit(4),
     )(inside(rows_own), inside(other))
     states = pl.pallas_call(
         state_kernel,
         out_shape=(sa, sb, sa, sa, sb, sb),
         in_specs=[VMEM] * 7,
         out_specs=[VMEM] * 6,
+        compiler_params=limit(4),
         cost_estimate=cost(1024),
-    )(total, *state)
+    )(inside(total), *state)
 
     place = jnp.stack([x, y, core])
-    base = pltpu.with_memory_space_constraint(base_rows.reshape(4, 2, 2, 48, 4096), pltpu.HBM)
 
     def merge(distances, pick, pieces, before):
         n = len(distances)
@@ -253,17 +280,16 @@
         return pl.pallas_call(
             functools.partial(next_merge_kernel if before else merge_kernel, distances=distances, pick=pick),
             out_shape=shape((4, 2, 2, 48, 4096), HALF),
-            in_specs=[SMEM, VMEM] + [VMEM] * len(pieces) + [HBM] + [HBM] * len(before),
+            in_specs=[SMEM, VMEM, VMEM] + [VMEM] * len(pieces) + [HBM] * len(before),
             out_specs=HBM,
             input_output_aliases={3 + len(pieces): 0} if before else {},
             scratch_shapes=[
                 pltpu.VMEM((8 * n, 4, 2, 48, 256), HALF),
                 pltpu.SemaphoreType.DMA((8 * n,)),
-                pltpu.SemaphoreType.DMA((8 * n,)),
             ],
-            compiler_params=pltpu.CompilerParams(vmem_limit_bytes=(6 + 4 * n) * 1024 * 1024),
+            compiler_params=limit(2 + 2 * n),
             cost_estimate=cost(1024),
-        )(place, inside(blocks), *pieces, base, *before)
+        )(place, inside(blocks), inside(base), *[inside(v) for v in pieces], *before)
 
     merged = merge((0,), pick_first, [everything, other], None)
     near, merged, states = lax.optimization_barrier((near, merged, states))
@@ -273,13 +299,13 @@
         out_shape=(half,) * 4 + (shape((8192, 128), HALF),),
         in_specs=[VMEM] * 4,
         out_specs=(VMEM,) * 5,
+        compiler_params=limit(8),
     )(*near)
     far = [hop(relayed[2 * s + h], second[h], 1 + 2 * s) for s in range(2) for h in range(2)]
     near_other = hop(everything, "core", 1)
-    merged = merge((1,), functools.partial(pick_near, start=0), near[:2] + [near_other], merged)
+    merged = merge((1, 3), pick_near, [*near, near_other], merged)
     far, merged = lax.optimization_barrier((far, merged))
     far_other = [hop(v, "core", 1) for v in far]
-    merged = merge((3,), functools.partial(pick_near, start=4096), near[2:] + [near_other], merged)
     merged = merge((2,), pick_far, far + far_other, merged)
     new_a, new_b, new_ma, new_va, new_mb, new_vb = states
     return (new_a, new_b, new_ma, new_va, new_mb, new_vb, merged.reshape(16, 48, 4096))

time: 103 us -> 95.6 us (0.928)
  Pallas kernels: 24.8 us -> 19.6 us
    pallas_call x4 -> x3, Pallas kernels: 14.9 us -> 11.7 us  [merge(): pl.pallas_call(functools.partial(next_merge_kernel if before else merge_k...]
    pallas_call x1, Pallas kernels: 3.21 us -> 0.2 us  [per_device(): pl.pallas_call(relay_kernel, out_shape=(half,) * 4 + (shape((8192, 128),...]
    pallas_call x3 -> x4, Pallas kernels: 4.76 us -> 6.78 us  [the longest x1 2.87 us: per_device(): pl.pallas_call(stash_kernel, out_shape=pltpu.VMEM((4, 2, 2, 48, 4096), HA...]
    unnamed x14 -> x8, local copies, waits for them, and re-layouts: 3.15 us -> 2.33 us
  transfers between devices with their start and end apart: 21 -> 21, of which waited for: 9 -> 12; matrix products, arithmetic and copies ran while one was open for 0% -> 0% of each run, Pallas kernels for 13% -> 13%
where the time goes in v3:
time: 95.6 us; the launch traced here: 95.3 us
  waiting for transfers between devices  28.6 us (30%)
  starting transfers between devices  28 us (29%)
  Pallas kernels  19.6 us (21%)
  blocking collectives  15.8 us (17%)
  local copies, waits for them, and re-layouts  2.33 us (2%)
    ppermute x20, starting transfers between devices, hop(): return lax.ppermute(value, axis, [(i, (i + k) % n) for i in range(n)])  21.1 us
    ppermute x20, waiting for transfers between devices, hop(): return lax.ppermute(value, axis, [(i, (i + k) % n) for i in range(n)])  15.8 us
    all_to_all x1, blocking collectives, per_device(): got = lax.all_to_all(packed, ('zl', 'core'), 0, 0, tiled=True)  15.8 us
    all_to_all x1, waiting for transfers between devices, per_device(): line = lax.all_to_all(send, ('zl', 'zh'), 0, 0, tiled=True)  12.8 us
    pallas_call x3, Pallas kernels, merge(): pl.pallas_call(functools.partial(next_merge_kernel if before else merge_k...  11.7 us
    all_to_all x1, starting transfers between devices, per_device(): line = lax.all_to_all(send, ('zl', 'zh'), 0, 0, tiled=True)  6.93 us
    pallas_call x1, Pallas kernels, per_device(): pl.pallas_call(stash_kernel, out_shape=pltpu.VMEM((4, 2, 2, 48, 4096), HA...  2.87 us
    unnamed x8, local copies, waits for them, and re-layouts  2.33 us
  transfers between devices with their start and end apart: 21, of which 12 were waited for; matrix products, arithmetic and copies ran while one was open for 0% of the time, Pallas kernels for 13%

profile of v3, /device:TPU:39, one launch (start us, length us, event | category | flops | bytes accessed | tf_op | source)
XLA Modules:
  0.0 95.3 jit_solution(4520074931844004521)
XLA Ops:
  0.6 1.4 %shard_map.144 = (bf16[8,176,128]{2,1,0:T(8,128)(2,1)S(1)}, f32[2,64,128]{2,1,0:T(8,128)S(1)}, f32[2,48,64]{2,1,0:T(8,128)S(1)}, f32[2,64,128]{2,1,0:T(8,128)S(1...) custom-call(f32[1,16,64,128]{3,2,1,0:T(8,128)} %refs_0_.1, ...), custom_call_target="tpu_custom_call" | custom-call | tf_op jit(solution)/shard_map/pallas_call | solution.py:207
  2.0 0.0 copy-start
  2.0 15.8 %all_to_all.10.got = bf16[8,176,128]{2,1,0:T(8,128)(2,1)S(1)} all-to-all(bf16[8,176,128]{2,1,0:T(8,128)(2,1)S(1)} %get-tuple-element.58), channel_id=1, replica_groups=mesh['zl'=4,'core'=2,'y'=4,'x'=4,'zh'=2] {'zl','core'}, dimensions={0} | all-to-all | bytes 720896 | tf_op jit(solution)/shard_map/all_to_all | solution.py:215
  17.8 0.9 shard_map.145
  18.7 0.0 copy-start.2
  18.7 0.6 copy-done.2
  19.4 6.9 %all-to-all-start.1 = ((bf16[8,176,128]{2,1,0:T(8,128)(2,1)}), bf16[8,176,128]{2,1,0:T(8,128)(2,1)S(1)}, u32[]{:S(2)}, u32[]{:S(2)}) async-start(bf16[8,176,128]{2,1,0:T(8,128)(2,1)} %get-tuple-element.65), calls=%async_computation.1 | async-start | bytes 720896 | tf_op jit(solution)/shard_map/all_to_all | solution.py:224
  26.3 12.8 %all-to-all-done.1.line = bf16[8,176,128]{2,1,0:T(8,128)(2,1)S(1)} async-done(((bf16[8,176,128]{2,1,0:T(8,128)(2,1)}), bf16[8,176,128]{2,1,0:T(8,128)(2,1)S(1)}, u32[]{:S(2)}, u32[]{:S(2)}) %all-to-all-start.1) | async-done | bytes 360480 | tf_op jit(solution)/shard_map/all_to_all | solution.py:224
  39.1 0.0 copy-done
  39.1 0.6 collective-permute-start.2
  39.7 0.8 collective-permute-start.1
  40.6 1.8 %collective-permute-start = (bf16[512,128]{1,0:T(8,128)(2,1)S(1)}, bf16[512,128]{1,0:T(8,128)(2,1)S(1)}, u32[]{:S(2)}, u32[]{:S(2)}) collective-permute-start(bf16[512,128]{1,0:T(8,128)(2,1)S(1)} %get-tuple-element.68.refs_0_), channel_id=1, source_target_pairs={{0,2},{2,4},{4,6},{6,0},{1,3},{3,5},{5,7},{7,1},{8,10},{10,12},{12... | collective-permute-start | bytes 393224 | tf_op jit(solution)/shard_map/ppermute | solution.py:192
  42.4 2.7 %collective-permute-start.5 = (bf16[512,128]{1,0:T(8,128)(2,1)S(1)}, bf16[512,128]{1,0:T(8,128)(2,1)S(1)}, u32[]{:S(2)}, u32[]{:S(2)}) collective-permute-start(bf16[512,128]{1,0:T(8,128)(2,1)S(1)} %get-tuple-element.72.refs_4_), channel_id=1, source_target_pairs={{0,24},{8,0},{16,8},{24,16},{1,25},{9,1},{17,9},{25,17},{2,26},{10... | collective-permute-start | bytes 393224 | tf_op jit(solution)/shard_map/ppermute | solution.py:192
  45.1 0.3 collective-permute-start.4
  45.5 2.3 %collective-permute-done.2.refs_3_ = bf16[512,128]{1,0:T(8,128)(2,1)S(1)} collective-permute-done((bf16[512,128]{1,0:T(8,128)(2,1)S(1)}, bf16[512,128]{1,0:T(8,128)(2,1)S(1)}, u32[]{:S(2)}, u32[]{:S(2)}) %collective-permute-start.2) | collective-permute-done | bytes 131104 | tf_op jit(solution)/shard_map/ppermute | solution.py:192
  47.7 1.3 %collective-permute-start.3 = (bf16[512,128]{1,0:T(8,128)(2,1)S(1)}, bf16[512,128]{1,0:T(8,128)(2,1)S(1)}, u32[]{:S(2)}, u32[]{:S(2)}) collective-permute-start(bf16[512,128]{1,0:T(8,128)(2,1)S(1)} %get-tuple-element.72.refs_4_), channel_id=1, source_target_pairs={{0,8},{8,16},{16,24},{24,0},{1,9},{9,17},{17,25},{25,1},{2,10},{10... | collective-permute-start | bytes 393224 | tf_op jit(solution)/shard_map/ppermute | solution.py:192
  49.0 0.0 collective-permute-done.1.refs_2_
  49.0 0.0 collective-permute-done.refs_1_
  49.0 0.0 collective-permute-done.5.refs_7_
  49.0 1.4 %collective-permute-done.4.refs_6_ = bf16[512,128]{1,0:T(8,128)(2,1)S(1)} collective-permute-done((bf16[512,128]{1,0:T(8,128)(2,1)S(1)}, bf16[512,128]{1,0:T(8,128)(2,1)S(1)}, u32[]{:S(2)}, u32[]{:S(2)}) %collective-permute-start.4) | collective-permute-done | bytes 131104 | tf_op jit(solution)/shard_map/ppermute | solution.py:192
  50.4 4.7 %collective-permute-done.3.refs_5_ = bf16[512,128]{1,0:T(8,128)(2,1)S(1)} collective-permute-done((bf16[512,128]{1,0:T(8,128)(2,1)S(1)}, bf16[512,128]{1,0:T(8,128)(2,1)S(1)}, u32[]{:S(2)}, u32[]{:S(2)}) %collective-permute-start.3) | collective-permute-done | bytes 131104 | tf_op jit(solution)/shard_map/ppermute | solution.py:192
  55.2 1.6 %shard_map.147 = (bf16[2048,128]{1,0:T(8,128)(2,1)}, bf16[2048,128]{1,0:T(8,128)(2,1)}, bf16[4288,128]{1,0:T(8,128)(2,1)}) custom-call(bf16[512,128]{1,0:T(8,128)(2,1)S(1)} %get-tuple-element.68.refs_0_, bf16[512,128]{1,0:T(8,128)(2,1)S(1)} %collective-permute-done.refs_1_, bf16[512,128]{1,0:T(8,128)(2,1)S(1)} %collective-permute-done.1.refs_2_, ...), custom_call_target="tpu_custom_call" | custom-call | tf_op jit(solution)/shard_map/pallas_call | solution.py:239
  56.8 1.0 %collective-permute-start.10 = (bf16[4288,128]{1,0:T(8,128)(2,1)}, bf16[4288,128]{1,0:T(8,128)(2,1)S(1)}, u32[]{:S(2)}, u32[]{:S(2)}) collective-permute-start(bf16[4288,128]{1,0:T(8,128)(2,1)} %get-tuple-element.79.refs_0_), channel_id=1, source_target_pairs={{0,32},{32,0},{1,33},{33,1},{2,34},{34,2},{3,35},{35,3},{4,36},{36... | collective-permute-start | bytes 3293192 | tf_op jit(solution)/shard_map/ppermute | solution.py:192
  57.8 0.0 collective-permute-start.9
  57.8 2.7 %collective-permute-start.7 = (bf16[2048,128]{1,0:T(8,128)(2,1)}, bf16[2048,128]{1,0:T(8,128)(2,1)S(1)}, u32[]{:S(2)}, u32[]{:S(2)}) collective-permute-start(bf16[2048,128]{1,0:T(8,128)(2,1)} %get-tuple-element.78), channel_id=1, source_target_pairs={{0,2},{2,4},{4,6},{6,0},{1,3},{3,5},{5,7},{7,1},{8,10},{10,12},{12... | collective-permute-start | bytes 1572872 | tf_op jit(solution)/shard_map/ppermute | solution.py:192
  60.5 0.6 collective-permute-start.8
  61.1 0.8 collective-permute-start.6
  61.9 0.1 pad_add_fusion.place
  62.0 0.0 copy-start.1
  62.0 0.8 copy-done.1
  62.8 0.0 copy-start.3
  62.8 0.9 copy-done.3
  63.7 0.8 shard_map.151
  64.5 2.9 %shard_map.149.base = bf16[4,2,2,48,4096]{4,3,2,1,0:T(8,128)(2,1)S(1)} custom-call(bf16[4,2,2,48,4096]{4,3,2,1,0:T(8,128)(2,1)} %bitcast.7), custom_call_target="tpu_custom_call" | custom-call | bytes 1024 | tf_op jit(solution)/shard_map/pallas_call | solution.py:250
  67.4 0.0 collective-permute-done.10.other.refs_1_
  67.4 0.1 shard_map.148.blocks
  67.5 3.8 %shard_map.150.refs_5_ = bf16[4,2,2,48,4096]{4,3,2,1,0:T(8,128)(2,1)} custom-call(s32[3]{0:T(128)S(1)} %pad_add_fusion.place, bf16[2,2,192,256]{3,2,1,0:T(8,128)(2,1)S(1)} %shard_map.148.blocks, bf16[4,2,2,48,4096]{4,3,2,1,0:T(8,128)(2,1)S(1)} %shard_map.149.base, bf16[4288,128]{1,0:T(8,128)(2,1)} %get-tuple-element.79.refs_0_, ...), custom_call_target="tpu_custom_call" | custom-call | bytes 1024 | tf_op jit(solution)/shard_map/pallas_call | solution.py:280
  71.2 1.5 %collective-permute-done.9.down_1.refs_3_ = bf16[2048,128]{1,0:T(8,128)(2,1)S(1)} collective-permute-done((bf16[2048,128]{1,0:T(8,128)(2,1)}, bf16[2048,128]{1,0:T(8,128)(2,1)S(1)}, u32[]{:S(2)}, u32[]{:S(2)}) %collective-permute-start.9) | collective-permute-done | bytes 524320 | tf_op jit(solution)/shard_map/ppermute | solution.py:192
  72.8 0.0 collective-permute-done.7.up_1.refs_1_
  72.8 0.8 collective-permute-done.8.down_0.refs_2_
  73.6 1.5 %collective-permute-done.6.up_0.refs_0_ = bf16[2048,128]{1,0:T(8,128)(2,1)S(1)} collective-permute-done((bf16[2048,128]{1,0:T(8,128)(2,1)}, bf16[2048,128]{1,0:T(8,128)(2,1)S(1)}, u32[]{:S(2)}, u32[]{:S(2)}) %collective-permute-start.6) | collective-permute-done | bytes 524320 | tf_op jit(solution)/shard_map/ppermute | solution.py:192
  75.1 0.2 shard_map.152
  75.3 1.8 %collective-permute-start.15 = (bf16[8192,128]{1,0:T(8,128)(2,1)S(1)}, bf16[8192,128]{1,0:T(8,128)(2,1)S(1)}, u32[]{:S(2)}, u32[]{:S(2)}) collective-permute-start(bf16[8192,128]{1,0:T(8,128)(2,1)S(1)} %get-tuple-element.102), channel_id=1, source_target_pairs={{0,32},{32,0},{1,33},{33,1},{2,34},{34,2},{3,35},{35,3},{4,36},{36... | collective-permute-start | bytes 6291464 | tf_op jit(solution)/shard_map/ppermute | solution.py:192
  77.2 0.0 collective-permute-start.11
  77.2 0.0 collective-permute-start.12
  77.2 2.7 %collective-permute-start.13 = (bf16[1024,128]{1,0:T(8,128)(2,1)S(1)}, bf16[1024,128]{1,0:T(8,128)(2,1)S(1)}, u32[]{:S(2)}, u32[]{:S(2)}) collective-permute-start(bf16[1024,128]{1,0:T(8,128)(2,1)S(1)} %get-tuple-element.100), channel_id=1, source_target_pairs={{0,24},{8,0},{16,8},{24,16},{1,25},{9,1},{17,9},{25,17},{2,26},{10... | collective-permute-start | bytes 786440 | tf_op jit(solution)/shard_map/ppermute | solution.py:192
  79.9 1.5 %collective-permute-start.14 = (bf16[1024,128]{1,0:T(8,128)(2,1)S(1)}, bf16[1024,128]{1,0:T(8,128)(2,1)S(1)}, u32[]{:S(2)}, u32[]{:S(2)}) collective-permute-start(bf16[1024,128]{1,0:T(8,128)(2,1)S(1)} %get-tuple-element.101), channel_id=1, source_target_pairs={{0,6},{2,0},{4,2},{6,4},{1,7},{3,1},{5,3},{7,5},{8,14},{10,8},{12,... | collective-permute-start | bytes 786440 | tf_op jit(solution)/shard_map/ppermute | solution.py:192
  81.3 0.0 collective-permute-done.15.refs_4_
  81.3 4.9 %shard_map.153.refs_8_ = bf16[4,2,2,48,4096]{4,3,2,1,0:T(8,128)(2,1)} custom-call(s32[3]{0:T(128)S(1)} %pad_add_fusion.place, bf16[2,2,192,256]{3,2,1,0:T(8,128)(2,1)S(1)} %shard_map.148.blocks, bf16[4,2,2,48,4096]{4,3,2,1,0:T(8,128)(2,1)S(1)} %shard_map.149.base, ...), custom_call_target="tpu_custom_call", output_to_operand_aliasing={{}: (8, {})} | custom-call | bytes 1024 | tf_op jit(solution)/shard_map/pallas_call | solution.py:280
  86.2 0.0 collective-permute-done.11.refs_0_
  86.2 0.0 collective-permute-done.12.refs_1_
  86.2 0.0 collective-permute-done.13.refs_2_
  86.3 1.7 %collective-permute-done.14.refs_3_ = bf16[1024,128]{1,0:T(8,128)(2,1)S(1)} collective-permute-done((bf16[1024,128]{1,0:T(8,128)(2,1)S(1)}, bf16[1024,128]{1,0:T(8,128)(2,1)S(1)}, u32[]{:S(2)}, u32[]{:S(2)}) %collective-permute-start.14) | collective-permute-done | bytes 262176 | tf_op jit(solution)/shard_map/ppermute | solution.py:192
  88.0 1.8 %collective-permute-start.16 = (bf16[1024,128]{1,0:T(8,128)(2,1)S(1)}, bf16[1024,128]{1,0:T(8,128)(2,1)S(1)}, u32[]{:S(2)}, u32[]{:S(2)}) collective-permute-start(bf16[1024,128]{1,0:T(8,128)(2,1)S(1)} %collective-permute-done.11.refs_0_), channel_id=1, source_target_pairs={{0,32},{32,0},{1,33},{33,1},{2,34},{34,2},{3,35},{35,3},{4,36},{36... | collective-permute-start | bytes 786440 | tf_op jit(solution)/shard_map/ppermute | solution.py:192
  89.8 0.0 collective-permute-start.17
  89.8 0.5 collective-permute-start.18
  90.3 0.0 collective-permute-start.19
  90.3 0.6 collective-permute-done.16.refs_4_
  91.0 0.4 collective-permute-done.17.refs_5_
  91.3 0.4 collective-permute-done.18.refs_6_
  91.7 0.4 collective-permute-done.19.refs_7_
  92.1 3.0 %shard_map.154 = bf16[4,2,2,48,4096]{4,3,2,1,0:T(8,128)(2,1)} custom-call(s32[3]{0:T(128)S(1)} %pad_add_fusion.place, bf16[2,2,192,256]{3,2,1,0:T(8,128)(2,1)S(1)} %shard_map.148.blocks, bf16[4,2,2,48,4096]{4,3,2,1,0:T(8,128)(2,1)S(1)} %shard_map.149.base, bf16[1024,128]{1,0:T(8,128)(2,1)S(1)} %collective-permute-done.11.refs_0_, ...), custom_call_target="tpu_custom_call", output_to_operand_aliasing={{}: (11, {})} | custom-call | bytes 1024 | tf_op jit(solution)/shard_map/pallas_call | solution.py:280
  (1 shorter events, 0.0 us)
Async XLA Ops:
  2.0 37.1 %copy-start = (f32[2,48,64]{2,1,0:T(8,128)}, f32[2,48,64]{2,1,0:T(8,128)S(1)}, u32[]{:S(2)}) copy-start(f32[2,48,64]{2,1,0:T(8,128)S(1)} %get-tuple-element.64.second_b) | copy-start | bytes 73732
  18.7 0.6 copy-start.2
  19.4 19.7 %all-to-all-start.1 = ((bf16[8,176,128]{2,1,0:T(8,128)(2,1)}), bf16[8,176,128]{2,1,0:T(8,128)(2,1)S(1)}, u32[]{:S(2)}, u32[]{:S(2)}) async-start(bf16[8,176,128]{2,1,0:T(8,128)(2,1)} %get-tuple-element.65), calls=%async_computation.1 | async-start | bytes 720896 | tf_op jit(solution)/shard_map/all_to_all | solution.py:224
  39.1 8.6 %collective-permute-start.2 = (bf16[512,128]{1,0:T(8,128)(2,1)S(1)}, bf16[512,128]{1,0:T(8,128)(2,1)S(1)}, u32[]{:S(2)}, u32[]{:S(2)}) collective-permute-start(bf16[512,128]{1,0:T(8,128)(2,1)S(1)} %get-tuple-element.68.refs_0_), channel_id=1, source_target_pairs={{0,6},{2,0},{4,2},{6,4},{1,7},{3,1},{5,3},{7,5},{8,14},{10,8},{12,... | collective-permute-start | bytes 393224 | tf_op jit(solution)/shard_map/ppermute | solution.py:192
  39.7 9.3 %collective-permute-start.1 = (bf16[512,128]{1,0:T(8,128)(2,1)S(1)}, bf16[512,128]{1,0:T(8,128)(2,1)S(1)}, u32[]{:S(2)}, u32[]{:S(2)}) collective-permute-start(bf16[512,128]{1,0:T(8,128)(2,1)S(1)} %get-tuple-element.68.refs_0_), channel_id=1, source_target_pairs={{0,4},{2,6},{4,0},{6,2},{1,5},{3,7},{5,1},{7,3},{8,12},{10,14},{12... | collective-permute-start | bytes 393224 | tf_op jit(solution)/shard_map/ppermute | solution.py:192
  40.6 8.5 %collective-permute-start = (bf16[512,128]{1,0:T(8,128)(2,1)S(1)}, bf16[512,128]{1,0:T(8,128)(2,1)S(1)}, u32[]{:S(2)}, u32[]{:S(2)}) collective-permute-start(bf16[512,128]{1,0:T(8,128)(2,1)S(1)} %get-tuple-element.68.refs_0_), channel_id=1, source_target_pairs={{0,2},{2,4},{4,6},{6,0},{1,3},{3,5},{5,7},{7,1},{8,10},{10,12},{12... | collective-permute-start | bytes 393224 | tf_op jit(solution)/shard_map/ppermute | solution.py:192
  42.4 6.7 %collective-permute-start.5 = (bf16[512,128]{1,0:T(8,128)(2,1)S(1)}, bf16[512,128]{1,0:T(8,128)(2,1)S(1)}, u32[]{:S(2)}, u32[]{:S(2)}) collective-permute-start(bf16[512,128]{1,0:T(8,128)(2,1)S(1)} %get-tuple-element.72.refs_4_), channel_id=1, source_target_pairs={{0,24},{8,0},{16,8},{24,16},{1,25},{9,1},{17,9},{25,17},{2,26},{10... | collective-permute-start | bytes 393224 | tf_op jit(solution)/shard_map/ppermute | solution.py:192
  45.1 5.3 %collective-permute-start.4 = (bf16[512,128]{1,0:T(8,128)(2,1)S(1)}, bf16[512,128]{1,0:T(8,128)(2,1)S(1)}, u32[]{:S(2)}, u32[]{:S(2)}) collective-permute-start(bf16[512,128]{1,0:T(8,128)(2,1)S(1)} %get-tuple-element.72.refs_4_), channel_id=1, source_target_pairs={{0,16},{8,24},{16,0},{24,8},{1,17},{9,25},{17,1},{25,9},{2,18},{10... | collective-permute-start | bytes 393224 | tf_op jit(solution)/shard_map/ppermute | solution.py:192
  47.7 7.4 %collective-permute-start.3 = (bf16[512,128]{1,0:T(8,128)(2,1)S(1)}, bf16[512,128]{1,0:T(8,128)(2,1)S(1)}, u32[]{:S(2)}, u32[]{:S(2)}) collective-permute-start(bf16[512,128]{1,0:T(8,128)(2,1)S(1)} %get-tuple-element.72.refs_4_), channel_id=1, source_target_pairs={{0,8},{8,16},{16,24},{24,0},{1,9},{9,17},{17,25},{25,1},{2,10},{10... | collective-permute-start | bytes 393224 | tf_op jit(solution)/shard_map/ppermute | solution.py:192
  56.8 10.6 %collective-permute-start.10 = (bf16[4288,128]{1,0:T(8,128)(2,1)}, bf16[4288,128]{1,0:T(8,128)(2,1)S(1)}, u32[]{:S(2)}, u32[]{:S(2)}) collective-permute-start(bf16[4288,128]{1,0:T(8,128)(2,1)} %get-tuple-element.79.refs_0_), channel_id=1, source_target_pairs={{0,32},{32,0},{1,33},{33,1},{2,34},{34,2},{3,35},{35,3},{4,36},{36... | collective-permute-start | bytes 3293192 | tf_op jit(solution)/shard_map/ppermute | solution.py:192
  57.8 15.0 %collective-permute-start.9 = (bf16[2048,128]{1,0:T(8,128)(2,1)}, bf16[2048,128]{1,0:T(8,128)(2,1)S(1)}, u32[]{:S(2)}, u32[]{:S(2)}) collective-permute-start(bf16[2048,128]{1,0:T(8,128)(2,1)} %get-tuple-element.78), channel_id=1, source_target_pairs={{0,6},{2,0},{4,2},{6,4},{1,7},{3,1},{5,3},{7,5},{8,14},{10,8},{12,... | collective-permute-start | bytes 1572872 | tf_op jit(solution)/shard_map/ppermute | solution.py:192
  57.8 15.0 %collective-permute-start.7 = (bf16[2048,128]{1,0:T(8,128)(2,1)}, bf16[2048,128]{1,0:T(8,128)(2,1)S(1)}, u32[]{:S(2)}, u32[]{:S(2)}) collective-permute-start(bf16[2048,128]{1,0:T(8,128)(2,1)} %get-tuple-element.78), channel_id=1, source_target_pairs={{0,2},{2,4},{4,6},{6,0},{1,3},{3,5},{5,7},{7,1},{8,10},{10,12},{12... | collective-permute-start | bytes 1572872 | tf_op jit(solution)/shard_map/ppermute | solution.py:192
  60.5 13.1 %collective-permute-start.8 = (bf16[2048,128]{1,0:T(8,128)(2,1)}, bf16[2048,128]{1,0:T(8,128)(2,1)S(1)}, u32[]{:S(2)}, u32[]{:S(2)}) collective-permute-start(bf16[2048,128]{1,0:T(8,128)(2,1)} %get-tuple-element.77), channel_id=1, source_target_pairs={{0,24},{8,0},{16,8},{24,16},{1,25},{9,1},{17,9},{25,17},{2,26},{10... | collective-permute-start | bytes 1572872 | tf_op jit(solution)/shard_map/ppermute | solution.py:192
  61.1 14.0 %collective-permute-start.6 = (bf16[2048,128]{1,0:T(8,128)(2,1)}, bf16[2048,128]{1,0:T(8,128)(2,1)S(1)}, u32[]{:S(2)}, u32[]{:S(2)}) collective-permute-start(bf16[2048,128]{1,0:T(8,128)(2,1)} %get-tuple-element.77), channel_id=1, source_target_pairs={{0,8},{8,16},{16,24},{24,0},{1,9},{9,17},{17,25},{25,1},{2,10},{10... | collective-permute-start | bytes 1572872 | tf_op jit(solution)/shard_map/ppermute | solution.py:192
  62.0 0.8 copy-start.1
  62.8 0.9 copy-start.3
  75.3 6.0 %collective-permute-start.15 = (bf16[8192,128]{1,0:T(8,128)(2,1)S(1)}, bf16[8192,128]{1,0:T(8,128)(2,1)S(1)}, u32[]{:S(2)}, u32[]{:S(2)}) collective-permute-start(bf16[8192,128]{1,0:T(8,128)(2,1)S(1)} %get-tuple-element.102), channel_id=1, source_target_pairs={{0,32},{32,0},{1,33},{33,1},{2,34},{34,2},{3,35},{35,3},{4,36},{36... | collective-permute-start | bytes 6291464 | tf_op jit(solution)/shard_map/ppermute | solution.py:192
  77.2 9.1 %collective-permute-start.11 = (bf16[1024,128]{1,0:T(8,128)(2,1)S(1)}, bf16[1024,128]{1,0:T(8,128)(2,1)S(1)}, u32[]{:S(2)}, u32[]{:S(2)}) collective-permute-start(bf16[1024,128]{1,0:T(8,128)(2,1)S(1)} %get-tuple-element.98), channel_id=1, source_target_pairs={{0,8},{8,16},{16,24},{24,0},{1,9},{9,17},{17,25},{25,1},{2,10},{10... | collective-permute-start | bytes 786440 | tf_op jit(solution)/shard_map/ppermute | solution.py:192
  77.2 9.1 %collective-permute-start.12 = (bf16[1024,128]{1,0:T(8,128)(2,1)S(1)}, bf16[1024,128]{1,0:T(8,128)(2,1)S(1)}, u32[]{:S(2)}, u32[]{:S(2)}) collective-permute-start(bf16[1024,128]{1,0:T(8,128)(2,1)S(1)} %get-tuple-element.99), channel_id=1, source_target_pairs={{0,2},{2,4},{4,6},{6,0},{1,3},{3,5},{5,7},{7,1},{8,10},{10,12},{12... | collective-permute-start | bytes 786440 | tf_op jit(solution)/shard_map/ppermute | solution.py:192
  77.2 9.1 %collective-permute-start.13 = (bf16[1024,128]{1,0:T(8,128)(2,1)S(1)}, bf16[1024,128]{1,0:T(8,128)(2,1)S(1)}, u32[]{:S(2)}, u32[]{:S(2)}) collective-permute-start(bf16[1024,128]{1,0:T(8,128)(2,1)S(1)} %get-tuple-element.100), channel_id=1, source_target_pairs={{0,24},{8,0},{16,8},{24,16},{1,25},{9,1},{17,9},{25,17},{2,26},{10... | collective-permute-start | bytes 786440 | tf_op jit(solution)/shard_map/ppermute | solution.py:192
  79.9 8.1 %collective-permute-start.14 = (bf16[1024,128]{1,0:T(8,128)(2,1)S(1)}, bf16[1024,128]{1,0:T(8,128)(2,1)S(1)}, u32[]{:S(2)}, u32[]{:S(2)}) collective-permute-start(bf16[1024,128]{1,0:T(8,128)(2,1)S(1)} %get-tuple-element.101), channel_id=1, source_target_pairs={{0,6},{2,0},{4,2},{6,4},{1,7},{3,1},{5,3},{7,5},{8,14},{10,8},{12,... | collective-permute-start | bytes 786440 | tf_op jit(solution)/shard_map/ppermute | solution.py:192
  88.0 3.0 %collective-permute-start.16 = (bf16[1024,128]{1,0:T(8,128)(2,1)S(1)}, bf16[1024,128]{1,0:T(8,128)(2,1)S(1)}, u32[]{:S(2)}, u32[]{:S(2)}) collective-permute-start(bf16[1024,128]{1,0:T(8,128)(2,1)S(1)} %collective-permute-done.11.refs_0_), channel_id=1, source_target_pairs={{0,32},{32,0},{1,33},{33,1},{2,34},{34,2},{3,35},{35,3},{4,36},{36... | collective-permute-start | bytes 786440 | tf_op jit(solution)/shard_map/ppermute | solution.py:192
  89.8 1.5 %collective-permute-start.17 = (bf16[1024,128]{1,0:T(8,128)(2,1)S(1)}, bf16[1024,128]{1,0:T(8,128)(2,1)S(1)}, u32[]{:S(2)}, u32[]{:S(2)}) collective-permute-start(bf16[1024,128]{1,0:T(8,128)(2,1)S(1)} %collective-permute-done.12.refs_1_), channel_id=1, source_target_pairs={{0,32},{32,0},{1,33},{33,1},{2,34},{34,2},{3,35},{35,3},{4,36},{36... | collective-permute-start | bytes 786440 | tf_op jit(solution)/shard_map/ppermute | solution.py:192
  89.8 1.9 %collective-permute-start.18 = (bf16[1024,128]{1,0:T(8,128)(2,1)S(1)}, bf16[1024,128]{1,0:T(8,128)(2,1)S(1)}, u32[]{:S(2)}, u32[]{:S(2)}) collective-permute-start(bf16[1024,128]{1,0:T(8,128)(2,1)S(1)} %collective-permute-done.13.refs_2_), channel_id=1, source_target_pairs={{0,32},{32,0},{1,33},{33,1},{2,34},{34,2},{3,35},{35,3},{4,36},{36... | collective-permute-start | bytes 786440 | tf_op jit(solution)/shard_map/ppermute | solution.py:192
  90.3 1.8 %collective-permute-start.19 = (bf16[1024,128]{1,0:T(8,128)(2,1)S(1)}, bf16[1024,128]{1,0:T(8,128)(2,1)S(1)}, u32[]{:S(2)}, u32[]{:S(2)}) collective-permute-start(bf16[1024,128]{1,0:T(8,128)(2,1)S(1)} %collective-permute-done.14.refs_3_), channel_id=1, source_target_pairs={{0,32},{32,0},{1,33},{33,1},{2,34},{34,2},{3,35},{35,3},{4,36},{36... | collective-permute-start | bytes 786440 | tf_op jit(solution)/shard_map/ppermute | solution.py:192

commit v4 on v3

--- a/solution.py
+++ b/solution.py
@@ -79,10 +79,12 @@
         send[peer, 128:176, :] = b_half
 
 
-def state_kernel(
-    total, factor_a, factor_b, moment_a, second_a, moment_b, second_b,
-    new_a, new_b, new_ma, new_va, new_mb, new_vb,
-):
+def state_kernel(total, *refs):
+    there, (new_a, new_b, new_ma, new_va, new_mb, new_vb) = refs[:6], refs[6:12]
+    here, sems = refs[12:18], refs[18]
+    for copy in fetched(there, here, sems):
+        copy.wait()
+    factor_a, factor_b, moment_a, second_a, moment_b, second_b = here
     grad_a, grad_b = apart(total)
     new_a[...], new_ma[...], new_va[...] = adam_update(
         factor_a[...], grad_a, moment_a[...], second_a[...]
@@ -140,37 +142,55 @@
 
 
 def merge_kernel(place, blocks, base, *refs, distances, pick):
-    n = len(distances)
-    out, held, write = refs[-3:]
+    out, held_0, held_1, write = refs[-4:]
     x, y, core = place[0], place[1], place[2]
 
-    def unit(d, h, inner):
-        ky, kx = (distances[d], inner) if h == 0 else (inner, distances[d])
-        column = lax.rem(y + 4 - ky, 4) * 1024 + lax.rem(x + 4 - kx, 4) * 256
-        return pl.ds(pl.multiple_of(column, 256), 256), (d * 2 + h) * 4 + inner
-
-    def copy_out(d, h, inner):
-        where, u = unit(d, h, inner)
-        return pltpu.make_async_copy(held.at[u], out.at[:, :, h, :, where], write.at[u])
-
-    units = [(d, h, inner) for d in range(n) for h in range(2) for inner in range(4)]
-    for d, h, inner in units:
-        where, u = unit(d, h, inner)
-        for side in range(2):
-            ref, row = pick(refs, side, d, h, inner)
-            piece = ref[row : row + 512].reshape(4, 2, 64, 128)
-            wide = jnp.concatenate([piece[:, zh].reshape(256, 128) for zh in range(2)], axis=-1)
-            delta = jnp.dot(blocks[side, h], wide, preferred_element_type=jnp.float32)
-            owner = core if side == 0 else 1 - core
-            old = base[:, owner, h, :, where].astype(jnp.float32)
-            held[u, :, owner] = (old + 0.125 * delta.reshape(4, 48, 256)).astype(HALF)
-        copy_out(d, h, inner).start()
-    for t in units:
-        copy_out(*t).wait()
+    def column(kx, ky):
+        return (x ^ kx) * 256, (y ^ ky) * 1024
+
+    def copy_0(d):
+        rows = column(0, distances[d])[1]
+        return pltpu.make_async_copy(
+            held_0.at[d], out.at[:, :, 0, :, pl.ds(pl.multiple_of(rows, 1024), 1024)], write.at[5 * d]
+        )
+
+    def copy_1(d, inner):
+        where = pl.multiple_of(sum(column(distances[d], inner)), 256)
+        return pltpu.make_async_copy(
+            held_1.at[d, inner], out.at[:, :, 1, :, pl.ds(where, 256)], write.at[5 * d + 1 + inner]
+        )
+
+    copies = []
+    for d, distance in enumerate(distances):
+        for h in range(2):
+            for inner in range(4):
+                kx, ky = (inner, distance) if h == 0 else (distance, inner)
+                near, far = column(kx, ky)
+                where = pl.ds(pl.multiple_of(near + far, 256), 256)
+                for side in range(2):
+                    ref, row = pick(refs, side, d, h, inner)
+                    piece = ref[row : row + 512].reshape(4, 2, 64, 128)
+                    wide = jnp.concatenate([piece[:, zh].reshape(256, 128) for zh in range(2)], axis=-1)
+                    delta = jnp.dot(blocks[side, h], wide, preferred_element_type=jnp.float32)
+                    owner = core if side == 0 else 1 - core
+                    old = base[:, owner, h, :, where].astype(jnp.float32)
+                    new = (old + 0.125 * delta.reshape(4, 48, 256)).astype(HALF)
+                    if h == 0:
+                        held_0[d, :, owner, :, pl.ds(pl.multiple_of(near, 256), 256)] = new
+                    else:
+                        held_1[d, inner, :, owner] = new
+                if h == 1:
+                    copies.append(copy_1(d, inner))
+                    copies[-1].start()
+            if h == 0:
+                copies.append(copy_0(d))
+                copies[-1].start()
+    for copy in copies:
+        copy.wait()
 
 
 def next_merge_kernel(place, blocks, base, *refs, **how):
-    merge_kernel(place, blocks, base, *refs[:-4], *refs[-3:], **how)
+    merge_kernel(place, blocks, base, *refs[:-5], *refs[-4:], **how)
 
 
 def pick_first(refs, side, d, h, inner):
@@ -189,7 +209,7 @@
 
 def hop(value, axis, k):
     n = lax.axis_size(axis)
-    return lax.ppermute(value, axis, [(i, (i + k) % n) for i in range(n)])
+    return lax.ppermute(value, axis, [(i, i ^ k) for i in range(n)])
 
 
 def swap(value, axis, mask):
@@ -266,11 +286,12 @@
     states = pl.pallas_call(
         state_kernel,
         out_shape=(sa, sb, sa, sa, sb, sb),
-        in_specs=[VMEM] * 7,
+        in_specs=[VMEM] + [HBM] * 6,
         out_specs=[VMEM] * 6,
+        scratch_shapes=[pltpu.VMEM(v.shape, f32) for v in needed[2:]] + [pltpu.SemaphoreType.DMA((6,))],
         compiler_params=limit(4),
         cost_estimate=cost(1024),
-    )(inside(total), *state)
+    )(inside(total), *[pltpu.with_memory_space_constraint(v, pltpu.HBM) for v in needed[2:]])
 
     place = jnp.stack([x, y, core])
 
@@ -284,8 +305,9 @@
             out_specs=HBM,
             input_output_aliases={3 + len(pieces): 0} if before else {},
             scratch_shapes=[
-                pltpu.VMEM((8 * n, 4, 2, 48, 256), HALF),
-                pltpu.SemaphoreType.DMA((8 * n,)),
+                pltpu.VMEM((n, 4, 2, 48, 1024), HALF),
+                pltpu.VMEM((n, 4, 4, 2, 48, 256), HALF),
+                pltpu.SemaphoreType.DMA((5 * n,)),
             ],
             compiler_params=limit(2 + 2 * n),
             cost_estimate=cost(1024),
@@ -301,7 +323,7 @@
         out_specs=(VMEM,) * 5,
         compiler_params=limit(8),
     )(*near)
-    far = [hop(relayed[2 * s + h], second[h], 1 + 2 * s) for s in range(2) for h in range(2)]
+    far = [hop(relayed[2 * s + h], second[h], 3 - 2 * s) for s in range(2) for h in range(2)]
     near_other = hop(everything, "core", 1)
     merged = merge((1, 3), pick_near, [*near, near_other], merged)
     far, merged = lax.optimization_barrier((far, merged))

time: 95.6 us -> 91.6 us (0.958)
  the two profiles are of different devices: /device:TPU:39 before, /device:TPU:33 now
where the time goes in v4:
time: 91.6 us; the launch traced here: 91.3 us
  waiting for transfers between devices  28.4 us (31%)
  starting transfers between devices  27.6 us (30%)
  Pallas kernels  18.6 us (20%)
  blocking collectives  15.8 us (17%)
    ppermute x20, starting transfers between devices, hop(): return lax.ppermute(value, axis, [(i, i ^ k) for i in range(n)])  20.6 us
    all_to_all x1, blocking collectives, per_device(): got = lax.all_to_all(packed, ('zl', 'core'), 0, 0, tiled=True)  15.8 us
    ppermute x20, waiting for transfers between devices, hop(): return lax.ppermute(value, axis, [(i, i ^ k) for i in range(n)])  15.6 us
    all_to_all x1, waiting for transfers between devices, per_device(): line = lax.all_to_all(send, ('zl', 'zh'), 0, 0, tiled=True)  12.8 us
    pallas_call x3, Pallas kernels, merge(): pl.pallas_call(functools.partial(next_merge_kernel if before else merge_k...  9.73 us
    all_to_all x1, starting transfers between devices, per_device(): line = lax.all_to_all(send, ('zl', 'zh'), 0, 0, tiled=True)  6.93 us
    pallas_call x1, Pallas kernels, per_device(): pl.pallas_call(stash_kernel, out_shape=pltpu.VMEM((4, 2, 2, 48, 4096), HA...  2.87 us
  transfers between devices with their start and end apart: 21, of which 16 were waited for; matrix products, arithmetic and copies ran while one was open for 0% of the time, Pallas kernels for 13%

profile of v4, /device:TPU:33, one launch (start us, length us, event | category | flops | bytes accessed | tf_op | source)
XLA Modules:
  0.0 91.3 jit_solution(1586719675016943038)
XLA Ops:
  0.6 1.4 %shard_map.144 = (bf16[8,176,128]{2,1,0:T(8,128)(2,1)S(1)}, f32[2,64,128]{2,1,0:T(8,128)S(1)}, f32[2,48,64]{2,1,0:T(8,128)S(1)}, f32[2,64,128]{2,1,0:T(8,128)S(1...) custom-call(f32[1,16,64,128]{3,2,1,0:T(8,128)} %refs_0_.2, ...), custom_call_target="tpu_custom_call" | custom-call | tf_op jit(solution)/shard_map/pallas_call | solution.py:227
  2.0 15.8 %all_to_all.10.got = bf16[8,176,128]{2,1,0:T(8,128)(2,1)S(1)} all-to-all(bf16[8,176,128]{2,1,0:T(8,128)(2,1)S(1)} %get-tuple-element.58), channel_id=1, replica_groups=mesh['zl'=4,'core'=2,'y'=4,'x'=4,'zh'=2] {'zl','core'}, dimensions={0} | all-to-all | bytes 720896 | tf_op jit(solution)/shard_map/all_to_all | solution.py:235
  17.8 0.9 %shard_map.145 = (bf16[8,176,128]{2,1,0:T(8,128)(2,1)}, f32[176,128]{1,0:T(8,128)S(1)}) custom-call(bf16[8,176,128]{2,1,0:T(8,128)(2,1)S(1)} %all_to_all.10.got, f32[2,64,128]{2,1,0:T(8,128)S(1)} %get-tuple-element.59.factor_a, f32[2,48,64]{2,1,0:T(8,128)S(1)} %get-tuple-element.60.factor_b, f32[2,64,128]{2,1,0:T(8,128)S(1)} %get-tuple-element.61.moment_a, ...), custom_call_target="tpu_custom_call" | custom-call | tf_op jit(solution)/shard_map/pallas_call | solution.py:237
  18.7 6.9 %all-to-all-start.1 = ((bf16[8,176,128]{2,1,0:T(8,128)(2,1)}), bf16[8,176,128]{2,1,0:T(8,128)(2,1)S(1)}, u32[]{:S(2)}, u32[]{:S(2)}) async-start(bf16[8,176,128]{2,1,0:T(8,128)(2,1)} %get-tuple-element.65), calls=%async_computation.1 | async-start | bytes 720896 | tf_op jit(solution)/shard_map/all_to_all | solution.py:244
  25.7 12.8 %all-to-all-done.1.line = bf16[8,176,128]{2,1,0:T(8,128)(2,1)S(1)} async-done(((bf16[8,176,128]{2,1,0:T(8,128)(2,1)}), bf16[8,176,128]{2,1,0:T(8,128)(2,1)S(1)}, u32[]{:S(2)}, u32[]{:S(2)}) %all-to-all-start.1) | async-done | bytes 360480 | tf_op jit(solution)/shard_map/all_to_all | solution.py:244
  38.5 2.6 %collective-permute-start.2 = (bf16[512,128]{1,0:T(8,128)(2,1)S(1)}, bf16[512,128]{1,0:T(8,128)(2,1)S(1)}, u32[]{:S(2)}, u32[]{:S(2)}) collective-permute-start(bf16[512,128]{1,0:T(8,128)(2,1)S(1)} %get-tuple-element.68.refs_0_), channel_id=1, source_target_pairs={{0,6},{2,4},{4,2},{6,0},{1,7},{3,5},{5,3},{7,1},{8,14},{10,12},{12... | collective-permute-start | bytes 393224 | tf_op jit(solution)/shard_map/ppermute | solution.py:212
  41.0 0.5 collective-permute-start.1
  41.5 0.3 collective-permute-start
  41.8 2.7 %collective-permute-start.5 = (bf16[512,128]{1,0:T(8,128)(2,1)S(1)}, bf16[512,128]{1,0:T(8,128)(2,1)S(1)}, u32[]{:S(2)}, u32[]{:S(2)}) collective-permute-start(bf16[512,128]{1,0:T(8,128)(2,1)S(1)} %get-tuple-element.72.refs_4_), channel_id=1, source_target_pairs={{0,24},{8,16},{16,8},{24,0},{1,25},{9,17},{17,9},{25,1},{2,26},{10... | collective-permute-start | bytes 393224 | tf_op jit(solution)/shard_map/ppermute | solution.py:212
  44.5 0.3 collective-permute-start.4
  44.9 1.4 %collective-permute-done.2.refs_3_ = bf16[512,128]{1,0:T(8,128)(2,1)S(1)} collective-permute-done((bf16[512,128]{1,0:T(8,128)(2,1)S(1)}, bf16[512,128]{1,0:T(8,128)(2,1)S(1)}, u32[]{:S(2)}, u32[]{:S(2)}) %collective-permute-start.2) | collective-permute-done | bytes 131104 | tf_op jit(solution)/shard_map/ppermute | solution.py:212
  46.3 1.3 %collective-permute-start.3 = (bf16[512,128]{1,0:T(8,128)(2,1)S(1)}, bf16[512,128]{1,0:T(8,128)(2,1)S(1)}, u32[]{:S(2)}, u32[]{:S(2)}) collective-permute-start(bf16[512,128]{1,0:T(8,128)(2,1)S(1)} %get-tuple-element.72.refs_4_), channel_id=1, source_target_pairs={{0,8},{8,0},{16,24},{24,16},{1,9},{9,1},{17,25},{25,17},{2,10},{10... | collective-permute-start | bytes 393224 | tf_op jit(solution)/shard_map/ppermute | solution.py:212
  47.6 0.0 collective-permute-done.1.refs_2_
  47.6 0.0 collective-permute-done.refs_1_
  47.6 2.1 %collective-permute-done.5.refs_7_ = bf16[512,128]{1,0:T(8,128)(2,1)S(1)} collective-permute-done((bf16[512,128]{1,0:T(8,128)(2,1)S(1)}, bf16[512,128]{1,0:T(8,128)(2,1)S(1)}, u32[]{:S(2)}, u32[]{:S(2)}) %collective-permute-start.5) | collective-permute-done | bytes 131104 | tf_op jit(solution)/shard_map/ppermute | solution.py:212
  49.7 0.3 collective-permute-done.4.refs_6_
  50.0 1.8 %collective-permute-done.3.refs_5_ = bf16[512,128]{1,0:T(8,128)(2,1)S(1)} collective-permute-done((bf16[512,128]{1,0:T(8,128)(2,1)S(1)}, bf16[512,128]{1,0:T(8,128)(2,1)S(1)}, u32[]{:S(2)}, u32[]{:S(2)}) %collective-permute-start.3) | collective-permute-done | bytes 131104 | tf_op jit(solution)/shard_map/ppermute | solution.py:212
  51.8 1.6 %shard_map.147 = (bf16[2048,128]{1,0:T(8,128)(2,1)}, bf16[2048,128]{1,0:T(8,128)(2,1)}, bf16[4288,128]{1,0:T(8,128)(2,1)}) custom-call(bf16[512,128]{1,0:T(8,128)(2,1)S(1)} %get-tuple-element.68.refs_0_, bf16[512,128]{1,0:T(8,128)(2,1)S(1)} %collective-permute-done.refs_1_, bf16[512,128]{1,0:T(8,128)(2,1)S(1)} %collective-permute-done.1.refs_2_, ...), custom_call_target="tpu_custom_call" | custom-call | tf_op jit(solution)/shard_map/pallas_call | solution.py:259
  53.4 2.0 %collective-permute-start.10 = (bf16[4288,128]{1,0:T(8,128)(2,1)}, bf16[4288,128]{1,0:T(8,128)(2,1)S(1)}, u32[]{:S(2)}, u32[]{:S(2)}) collective-permute-start(bf16[4288,128]{1,0:T(8,128)(2,1)} %get-tuple-element.79.refs_0_), channel_id=1, source_target_pairs={{0,32},{32,0},{1,33},{33,1},{2,34},{34,2},{3,35},{35,3},{4,36},{36... | collective-permute-start | bytes 3293192 | tf_op jit(solution)/shard_map/ppermute | solution.py:212
  55.4 2.2 %collective-permute-start.9 = (bf16[2048,128]{1,0:T(8,128)(2,1)}, bf16[2048,128]{1,0:T(8,128)(2,1)S(1)}, u32[]{:S(2)}, u32[]{:S(2)}) collective-permute-start(bf16[2048,128]{1,0:T(8,128)(2,1)} %get-tuple-element.78), channel_id=1, source_target_pairs={{0,6},{2,4},{4,2},{6,0},{1,7},{3,5},{5,3},{7,1},{8,14},{10,12},{12... | collective-permute-start | bytes 1572872 | tf_op jit(solution)/shard_map/ppermute | solution.py:212
  57.5 0.0 collective-permute-start.7
  57.5 2.7 %collective-permute-start.8 = (bf16[2048,128]{1,0:T(8,128)(2,1)}, bf16[2048,128]{1,0:T(8,128)(2,1)S(1)}, u32[]{:S(2)}, u32[]{:S(2)}) collective-permute-start(bf16[2048,128]{1,0:T(8,128)(2,1)} %get-tuple-element.77), channel_id=1, source_target_pairs={{0,24},{8,16},{16,8},{24,0},{1,25},{9,17},{17,9},{25,1},{2,26},{10... | collective-permute-start | bytes 1572872 | tf_op jit(solution)/shard_map/ppermute | solution.py:212
  60.3 0.0 collective-permute-start.6
  60.3 0.1 pad_add_fusion.place
  60.4 1.8 %shard_map.151 = (f32[2,64,128]{2,1,0:T(8,128)}, f32[2,48,64]{2,1,0:T(8,128)}, f32[2,64,128]{2,1,0:T(8,128)}, f32[2,64,128]{2,1,0:T(8,128)}, f32[2,48,64]{2,1,0:T(8,128)}, /*index=5*/f32[2,48,64]{2,1,0:T(8,128)}) custom-call(f32[176,128]{1,0:T(8,128)S(1)} %get-tuple-element.81.total, f32[2,64,128]{2,1,0:T(8,128)} %refs_0_.3, f32[2,48,64]{2,1,0:T(8,128)} %refs_1_.3, ...), custom_call_target="tpu_custom_call" | custom-call | bytes 1024 | tf_op jit(solution)/shard_map/pallas_call | solution.py:286
  62.1 2.9 %shard_map.149.base = bf16[4,2,2,48,4096]{4,3,2,1,0:T(8,128)(2,1)S(1)} custom-call(bf16[4,2,2,48,4096]{4,3,2,1,0:T(8,128)(2,1)} %bitcast.7), custom_call_target="tpu_custom_call" | custom-call | bytes 1024 | tf_op jit(solution)/shard_map/pallas_call | solution.py:270
  65.0 0.0 collective-permute-done.10.other.refs_1_
  65.0 0.1 shard_map.148.blocks
  65.1 3.3 %shard_map.150.refs_5_ = bf16[4,2,2,48,4096]{4,3,2,1,0:T(8,128)(2,1)} custom-call(s32[3]{0:T(128)S(1)} %pad_add_fusion.place, bf16[2,2,192,256]{3,2,1,0:T(8,128)(2,1)S(1)} %shard_map.148.blocks, bf16[4,2,2,48,4096]{4,3,2,1,0:T(8,128)(2,1)S(1)} %shard_map.149.base, bf16[4288,128]{1,0:T(8,128)(2,1)} %get-tuple-element.79.refs_0_, ...), custom_call_target="tpu_custom_call" | custom-call | bytes 1024 | tf_op jit(solution)/shard_map/pallas_call | solution.py:301
  68.4 1.9 %collective-permute-done.9.down_1.refs_3_ = bf16[2048,128]{1,0:T(8,128)(2,1)S(1)} collective-permute-done((bf16[2048,128]{1,0:T(8,128)(2,1)}, bf16[2048,128]{1,0:T(8,128)(2,1)S(1)}, u32[]{:S(2)}, u32[]{:S(2)}) %collective-permute-start.9) | collective-permute-done | bytes 524320 | tf_op jit(solution)/shard_map/ppermute | solution.py:212
  70.4 0.6 collective-permute-done.7.up_1.refs_1_
  71.0 1.1 %collective-permute-done.8.down_0.refs_2_ = bf16[2048,128]{1,0:T(8,128)(2,1)S(1)} collective-permute-done((bf16[2048,128]{1,0:T(8,128)(2,1)}, bf16[2048,128]{1,0:T(8,128)(2,1)S(1)}, u32[]{:S(2)}, u32[]{:S(2)}) %collective-permute-start.8) | collective-permute-done | bytes 524320 | tf_op jit(solution)/shard_map/ppermute | solution.py:212
  72.1 1.3 %collective-permute-done.6.up_0.refs_0_ = bf16[2048,128]{1,0:T(8,128)(2,1)S(1)} collective-permute-done((bf16[2048,128]{1,0:T(8,128)(2,1)}, bf16[2048,128]{1,0:T(8,128)(2,1)S(1)}, u32[]{:S(2)}, u32[]{:S(2)}) %collective-permute-start.6) | collective-permute-done | bytes 524320 | tf_op jit(solution)/shard_map/ppermute | solution.py:212
  73.4 0.2 shard_map.152
  73.6 1.5 %collective-permute-start.15 = (bf16[8192,128]{1,0:T(8,128)(2,1)S(1)}, bf16[8192,128]{1,0:T(8,128)(2,1)S(1)}, u32[]{:S(2)}, u32[]{:S(2)}) collective-permute-start(bf16[8192,128]{1,0:T(8,128)(2,1)S(1)} %get-tuple-element.102), channel_id=1, source_target_pairs={{0,32},{32,0},{1,33},{33,1},{2,34},{34,2},{3,35},{35,3},{4,36},{36... | collective-permute-start | bytes 6291464 | tf_op jit(solution)/shard_map/ppermute | solution.py:212
  75.1 1.2 %collective-permute-start.11 = (bf16[1024,128]{1,0:T(8,128)(2,1)S(1)}, bf16[1024,128]{1,0:T(8,128)(2,1)S(1)}, u32[]{:S(2)}, u32[]{:S(2)}) collective-permute-start(bf16[1024,128]{1,0:T(8,128)(2,1)S(1)} %get-tuple-element.98), channel_id=1, source_target_pairs={{0,24},{8,16},{16,8},{24,0},{1,25},{9,17},{17,9},{25,1},{2,26},{10... | collective-permute-start | bytes 786440 | tf_op jit(solution)/shard_map/ppermute | solution.py:212
  76.4 0.0 collective-permute-start.12
  76.4 0.0 collective-permute-start.13
  76.4 1.5 %collective-permute-start.14 = (bf16[1024,128]{1,0:T(8,128)(2,1)S(1)}, bf16[1024,128]{1,0:T(8,128)(2,1)S(1)}, u32[]{:S(2)}, u32[]{:S(2)}) collective-permute-start(bf16[1024,128]{1,0:T(8,128)(2,1)S(1)} %get-tuple-element.101), channel_id=1, source_target_pairs={{0,2},{2,0},{4,6},{6,4},{1,3},{3,1},{5,7},{7,5},{8,10},{10,8},{12,... | collective-permute-start | bytes 786440 | tf_op jit(solution)/shard_map/ppermute | solution.py:212
  77.8 1.1 %collective-permute-done.15.refs_4_ = bf16[8192,128]{1,0:T(8,128)(2,1)S(1)} collective-permute-done((bf16[8192,128]{1,0:T(8,128)(2,1)S(1)}, bf16[8192,128]{1,0:T(8,128)(2,1)S(1)}, u32[]{:S(2)}, u32[]{:S(2)}) %collective-permute-start.15) | collective-permute-done | bytes 2097184 | tf_op jit(solution)/shard_map/ppermute | solution.py:212
  78.9 3.9 %shard_map.153.refs_8_ = bf16[4,2,2,48,4096]{4,3,2,1,0:T(8,128)(2,1)} custom-call(s32[3]{0:T(128)S(1)} %pad_add_fusion.place, bf16[2,2,192,256]{3,2,1,0:T(8,128)(2,1)S(1)} %shard_map.148.blocks, bf16[4,2,2,48,4096]{4,3,2,1,0:T(8,128)(2,1)S(1)} %shard_map.149.base, ...), custom_call_target="tpu_custom_call", output_to_operand_aliasing={{}: (8, {})} | custom-call | bytes 1024 | tf_op jit(solution)/shard_map/pallas_call | solution.py:301
  82.8 1.4 %collective-permute-done.11.refs_0_ = bf16[1024,128]{1,0:T(8,128)(2,1)S(1)} collective-permute-done((bf16[1024,128]{1,0:T(8,128)(2,1)S(1)}, bf16[1024,128]{1,0:T(8,128)(2,1)S(1)}, u32[]{:S(2)}, u32[]{:S(2)}) %collective-permute-start.11) | collective-permute-done | bytes 262176 | tf_op jit(solution)/shard_map/ppermute | solution.py:212
  84.2 0.9 collective-permute-done.12.refs_1_
  85.1 0.0 collective-permute-done.13.refs_2_
  85.1 0.0 collective-permute-done.14.refs_3_
  85.1 1.2 %collective-permute-start.16 = (bf16[1024,128]{1,0:T(8,128)(2,1)S(1)}, bf16[1024,128]{1,0:T(8,128)(2,1)S(1)}, u32[]{:S(2)}, u32[]{:S(2)}) collective-permute-start(bf16[1024,128]{1,0:T(8,128)(2,1)S(1)} %collective-permute-done.11.refs_0_), channel_id=1, source_target_pairs={{0,32},{32,0},{1,33},{33,1},{2,34},{34,2},{3,35},{35,3},{4,36},{36... | collective-permute-start | bytes 786440 | tf_op jit(solution)/shard_map/ppermute | solution.py:212
  86.3 0.1 collective-permute-start.17
  86.4 0.4 collective-permute-start.18
  86.8 0.1 collective-permute-start.19
  86.9 0.6 collective-permute-done.16.refs_4_
  87.5 0.4 collective-permute-done.17.refs_5_
  87.8 0.4 collective-permute-done.18.refs_6_
  88.2 0.4 collective-permute-done.19.refs_7_
  88.6 2.5 %shard_map.154 = bf16[4,2,2,48,4096]{4,3,2,1,0:T(8,128)(2,1)} custom-call(s32[3]{0:T(128)S(1)} %pad_add_fusion.place, bf16[2,2,192,256]{3,2,1,0:T(8,128)(2,1)S(1)} %shard_map.148.blocks, bf16[4,2,2,48,4096]{4,3,2,1,0:T(8,128)(2,1)S(1)} %shard_map.149.base, bf16[1024,128]{1,0:T(8,128)(2,1)S(1)} %collective-permute-done.11.refs_0_, ...), custom_call_target="tpu_custom_call", output_to_operand_aliasing={{}: (11, {})} | custom-call | bytes 1024 | tf_op jit(solution)/shard_map/pallas_call | solution.py:301
  (1 shorter events, 0.0 us)
Async XLA Ops:
  18.7 19.7 %all-to-all-start.1 = ((bf16[8,176,128]{2,1,0:T(8,128)(2,1)}), bf16[8,176,128]{2,1,0:T(8,128)(2,1)S(1)}, u32[]{:S(2)}, u32[]{:S(2)}) async-start(bf16[8,176,128]{2,1,0:T(8,128)(2,1)} %get-tuple-element.65), calls=%async_computation.1 | async-start | bytes 720896 | tf_op jit(solution)/shard_map/all_to_all | solution.py:244
  38.5 7.9 %collective-permute-start.2 = (bf16[512,128]{1,0:T(8,128)(2,1)S(1)}, bf16[512,128]{1,0:T(8,128)(2,1)S(1)}, u32[]{:S(2)}, u32[]{:S(2)}) collective-permute-start(bf16[512,128]{1,0:T(8,128)(2,1)S(1)} %get-tuple-element.68.refs_0_), channel_id=1, source_target_pairs={{0,6},{2,4},{4,2},{6,0},{1,7},{3,5},{5,3},{7,1},{8,14},{10,12},{12... | collective-permute-start | bytes 393224 | tf_op jit(solution)/shard_map/ppermute | solution.py:212
  41.0 6.6 %collective-permute-start.1 = (bf16[512,128]{1,0:T(8,128)(2,1)S(1)}, bf16[512,128]{1,0:T(8,128)(2,1)S(1)}, u32[]{:S(2)}, u32[]{:S(2)}) collective-permute-start(bf16[512,128]{1,0:T(8,128)(2,1)S(1)} %get-tuple-element.68.refs_0_), channel_id=1, source_target_pairs={{0,4},{2,6},{4,0},{6,2},{1,5},{3,7},{5,1},{7,3},{8,12},{10,14},{12... | collective-permute-start | bytes 393224 | tf_op jit(solution)/shard_map/ppermute | solution.py:212
  41.5 6.1 %collective-permute-start = (bf16[512,128]{1,0:T(8,128)(2,1)S(1)}, bf16[512,128]{1,0:T(8,128)(2,1)S(1)}, u32[]{:S(2)}, u32[]{:S(2)}) collective-permute-start(bf16[512,128]{1,0:T(8,128)(2,1)S(1)} %get-tuple-element.68.refs_0_), channel_id=1, source_target_pairs={{0,2},{2,0},{4,6},{6,4},{1,3},{3,1},{5,7},{7,5},{8,10},{10,8},{12,... | collective-permute-start | bytes 393224 | tf_op jit(solution)/shard_map/ppermute | solution.py:212
  41.8 7.9 %collective-permute-start.5 = (bf16[512,128]{1,0:T(8,128)(2,1)S(1)}, bf16[512,128]{1,0:T(8,128)(2,1)S(1)}, u32[]{:S(2)}, u32[]{:S(2)}) collective-permute-start(bf16[512,128]{1,0:T(8,128)(2,1)S(1)} %get-tuple-element.72.refs_4_), channel_id=1, source_target_pairs={{0,24},{8,16},{16,8},{24,0},{1,25},{9,17},{17,9},{25,1},{2,26},{10... | collective-permute-start | bytes 393224 | tf_op jit(solution)/shard_map/ppermute | solution.py:212
  44.5 5.4 %collective-permute-start.4 = (bf16[512,128]{1,0:T(8,128)(2,1)S(1)}, bf16[512,128]{1,0:T(8,128)(2,1)S(1)}, u32[]{:S(2)}, u32[]{:S(2)}) collective-permute-start(bf16[512,128]{1,0:T(8,128)(2,1)S(1)} %get-tuple-element.72.refs_4_), channel_id=1, source_target_pairs={{0,16},{8,24},{16,0},{24,8},{1,17},{9,25},{17,1},{25,9},{2,18},{10... | collective-permute-start | bytes 393224 | tf_op jit(solution)/shard_map/ppermute | solution.py:212
  46.3 5.4 %collective-permute-start.3 = (bf16[512,128]{1,0:T(8,128)(2,1)S(1)}, bf16[512,128]{1,0:T(8,128)(2,1)S(1)}, u32[]{:S(2)}, u32[]{:S(2)}) collective-permute-start(bf16[512,128]{1,0:T(8,128)(2,1)S(1)} %get-tuple-element.72.refs_4_), channel_id=1, source_target_pairs={{0,8},{8,0},{16,24},{24,16},{1,9},{9,1},{17,25},{25,17},{2,10},{10... | collective-permute-start | bytes 393224 | tf_op jit(solution)/shard_map/ppermute | solution.py:212
  53.4 11.6 %collective-permute-start.10 = (bf16[4288,128]{1,0:T(8,128)(2,1)}, bf16[4288,128]{1,0:T(8,128)(2,1)S(1)}, u32[]{:S(2)}, u32[]{:S(2)}) collective-permute-start(bf16[4288,128]{1,0:T(8,128)(2,1)} %get-tuple-element.79.refs_0_), channel_id=1, source_target_pairs={{0,32},{32,0},{1,33},{33,1},{2,34},{34,2},{3,35},{35,3},{4,36},{36... | collective-permute-start | bytes 3293192 | tf_op jit(solution)/shard_map/ppermute | solution.py:212
  55.4 15.0 %collective-permute-start.9 = (bf16[2048,128]{1,0:T(8,128)(2,1)}, bf16[2048,128]{1,0:T(8,128)(2,1)S(1)}, u32[]{:S(2)}, u32[]{:S(2)}) collective-permute-start(bf16[2048,128]{1,0:T(8,128)(2,1)} %get-tuple-element.78), channel_id=1, source_target_pairs={{0,6},{2,4},{4,2},{6,0},{1,7},{3,5},{5,3},{7,1},{8,14},{10,12},{12... | collective-permute-start | bytes 1572872 | tf_op jit(solution)/shard_map/ppermute | solution.py:212
  57.5 13.4 %collective-permute-start.7 = (bf16[2048,128]{1,0:T(8,128)(2,1)}, bf16[2048,128]{1,0:T(8,128)(2,1)S(1)}, u32[]{:S(2)}, u32[]{:S(2)}) collective-permute-start(bf16[2048,128]{1,0:T(8,128)(2,1)} %get-tuple-element.78), channel_id=1, source_target_pairs={{0,2},{2,0},{4,6},{6,4},{1,3},{3,1},{5,7},{7,5},{8,10},{10,8},{12,... | collective-permute-start | bytes 1572872 | tf_op jit(solution)/shard_map/ppermute | solution.py:212
  57.5 14.6 %collective-permute-start.8 = (bf16[2048,128]{1,0:T(8,128)(2,1)}, bf16[2048,128]{1,0:T(8,128)(2,1)S(1)}, u32[]{:S(2)}, u32[]{:S(2)}) collective-permute-start(bf16[2048,128]{1,0:T(8,128)(2,1)} %get-tuple-element.77), channel_id=1, source_target_pairs={{0,24},{8,16},{16,8},{24,0},{1,25},{9,17},{17,9},{25,1},{2,26},{10... | collective-permute-start | bytes 1572872 | tf_op jit(solution)/shard_map/ppermute | solution.py:212
  60.3 13.1 %collective-permute-start.6 = (bf16[2048,128]{1,0:T(8,128)(2,1)}, bf16[2048,128]{1,0:T(8,128)(2,1)S(1)}, u32[]{:S(2)}, u32[]{:S(2)}) collective-permute-start(bf16[2048,128]{1,0:T(8,128)(2,1)} %get-tuple-element.77), channel_id=1, source_target_pairs={{0,8},{8,0},{16,24},{24,16},{1,9},{9,1},{17,25},{25,17},{2,10},{10... | collective-permute-start | bytes 1572872 | tf_op jit(solution)/shard_map/ppermute | solution.py:212
  73.6 5.3 %collective-permute-start.15 = (bf16[8192,128]{1,0:T(8,128)(2,1)S(1)}, bf16[8192,128]{1,0:T(8,128)(2,1)S(1)}, u32[]{:S(2)}, u32[]{:S(2)}) collective-permute-start(bf16[8192,128]{1,0:T(8,128)(2,1)S(1)} %get-tuple-element.102), channel_id=1, source_target_pairs={{0,32},{32,0},{1,33},{33,1},{2,34},{34,2},{3,35},{35,3},{4,36},{36... | collective-permute-start | bytes 6291464 | tf_op jit(solution)/shard_map/ppermute | solution.py:212
  75.1 9.1 %collective-permute-start.11 = (bf16[1024,128]{1,0:T(8,128)(2,1)S(1)}, bf16[1024,128]{1,0:T(8,128)(2,1)S(1)}, u32[]{:S(2)}, u32[]{:S(2)}) collective-permute-start(bf16[1024,128]{1,0:T(8,128)(2,1)S(1)} %get-tuple-element.98), channel_id=1, source_target_pairs={{0,24},{8,16},{16,8},{24,0},{1,25},{9,17},{17,9},{25,1},{2,26},{10... | collective-permute-start | bytes 786440 | tf_op jit(solution)/shard_map/ppermute | solution.py:212
  76.4 8.7 %collective-permute-start.12 = (bf16[1024,128]{1,0:T(8,128)(2,1)S(1)}, bf16[1024,128]{1,0:T(8,128)(2,1)S(1)}, u32[]{:S(2)}, u32[]{:S(2)}) collective-permute-start(bf16[1024,128]{1,0:T(8,128)(2,1)S(1)} %get-tuple-element.99), channel_id=1, source_target_pairs={{0,6},{2,4},{4,2},{6,0},{1,7},{3,5},{5,3},{7,1},{8,14},{10,12},{12... | collective-permute-start | bytes 786440 | tf_op jit(solution)/shard_map/ppermute | solution.py:212
  76.4 8.7 %collective-permute-start.13 = (bf16[1024,128]{1,0:T(8,128)(2,1)S(1)}, bf16[1024,128]{1,0:T(8,128)(2,1)S(1)}, u32[]{:S(2)}, u32[]{:S(2)}) collective-permute-start(bf16[1024,128]{1,0:T(8,128)(2,1)S(1)} %get-tuple-element.100), channel_id=1, source_target_pairs={{0,8},{8,0},{16,24},{24,16},{1,9},{9,1},{17,25},{25,17},{2,10},{10... | collective-permute-start | bytes 786440 | tf_op jit(solution)/shard_map/ppermute | solution.py:212
  76.4 8.7 %collective-permute-start.14 = (bf16[1024,128]{1,0:T(8,128)(2,1)S(1)}, bf16[1024,128]{1,0:T(8,128)(2,1)S(1)}, u32[]{:S(2)}, u32[]{:S(2)}) collective-permute-start(bf16[1024,128]{1,0:T(8,128)(2,1)S(1)} %get-tuple-element.101), channel_id=1, source_target_pairs={{0,2},{2,0},{4,6},{6,4},{1,3},{3,1},{5,7},{7,5},{8,10},{10,8},{12,... | collective-permute-start | bytes 786440 | tf_op jit(solution)/shard_map/ppermute | solution.py:212
  85.1 2.4 %collective-permute-start.16 = (bf16[1024,128]{1,0:T(8,128)(2,1)S(1)}, bf16[1024,128]{1,0:T(8,128)(2,1)S(1)}, u32[]{:S(2)}, u32[]{:S(2)}) collective-permute-start(bf16[1024,128]{1,0:T(8,128)(2,1)S(1)} %collective-permute-done.11.refs_0_), channel_id=1, source_target_pairs={{0,32},{32,0},{1,33},{33,1},{2,34},{34,2},{3,35},{35,3},{4,36},{36... | collective-permute-start | bytes 786440 | tf_op jit(solution)/shard_map/ppermute | solution.py:212
  86.3 1.5 %collective-permute-start.17 = (bf16[1024,128]{1,0:T(8,128)(2,1)S(1)}, bf16[1024,128]{1,0:T(8,128)(2,1)S(1)}, u32[]{:S(2)}, u32[]{:S(2)}) collective-permute-start(bf16[1024,128]{1,0:T(8,128)(2,1)S(1)} %collective-permute-done.12.refs_1_), channel_id=1, source_target_pairs={{0,32},{32,0},{1,33},{33,1},{2,34},{34,2},{3,35},{35,3},{4,36},{36... | collective-permute-start | bytes 786440 | tf_op jit(solution)/shard_map/ppermute | solution.py:212
  86.4 1.8 %collective-permute-start.18 = (bf16[1024,128]{1,0:T(8,128)(2,1)S(1)}, bf16[1024,128]{1,0:T(8,128)(2,1)S(1)}, u32[]{:S(2)}, u32[]{:S(2)}) collective-permute-start(bf16[1024,128]{1,0:T(8,128)(2,1)S(1)} %collective-permute-done.13.refs_2_), channel_id=1, source_target_pairs={{0,32},{32,0},{1,33},{33,1},{2,34},{34,2},{3,35},{35,3},{4,36},{36... | collective-permute-start | bytes 786440 | tf_op jit(solution)/shard_map/ppermute | solution.py:212
  86.8 1.8 %collective-permute-start.19 = (bf16[1024,128]{1,0:T(8,128)(2,1)S(1)}, bf16[1024,128]{1,0:T(8,128)(2,1)S(1)}, u32[]{:S(2)}, u32[]{:S(2)}) collective-permute-start(bf16[1024,128]{1,0:T(8,128)(2,1)S(1)} %collective-permute-done.14.refs_3_), channel_id=1, source_target_pairs={{0,32},{32,0},{1,33},{33,1},{2,34},{34,2},{3,35},{35,3},{4,36},{36... | collective-permute-start | bytes 786440 | tf_op jit(solution)/shard_map/ppermute | solution.py:212

commit v5 on v4

--- a/solution.py
+++ b/solution.py
@@ -42,41 +42,46 @@
     return copies
 
 
-def pack_kernel(*refs):
-    there, out, here = refs[:8], refs[8], refs[9:15]
-    grad_a, grad_b, sems = refs[15:]
+def pack_kernel(place, *refs):
+    there, (keep, give), here = refs[:8], refs[8:10], refs[10:16]
+    grad_a, grad_b, sems = refs[16:]
     copies = fetched(there, (grad_a, grad_b, *here), sems)
     copies[0].wait()
     copies[1].wait()
-    out[:, 0:128, :] = grad_a[0].reshape(8, 128, 128).astype(HALF)
-    for owner in range(8):
-        pair = jnp.concatenate([grad_b[0, 2 * owner], grad_b[0, 2 * owner + 1]], axis=-1)
-        out[owner, 128:176, :] = pair.astype(HALF)
+    core = place[0]
+    for out, owner_core in ((keep, core), (give, 1 - core)):
+        for zl in range(4):
+            expert = 4 * zl + 2 * owner_core
+            out[zl, 0:128] = grad_a[0, pl.ds(expert, 2)].reshape(128, 128).astype(out.dtype)
+            both = jnp.concatenate([grad_b[0, expert], grad_b[0, expert + 1]], axis=-1)
+            out[zl, 128:176] = both.astype(out.dtype)
     for copy in copies[2:]:
         copy.wait()
 
 
-def summed(got):
-    total = got[0].astype(jnp.float32)
-    for learner in range(1, 8):
-        total = total + got[learner].astype(jnp.float32)
-    return total
+def pair_sum_kernel(place, keep, given, own, out_1, out_2, out_3):
+    zl = place[1]
+    own[...] = keep[zl] + given[zl].astype(jnp.float32)
+    for a, out in ((1, out_1), (2, out_2), (3, out_3)):
+        out[...] = (keep[zl ^ a] + given[zl ^ a].astype(jnp.float32)).astype(HALF)
 
 
 def apart(total):
     return total[0:128].reshape(2, 64, 128), [total[128:176, 64 * e : 64 * e + 64] for e in range(2)]
 
 
-def send_kernel(got, factor_a, factor_b, moment_a, second_a, moment_b, second_b, send, total):
-    total[...] = summed(got)
+def send_kernel(
+    own, got_1, got_2, got_3, factor_a, factor_b, moment_a, second_a, moment_b, second_b, send, send_a, total
+):
+    total[...] = own[...] + (got_1[...].astype(jnp.float32) + (got_2[...].astype(jnp.float32) + got_3[...].astype(jnp.float32)))
     grad_a, grad_b = apart(total)
     a = adam_update(factor_a[...], grad_a, moment_a[...], second_a[...])[0]
     b = [adam_update(factor_b[e], grad_b[e], moment_b[e], second_b[e])[0] for e in range(2)]
     a_half = a.astype(HALF).reshape(128, 128)
     b_half = jnp.concatenate(b, axis=-1).astype(HALF)
-    for peer in range(8):
-        send[peer, 0:128, :] = a_half
-        send[peer, 128:176, :] = b_half
+    send[0:128] = a_half
+    send[128:176] = b_half
+    send_a[...] = a_half
 
 
 def state_kernel(total, *refs):
@@ -95,12 +100,21 @@
         )
 
 
-def split_kernel(place, line, half_0, half_1, rows):
-    half_0[...] = line[:, 0:64].reshape(512, 128)
-    half_1[...] = line[:, 64:128].reshape(512, 128)
-    zh = place[0]
-    for zl in range(4):
-        rows[zl] = line[2 * zl + zh, 128:176]
+def pair_kernel(send, across, pair):
+    pair[0:128] = send[0:128]
+    pair[128:256] = across[...]
+    pair[256:304] = send[128:176]
+
+
+def split_kernel(place, *refs):
+    half_0, half_1, rows = refs[4:]
+    zl, zh = place[0], place[1]
+    for a in range(4):
+        for b in range(2):
+            slot = (zl ^ a) * 2 + (zh ^ b)
+            half_0[slot] = refs[a][128 * b : 128 * b + 64]
+            half_1[slot] = refs[a][128 * b + 64 : 128 * b + 128]
+        rows[zl ^ a] = refs[a][256:304]
 
 
 def join_kernel(*refs):
@@ -224,33 +238,52 @@
     shape = jax.ShapeDtypeStruct
     sa, sb = shape((2, 64, 128), f32), shape((2, 48, 64), f32)
     needed = (grad_a, grad_b, factor_a, factor_b, moment_a, second_a, moment_b, second_b)
-    packed, *state = pl.pallas_call(
+    x, y, core, zl, zh = (lax.axis_index(a).astype(jnp.int32) for a in ("x", "y", "core", "zl", "zh"))
+    where = jnp.stack([core, zl])
+    keep, give, *state = pl.pallas_call(
         pack_kernel,
-        out_shape=[pltpu.VMEM((8, 176, 128), HALF)] + [pltpu.VMEM(v.shape, f32) for v in needed[2:]],
-        in_specs=[HBM] * 8,
-        out_specs=[VMEM] * 7,
+        out_shape=[pltpu.VMEM((4, 176, 128), f32), pltpu.VMEM((4, 176, 128), HALF)]
+        + [pltpu.VMEM(v.shape, f32) for v in needed[2:]],
+        in_specs=[SMEM] + [HBM] * 8,
+        out_specs=[VMEM] * 8,
         scratch_shapes=[pltpu.VMEM(v.shape, f32) for v in needed[:2]] + [pltpu.SemaphoreType.DMA((8,))],
         compiler_params=limit(4),
-    )(*[pltpu.with_memory_space_constraint(v, pltpu.HBM) for v in needed])
-    got = lax.all_to_all(packed, ("zl", "core"), 0, 0, tiled=True)
+    )(where, *[pltpu.with_memory_space_constraint(v, pltpu.HBM) for v in needed])
+    own, *parts = pl.pallas_call(
+        pair_sum_kernel,
+        out_shape=[pltpu.VMEM((176, 128), f32)] + [pltpu.VMEM((176, 128), HALF)] * 3,
+        in_specs=[SMEM] + [VMEM] * 2,
+        out_specs=[VMEM] * 4,
+        compiler_params=limit(4),
+    )(where, inside(keep), inside(hop(give, "core", 1)))
+    parts = [hop(v, "zl", a) for a, v in enumerate(parts, 1)]
+    parts = lax.optimization_barrier(parts)
     state = [inside(v) for v in state]
-    send, total = pl.pallas_call(
+    send, send_a, total = pl.pallas_call(
         send_kernel,
-        out_shape=(pltpu.VMEM((8, 176, 128), HALF), pltpu.VMEM((176, 128), f32)),
-        in_specs=[VMEM] * 7,
-        out_specs=(VMEM,) * 2,
-        compiler_params=limit(4),
-    )(inside(got), *state)
-    line = lax.all_to_all(send, ("zl", "zh"), 0, 0, tiled=True)
-
-    x, y, core, zh = (lax.axis_index(a).astype(jnp.int32) for a in ("x", "y", "core", "zh"))
+        out_shape=(pltpu.VMEM((176, 128), HALF), pltpu.VMEM((128, 128), HALF), pltpu.VMEM((176, 128), f32)),
+        in_specs=[VMEM] * 10,
+        out_specs=(VMEM,) * 3,
+        compiler_params=limit(4),
+    )(inside(own), *[inside(v) for v in parts], *state)
+    pair = pl.pallas_call(
+        pair_kernel,
+        out_shape=pltpu.VMEM((304, 128), HALF),
+        in_specs=[VMEM] * 2,
+        out_specs=VMEM,
+        compiler_params=limit(2),
+    )(inside(send), inside(hop(send_a, "zh", 1)))
+    line = [pair] + [hop(pair, "zl", a) for a in (1, 2, 3)]
+    line = lax.optimization_barrier(line)
+
     half_0, half_1, rows_own = pl.pallas_call(
         split_kernel,
-        out_shape=(pltpu.VMEM((512, 128), HALF), pltpu.VMEM((512, 128), HALF), pltpu.VMEM((4, 48, 128), HALF)),
-        in_specs=[SMEM, VMEM],
+        out_shape=(pltpu.VMEM((8, 64, 128), HALF),) * 2 + (pltpu.VMEM((4, 48, 128), HALF),),
+        in_specs=[SMEM] + [VMEM] * 4,
         out_specs=(VMEM,) * 3,
         compiler_params=limit(4),
-    )(zh.reshape(1), inside(line))
+    )(jnp.stack([zl, zh]), *[inside(v) for v in line])
+    half_0, half_1 = half_0.reshape(512, 128), half_1.reshape(512, 128)
     halves = half_0, half_1
 
     first, second = ("x", "y"), ("y", "x")

time: 91.6 us -> 84.4 us (0.921)
  the two profiles are of different devices: /device:TPU:33 before, /device:TPU:1 now
where the time goes in v5:
time: 84.4 us; the launch traced here: 84.2 us
  starting transfers between devices  39.1 us (46%)
  waiting for transfers between devices  24.5 us (29%)
  Pallas kernels  19.5 us (23%)
  between operations  0.9 us (1%)
    ppermute x28, starting transfers between devices, hop(): return lax.ppermute(value, axis, [(i, i ^ k) for i in range(n)])  39.1 us
    ppermute x28, waiting for transfers between devices, hop(): return lax.ppermute(value, axis, [(i, i ^ k) for i in range(n)])  24.5 us
    pallas_call x3, Pallas kernels, merge(): pl.pallas_call(functools.partial(next_merge_kernel if before else merge_k...  9.72 us
    pallas_call x1, Pallas kernels, per_device(): pl.pallas_call(stash_kernel, out_shape=pltpu.VMEM((4, 2, 2, 48, 4096), HA...  2.87 us
    pallas_call x1, Pallas kernels, per_device(): pl.pallas_call(pack_kernel, out_shape=[pltpu.VMEM((4, 176, 128), f32), pl...  1.9 us
    pallas_call x1, Pallas kernels, per_device(): pl.pallas_call(state_kernel, out_shape=(sa, sb, sa, sa, sb, sb), in_specs...  1.77 us
  transfers between devices with their start and end apart: 28, of which 20 were waited for; matrix products, arithmetic and copies ran while one was open for 0% of the time, Pallas kernels for 14%

profile of v5, /device:TPU:1, one launch (start us, length us, event | category | flops | bytes accessed | tf_op | source)
XLA Modules:
  0.0 84.2 jit_solution(11170108119978839889)
XLA Ops:
  0.6 0.1 pad_add_fusion
  0.7 1.9 %shard_map.144 = (f32[4,176,128]{2,1,0:T(8,128)S(1)}, bf16[4,176,128]{2,1,0:T(8,128)(2,1)S(1)}, f32[2,64,128]{2,1,0:T(8,128)S(1)}, f32[2,48,64]{2,1,0:T(8,128)S(...) custom-call(s32[2]{0:T(128)S(1)} %get-tuple-element.136.place, ...), custom_call_target="tpu_custom_call" | custom-call | tf_op jit(solution)/shard_map/pallas_call | solution.py:243
  2.6 3.3 %collective-permute-start = (bf16[4,176,128]{2,1,0:T(8,128)(2,1)S(1)}, bf16[4,176,128]{2,1,0:T(8,128)(2,1)S(1)}, u32[]{:S(2)}, u32[]{:S(2)}) collective-permute-start(bf16[4,176,128]{2,1,0:T(8,128)(2,1)S(1)} %get-tuple-element.72), channel_id=1, source_target_pairs={{0,32},{32,0},{1,33},{33,1},{2,34},{34,2},{3,35},{35,3},{4,36},{36... | collective-permute-start | bytes 540680 | tf_op jit(solution)/shard_map/ppermute | solution.py:226
  6.0 1.0 %collective-permute-done.given = bf16[4,176,128]{2,1,0:T(8,128)(2,1)S(1)} collective-permute-done((bf16[4,176,128]{2,1,0:T(8,128)(2,1)S(1)}, bf16[4,176,128]{2,1,0:T(8,128)(2,1)S(1)}, u32[]{:S(2)}, u32[]{:S(2)}) %collective-permute-start) | collective-permute-done | bytes 180256 | tf_op jit(solution)/shard_map/ppermute | solution.py:226
  7.0 0.6 shard_map.145
  7.6 0.1 collective-permute-start.1
  7.7 2.9 %collective-permute-start.2 = (bf16[176,128]{1,0:T(8,128)(2,1)S(1)}, bf16[176,128]{1,0:T(8,128)(2,1)S(1)}, u32[]{:S(2)}, u32[]{:S(2)}) collective-permute-start(bf16[176,128]{1,0:T(8,128)(2,1)S(1)} %get-tuple-element.75), channel_id=1, source_target_pairs={{0,128},{64,192},{128,0},{192,64},{1,129},{65,193},{129,1},{193,65... | collective-permute-start | bytes 135176 | tf_op jit(solution)/shard_map/ppermute | solution.py:226
  10.6 0.7 collective-permute-start.3
  11.2 0.0 collective-permute-done.1.got_1
  11.2 0.8 collective-permute-done.2.got_2
  12.0 3.3 %collective-permute-done.3.got_3 = bf16[176,128]{1,0:T(8,128)(2,1)S(1)} collective-permute-done((bf16[176,128]{1,0:T(8,128)(2,1)S(1)}, bf16[176,128]{1,0:T(8,128)(2,1)S(1)}, u32[]{:S(2)}, u32[]{:S(2)}) %collective-permute-start.3) | collective-permute-done | bytes 45088 | tf_op jit(solution)/shard_map/ppermute | solution.py:226
  15.3 0.2 shard_map.146
  15.5 4.3 %collective-permute-start.4 = (bf16[128,128]{1,0:T(8,128)(2,1)S(1)}, bf16[128,128]{1,0:T(8,128)(2,1)S(1)}, u32[]{:S(2)}, u32[]{:S(2)}) collective-permute-start(bf16[128,128]{1,0:T(8,128)(2,1)S(1)} %get-tuple-element.87), channel_id=1, source_target_pairs={{0,1},{1,0},{2,3},{3,2},{4,5},{5,4},{6,7},{7,6},{8,9},{9,8},{10,11... | collective-permute-start | bytes 98312 | tf_op jit(solution)/shard_map/ppermute | solution.py:226
  19.8 2.4 %collective-permute-done.4.across = bf16[128,128]{1,0:T(8,128)(2,1)S(1)} collective-permute-done((bf16[128,128]{1,0:T(8,128)(2,1)S(1)}, bf16[128,128]{1,0:T(8,128)(2,1)S(1)}, u32[]{:S(2)}, u32[]{:S(2)}) %collective-permute-start.4) | collective-permute-done | bytes 32800 | tf_op jit(solution)/shard_map/ppermute | solution.py:226
  22.2 0.8 collective-permute-start.7
  23.0 0.1 collective-permute-start.6
  23.1 2.6 %collective-permute-start.5 = (bf16[304,128]{1,0:T(8,128)(2,1)S(1)}, bf16[304,128]{1,0:T(8,128)(2,1)S(1)}, u32[]{:S(2)}, u32[]{:S(2)}) collective-permute-start(bf16[304,128]{1,0:T(8,128)(2,1)S(1)} %shard_map.147.refs_0_), channel_id=1, source_target_pairs={{0,64},{64,0},{128,192},{192,128},{1,65},{65,1},{129,193},{193,129... | collective-permute-start | bytes 233480 | tf_op jit(solution)/shard_map/ppermute | solution.py:226
  25.8 1.7 %collective-permute-done.7.refs_3_ = bf16[304,128]{1,0:T(8,128)(2,1)S(1)} collective-permute-done((bf16[304,128]{1,0:T(8,128)(2,1)S(1)}, bf16[304,128]{1,0:T(8,128)(2,1)S(1)}, u32[]{:S(2)}, u32[]{:S(2)}) %collective-permute-start.7) | collective-permute-done | bytes 77856 | tf_op jit(solution)/shard_map/ppermute | solution.py:226
  27.4 2.0 %collective-permute-done.6.refs_2_ = bf16[304,128]{1,0:T(8,128)(2,1)S(1)} collective-permute-done((bf16[304,128]{1,0:T(8,128)(2,1)S(1)}, bf16[304,128]{1,0:T(8,128)(2,1)S(1)}, u32[]{:S(2)}, u32[]{:S(2)}) %collective-permute-start.6) | collective-permute-done | bytes 77856 | tf_op jit(solution)/shard_map/ppermute | solution.py:226
  29.4 0.0 collective-permute-done.5.refs_1_
  29.4 0.6 shard_map.148
  30.0 2.5 %collective-permute-start.13 = (bf16[512,128]{1,0:T(8,128)(2,1)S(1)}, bf16[512,128]{1,0:T(8,128)(2,1)S(1)}, u32[]{:S(2)}, u32[]{:S(2)}) collective-permute-start(bf16[512,128]{1,0:T(8,128)(2,1)S(1)} %bitcast.13), channel_id=1, source_target_pairs={{0,24},{8,16},{16,8},{24,0},{1,25},{9,17},{17,9},{25,1},{2,26},{10... | collective-permute-start | bytes 393224 | tf_op jit(solution)/shard_map/ppermute | solution.py:226
  32.5 0.3 collective-permute-start.12
  32.8 0.5 collective-permute-start.11
  33.3 2.3 %collective-permute-start.10 = (bf16[512,128]{1,0:T(8,128)(2,1)S(1)}, bf16[512,128]{1,0:T(8,128)(2,1)S(1)}, u32[]{:S(2)}, u32[]{:S(2)}) collective-permute-start(bf16[512,128]{1,0:T(8,128)(2,1)S(1)} %bitcast.9), channel_id=1, source_target_pairs={{0,6},{2,4},{4,2},{6,0},{1,7},{3,5},{5,3},{7,1},{8,14},{10,12},{12... | collective-permute-start | bytes 393224 | tf_op jit(solution)/shard_map/ppermute | solution.py:226
  35.6 0.5 collective-permute-start.9
  36.2 0.0 collective-permute-done.13.refs_7_
  36.2 0.8 %collective-permute-start.8 = (bf16[512,128]{1,0:T(8,128)(2,1)S(1)}, bf16[512,128]{1,0:T(8,128)(2,1)S(1)}, u32[]{:S(2)}, u32[]{:S(2)}) collective-permute-start(bf16[512,128]{1,0:T(8,128)(2,1)S(1)} %bitcast.11), channel_id=1, source_target_pairs={{0,2},{2,0},{4,6},{6,4},{1,3},{3,1},{5,7},{7,5},{8,10},{10,8},{12,... | collective-permute-start | bytes 393224 | tf_op jit(solution)/shard_map/ppermute | solution.py:226
  37.0 0.8 collective-permute-done.12.refs_6_
  37.8 0.0 collective-permute-done.11.refs_5_
  37.8 1.1 %collective-permute-done.10.refs_3_ = bf16[512,128]{1,0:T(8,128)(2,1)S(1)} collective-permute-done((bf16[512,128]{1,0:T(8,128)(2,1)S(1)}, bf16[512,128]{1,0:T(8,128)(2,1)S(1)}, u32[]{:S(2)}, u32[]{:S(2)}) %collective-permute-start.10) | collective-permute-done | bytes 131104 | tf_op jit(solution)/shard_map/ppermute | solution.py:226
  39.0 2.0 %collective-permute-done.9.refs_2_ = bf16[512,128]{1,0:T(8,128)(2,1)S(1)} collective-permute-done((bf16[512,128]{1,0:T(8,128)(2,1)S(1)}, bf16[512,128]{1,0:T(8,128)(2,1)S(1)}, u32[]{:S(2)}, u32[]{:S(2)}) %collective-permute-start.9) | collective-permute-done | bytes 131104 | tf_op jit(solution)/shard_map/ppermute | solution.py:226
  41.0 1.6 %shard_map.149 = (bf16[2048,128]{1,0:T(8,128)(2,1)}, bf16[2048,128]{1,0:T(8,128)(2,1)}, bf16[4288,128]{1,0:T(8,128)(2,1)}) custom-call(bf16[512,128]{1,0:T(8,128)(2,1)S(1)} %bitcast.12, bf16[512,128]{1,0:T(8,128)(2,1)S(1)} %collective-permute-done.8.refs_1_, bf16[512,128]{1,0:T(8,128)(2,1)S(1)} %collective-permute-done.9.refs_2_, ...), custom_call_target="tpu_custom_call" | custom-call | tf_op jit(solution)/shard_map/pallas_call | solution.py:292
  42.6 6.1 %collective-permute-start.18 = (bf16[4288,128]{1,0:T(8,128)(2,1)}, bf16[4288,128]{1,0:T(8,128)(2,1)S(1)}, u32[]{:S(2)}, u32[]{:S(2)}) collective-permute-start(bf16[4288,128]{1,0:T(8,128)(2,1)} %get-tuple-element.105.refs_0_), channel_id=1, source_target_pairs={{0,32},{32,0},{1,33},{33,1},{2,34},{34,2},{3,35},{35,3},{4,36},{36... | collective-permute-start | bytes 3293192 | tf_op jit(solution)/shard_map/ppermute | solution.py:226
  48.7 1.7 %collective-permute-start.17 = (bf16[2048,128]{1,0:T(8,128)(2,1)}, bf16[2048,128]{1,0:T(8,128)(2,1)S(1)}, u32[]{:S(2)}, u32[]{:S(2)}) collective-permute-start(bf16[2048,128]{1,0:T(8,128)(2,1)} %get-tuple-element.104), channel_id=1, source_target_pairs={{0,6},{2,4},{4,2},{6,0},{1,7},{3,5},{5,3},{7,1},{8,14},{10,12},{12... | collective-permute-start | bytes 1572872 | tf_op jit(solution)/shard_map/ppermute | solution.py:226
  50.4 2.8 %collective-permute-start.16 = (bf16[2048,128]{1,0:T(8,128)(2,1)}, bf16[2048,128]{1,0:T(8,128)(2,1)S(1)}, u32[]{:S(2)}, u32[]{:S(2)}) collective-permute-start(bf16[2048,128]{1,0:T(8,128)(2,1)} %get-tuple-element.103), channel_id=1, source_target_pairs={{0,24},{8,16},{16,8},{24,0},{1,25},{9,17},{17,9},{25,1},{2,26},{10... | collective-permute-start | bytes 1572872 | tf_op jit(solution)/shard_map/ppermute | solution.py:226
  53.2 0.0 collective-permute-start.14
  53.2 0.1 pad_add_fusion.2.place
  53.2 1.8 %shard_map.153 = (f32[2,64,128]{2,1,0:T(8,128)}, f32[2,48,64]{2,1,0:T(8,128)}, f32[2,64,128]{2,1,0:T(8,128)}, f32[2,64,128]{2,1,0:T(8,128)}, f32[2,48,64]{2,1,0:T(8,128)}, /*index=5*/f32[2,48,64]{2,1,0:T(8,128)}) custom-call(f32[176,128]{1,0:T(8,128)S(1)} %get-tuple-element.107.total, f32[2,64,128]{2,1,0:T(8,128)} %refs_0_.3, f32[2,48,64]{2,1,0:T(8,128)} %refs_1_.3, ...), custom_call_target="tpu_custom_call" | custom-call | bytes 1024 | tf_op jit(solution)/shard_map/pallas_call | solution.py:319
  55.0 2.9 %shard_map.151.base = bf16[4,2,2,48,4096]{4,3,2,1,0:T(8,128)(2,1)S(1)} custom-call(bf16[4,2,2,48,4096]{4,3,2,1,0:T(8,128)(2,1)} %bitcast.18), custom_call_target="tpu_custom_call" | custom-call | bytes 1024 | tf_op jit(solution)/shard_map/pallas_call | solution.py:303
  57.9 0.1 shard_map.150.blocks
  58.0 3.3 %shard_map.152.refs_5_ = bf16[4,2,2,48,4096]{4,3,2,1,0:T(8,128)(2,1)} custom-call(s32[3]{0:T(128)S(1)} %pad_add_fusion.2.place, bf16[2,2,192,256]{3,2,1,0:T(8,128)(2,1)S(1)} %shard_map.150.blocks, bf16[4,2,2,48,4096]{4,3,2,1,0:T(8,128)(2,1)S(1)} %shard_map.151.base, bf16[4288,128]{1,0:T(8,128)(2,1)} %get-tuple-element.105.refs_0_, ...), custom_call_target="tpu_custom_call" | custom-call | bytes 1024 | tf_op jit(solution)/shard_map/pallas_call | solution.py:334
  61.3 2.4 %collective-permute-done.17.down_1.refs_3_ = bf16[2048,128]{1,0:T(8,128)(2,1)S(1)} collective-permute-done((bf16[2048,128]{1,0:T(8,128)(2,1)}, bf16[2048,128]{1,0:T(8,128)(2,1)S(1)}, u32[]{:S(2)}, u32[]{:S(2)}) %collective-permute-start.17) | collective-permute-done | bytes 524320 | tf_op jit(solution)/shard_map/ppermute | solution.py:226
  63.7 0.2 collective-permute-done.15.up_1.refs_1_
  63.9 1.1 %collective-permute-done.16.down_0.refs_2_ = bf16[2048,128]{1,0:T(8,128)(2,1)S(1)} collective-permute-done((bf16[2048,128]{1,0:T(8,128)(2,1)}, bf16[2048,128]{1,0:T(8,128)(2,1)S(1)}, u32[]{:S(2)}, u32[]{:S(2)}) %collective-permute-start.16) | collective-permute-done | bytes 524320 | tf_op jit(solution)/shard_map/ppermute | solution.py:226
  65.0 1.1 %collective-permute-done.14.up_0.refs_0_ = bf16[2048,128]{1,0:T(8,128)(2,1)S(1)} collective-permute-done((bf16[2048,128]{1,0:T(8,128)(2,1)}, bf16[2048,128]{1,0:T(8,128)(2,1)S(1)}, u32[]{:S(2)}, u32[]{:S(2)}) %collective-permute-start.14) | collective-permute-done | bytes 524320 | tf_op jit(solution)/shard_map/ppermute | solution.py:226
  66.0 0.2 shard_map.154
  66.2 1.8 %collective-permute-start.23 = (bf16[8192,128]{1,0:T(8,128)(2,1)S(1)}, bf16[8192,128]{1,0:T(8,128)(2,1)S(1)}, u32[]{:S(2)}, u32[]{:S(2)}) collective-permute-start(bf16[8192,128]{1,0:T(8,128)(2,1)S(1)} %get-tuple-element.128), channel_id=1, source_target_pairs={{0,32},{32,0},{1,33},{33,1},{2,34},{34,2},{3,35},{35,3},{4,36},{36... | collective-permute-start | bytes 6291464 | tf_op jit(solution)/shard_map/ppermute | solution.py:226
  68.0 1.2 %collective-permute-start.19 = (bf16[1024,128]{1,0:T(8,128)(2,1)S(1)}, bf16[1024,128]{1,0:T(8,128)(2,1)S(1)}, u32[]{:S(2)}, u32[]{:S(2)}) collective-permute-start(bf16[1024,128]{1,0:T(8,128)(2,1)S(1)} %get-tuple-element.124), channel_id=1, source_target_pairs={{0,24},{8,16},{16,8},{24,0},{1,25},{9,17},{17,9},{25,1},{2,26},{10... | collective-permute-start | bytes 786440 | tf_op jit(solution)/shard_map/ppermute | solution.py:226
  69.2 1.0 %collective-permute-start.20 = (bf16[1024,128]{1,0:T(8,128)(2,1)S(1)}, bf16[1024,128]{1,0:T(8,128)(2,1)S(1)}, u32[]{:S(2)}, u32[]{:S(2)}) collective-permute-start(bf16[1024,128]{1,0:T(8,128)(2,1)S(1)} %get-tuple-element.125), channel_id=1, source_target_pairs={{0,6},{2,4},{4,2},{6,0},{1,7},{3,5},{5,3},{7,1},{8,14},{10,12},{12... | collective-permute-start | bytes 786440 | tf_op jit(solution)/shard_map/ppermute | solution.py:226
  70.2 0.9 %collective-permute-start.22 = (bf16[1024,128]{1,0:T(8,128)(2,1)S(1)}, bf16[1024,128]{1,0:T(8,128)(2,1)S(1)}, u32[]{:S(2)}, u32[]{:S(2)}) collective-permute-start(bf16[1024,128]{1,0:T(8,128)(2,1)S(1)} %get-tuple-element.127), channel_id=1, source_target_pairs={{0,2},{2,0},{4,6},{6,4},{1,3},{3,1},{5,7},{7,5},{8,10},{10,8},{12,... | collective-permute-start | bytes 786440 | tf_op jit(solution)/shard_map/ppermute | solution.py:226
  71.1 0.7 collective-permute-done.23.refs_4_
  71.8 3.9 %shard_map.155.refs_8_ = bf16[4,2,2,48,4096]{4,3,2,1,0:T(8,128)(2,1)} custom-call(s32[3]{0:T(128)S(1)} %pad_add_fusion.2.place, bf16[2,2,192,256]{3,2,1,0:T(8,128)(2,1)S(1)} %shard_map.150.blocks, bf16[4,2,2,48,4096]{4,3,2,1,0:T(8,128)(2,1)S(1)} %shard_map.151.base, ...), custom_call_target="tpu_custom_call", output_to_operand_aliasing={{}: (8, {})} | custom-call | bytes 1024 | tf_op jit(solution)/shard_map/pallas_call | solution.py:334
  75.7 1.4 %collective-permute-done.19.refs_0_ = bf16[1024,128]{1,0:T(8,128)(2,1)S(1)} collective-permute-done((bf16[1024,128]{1,0:T(8,128)(2,1)S(1)}, bf16[1024,128]{1,0:T(8,128)(2,1)S(1)}, u32[]{:S(2)}, u32[]{:S(2)}) %collective-permute-start.19) | collective-permute-done | bytes 262176 | tf_op jit(solution)/shard_map/ppermute | solution.py:226
  77.1 0.9 %collective-permute-done.20.refs_1_ = bf16[1024,128]{1,0:T(8,128)(2,1)S(1)} collective-permute-done((bf16[1024,128]{1,0:T(8,128)(2,1)S(1)}, bf16[1024,128]{1,0:T(8,128)(2,1)S(1)}, u32[]{:S(2)}, u32[]{:S(2)}) %collective-permute-start.20) | collective-permute-done | bytes 262176 | tf_op jit(solution)/shard_map/ppermute | solution.py:226
  78.0 1.2 %collective-permute-start.24 = (bf16[1024,128]{1,0:T(8,128)(2,1)S(1)}, bf16[1024,128]{1,0:T(8,128)(2,1)S(1)}, u32[]{:S(2)}, u32[]{:S(2)}) collective-permute-start(bf16[1024,128]{1,0:T(8,128)(2,1)S(1)} %collective-permute-done.19.refs_0_), channel_id=1, source_target_pairs={{0,32},{32,0},{1,33},{33,1},{2,34},{34,2},{3,35},{35,3},{4,36},{36... | collective-permute-start | bytes 786440 | tf_op jit(solution)/shard_map/ppermute | solution.py:226
  79.2 0.1 collective-permute-start.25
  79.3 0.4 collective-permute-start.26
  79.7 0.1 collective-permute-start.27
  79.8 0.6 collective-permute-done.24.refs_4_
  80.3 0.4 collective-permute-done.25.refs_5_
  80.7 0.4 collective-permute-done.26.refs_6_
  81.1 0.4 collective-permute-done.27.refs_7_
  81.5 2.5 %shard_map.156 = bf16[4,2,2,48,4096]{4,3,2,1,0:T(8,128)(2,1)} custom-call(s32[3]{0:T(128)S(1)} %pad_add_fusion.2.place, bf16[2,2,192,256]{3,2,1,0:T(8,128)(2,1)S(1)} %shard_map.150.blocks, bf16[4,2,2,48,4096]{4,3,2,1,0:T(8,128)(2,1)S(1)} %shard_map.151.base, bf16[1024,128]{1,0:T(8,128)(2,1)S(1)} %collective-permute-done.19.refs_0_, ...), custom_call_target="tpu_custom_call", output_to_operand_aliasing={{}: (11, {})} | custom-call | bytes 1024 | tf_op jit(solution)/shard_map/pallas_call | solution.py:334
  (7 shorter events, 0.0 us)
Async XLA Ops:
  2.6 4.4 %collective-permute-start = (bf16[4,176,128]{2,1,0:T(8,128)(2,1)S(1)}, bf16[4,176,128]{2,1,0:T(8,128)(2,1)S(1)}, u32[]{:S(2)}, u32[]{:S(2)}) collective-permute-start(bf16[4,176,128]{2,1,0:T(8,128)(2,1)S(1)} %get-tuple-element.72), channel_id=1, source_target_pairs={{0,32},{32,0},{1,33},{33,1},{2,34},{34,2},{3,35},{35,3},{4,36},{36... | collective-permute-start | bytes 540680 | tf_op jit(solution)/shard_map/ppermute | solution.py:226
  7.6 3.6 %collective-permute-start.1 = (bf16[176,128]{1,0:T(8,128)(2,1)S(1)}, bf16[176,128]{1,0:T(8,128)(2,1)S(1)}, u32[]{:S(2)}, u32[]{:S(2)}) collective-permute-start(bf16[176,128]{1,0:T(8,128)(2,1)S(1)} %get-tuple-element.74), channel_id=1, source_target_pairs={{0,64},{64,0},{128,192},{192,128},{1,65},{65,1},{129,193},{193,129... | collective-permute-start | bytes 135176 | tf_op jit(solution)/shard_map/ppermute | solution.py:226
  7.7 4.3 %collective-permute-start.2 = (bf16[176,128]{1,0:T(8,128)(2,1)S(1)}, bf16[176,128]{1,0:T(8,128)(2,1)S(1)}, u32[]{:S(2)}, u32[]{:S(2)}) collective-permute-start(bf16[176,128]{1,0:T(8,128)(2,1)S(1)} %get-tuple-element.75), channel_id=1, source_target_pairs={{0,128},{64,192},{128,0},{192,64},{1,129},{65,193},{129,1},{193,65... | collective-permute-start | bytes 135176 | tf_op jit(solution)/shard_map/ppermute | solution.py:226
  10.6 4.7 %collective-permute-start.3 = (bf16[176,128]{1,0:T(8,128)(2,1)S(1)}, bf16[176,128]{1,0:T(8,128)(2,1)S(1)}, u32[]{:S(2)}, u32[]{:S(2)}) collective-permute-start(bf16[176,128]{1,0:T(8,128)(2,1)S(1)} %get-tuple-element.76), channel_id=1, source_target_pairs={{0,192},{64,128},{128,64},{192,0},{1,193},{65,129},{129,65},{193,1... | collective-permute-start | bytes 135176 | tf_op jit(solution)/shard_map/ppermute | solution.py:226
  15.5 6.7 %collective-permute-start.4 = (bf16[128,128]{1,0:T(8,128)(2,1)S(1)}, bf16[128,128]{1,0:T(8,128)(2,1)S(1)}, u32[]{:S(2)}, u32[]{:S(2)}) collective-permute-start(bf16[128,128]{1,0:T(8,128)(2,1)S(1)} %get-tuple-element.87), channel_id=1, source_target_pairs={{0,1},{1,0},{2,3},{3,2},{4,5},{5,4},{6,7},{7,6},{8,9},{9,8},{10,11... | collective-permute-start | bytes 98312 | tf_op jit(solution)/shard_map/ppermute | solution.py:226
  22.2 5.2 %collective-permute-start.7 = (bf16[304,128]{1,0:T(8,128)(2,1)S(1)}, bf16[304,128]{1,0:T(8,128)(2,1)S(1)}, u32[]{:S(2)}, u32[]{:S(2)}) collective-permute-start(bf16[304,128]{1,0:T(8,128)(2,1)S(1)} %shard_map.147.refs_0_), channel_id=1, source_target_pairs={{0,192},{64,128},{128,64},{192,0},{1,193},{65,129},{129,65},{193,1... | collective-permute-start | bytes 233480 | tf_op jit(solution)/shard_map/ppermute | solution.py:226
  23.0 6.4 %collective-permute-start.6 = (bf16[304,128]{1,0:T(8,128)(2,1)S(1)}, bf16[304,128]{1,0:T(8,128)(2,1)S(1)}, u32[]{:S(2)}, u32[]{:S(2)}) collective-permute-start(bf16[304,128]{1,0:T(8,128)(2,1)S(1)} %shard_map.147.refs_0_), channel_id=1, source_target_pairs={{0,128},{64,192},{128,0},{192,64},{1,129},{65,193},{129,1},{193,65... | collective-permute-start | bytes 233480 | tf_op jit(solution)/shard_map/ppermute | solution.py:226
  23.1 6.3 %collective-permute-start.5 = (bf16[304,128]{1,0:T(8,128)(2,1)S(1)}, bf16[304,128]{1,0:T(8,128)(2,1)S(1)}, u32[]{:S(2)}, u32[]{:S(2)}) collective-permute-start(bf16[304,128]{1,0:T(8,128)(2,1)S(1)} %shard_map.147.refs_0_), channel_id=1, source_target_pairs={{0,64},{64,0},{128,192},{192,128},{1,65},{65,1},{129,193},{193,129... | collective-permute-start | bytes 233480 | tf_op jit(solution)/shard_map/ppermute | solution.py:226
  30.0 6.2 %collective-permute-start.13 = (bf16[512,128]{1,0:T(8,128)(2,1)S(1)}, bf16[512,128]{1,0:T(8,128)(2,1)S(1)}, u32[]{:S(2)}, u32[]{:S(2)}) collective-permute-start(bf16[512,128]{1,0:T(8,128)(2,1)S(1)} %bitcast.13), channel_id=1, source_target_pairs={{0,24},{8,16},{16,8},{24,0},{1,25},{9,17},{17,9},{25,1},{2,26},{10... | collective-permute-start | bytes 393224 | tf_op jit(solution)/shard_map/ppermute | solution.py:226
  32.5 5.3 %collective-permute-start.12 = (bf16[512,128]{1,0:T(8,128)(2,1)S(1)}, bf16[512,128]{1,0:T(8,128)(2,1)S(1)}, u32[]{:S(2)}, u32[]{:S(2)}) collective-permute-start(bf16[512,128]{1,0:T(8,128)(2,1)S(1)} %bitcast.14), channel_id=1, source_target_pairs={{0,16},{8,24},{16,0},{24,8},{1,17},{9,25},{17,1},{25,9},{2,18},{10... | collective-permute-start | bytes 393224 | tf_op jit(solution)/shard_map/ppermute | solution.py:226
  32.8 5.0 %collective-permute-start.11 = (bf16[512,128]{1,0:T(8,128)(2,1)S(1)}, bf16[512,128]{1,0:T(8,128)(2,1)S(1)}, u32[]{:S(2)}, u32[]{:S(2)}) collective-permute-start(bf16[512,128]{1,0:T(8,128)(2,1)S(1)} %bitcast.15), channel_id=1, source_target_pairs={{0,8},{8,0},{16,24},{24,16},{1,9},{9,1},{17,25},{25,17},{2,10},{10... | collective-permute-start | bytes 393224 | tf_op jit(solution)/shard_map/ppermute | solution.py:226
  33.3 5.6 %collective-permute-start.10 = (bf16[512,128]{1,0:T(8,128)(2,1)S(1)}, bf16[512,128]{1,0:T(8,128)(2,1)S(1)}, u32[]{:S(2)}, u32[]{:S(2)}) collective-permute-start(bf16[512,128]{1,0:T(8,128)(2,1)S(1)} %bitcast.9), channel_id=1, source_target_pairs={{0,6},{2,4},{4,2},{6,0},{1,7},{3,5},{5,3},{7,1},{8,14},{10,12},{12... | collective-permute-start | bytes 393224 | tf_op jit(solution)/shard_map/ppermute | solution.py:226
  35.6 5.3 %collective-permute-start.9 = (bf16[512,128]{1,0:T(8,128)(2,1)S(1)}, bf16[512,128]{1,0:T(8,128)(2,1)S(1)}, u32[]{:S(2)}, u32[]{:S(2)}) collective-permute-start(bf16[512,128]{1,0:T(8,128)(2,1)S(1)} %bitcast.10), channel_id=1, source_target_pairs={{0,4},{2,6},{4,0},{6,2},{1,5},{3,7},{5,1},{7,3},{8,12},{10,14},{12... | collective-permute-start | bytes 393224 | tf_op jit(solution)/shard_map/ppermute | solution.py:226
  36.2 4.8 %collective-permute-start.8 = (bf16[512,128]{1,0:T(8,128)(2,1)S(1)}, bf16[512,128]{1,0:T(8,128)(2,1)S(1)}, u32[]{:S(2)}, u32[]{:S(2)}) collective-permute-start(bf16[512,128]{1,0:T(8,128)(2,1)S(1)} %bitcast.11), channel_id=1, source_target_pairs={{0,2},{2,0},{4,6},{6,4},{1,3},{3,1},{5,7},{7,5},{8,10},{10,8},{12,... | collective-permute-start | bytes 393224 | tf_op jit(solution)/shard_map/ppermute | solution.py:226
  42.6 15.3 %collective-permute-start.18 = (bf16[4288,128]{1,0:T(8,128)(2,1)}, bf16[4288,128]{1,0:T(8,128)(2,1)S(1)}, u32[]{:S(2)}, u32[]{:S(2)}) collective-permute-start(bf16[4288,128]{1,0:T(8,128)(2,1)} %get-tuple-element.105.refs_0_), channel_id=1, source_target_pairs={{0,32},{32,0},{1,33},{33,1},{2,34},{34,2},{3,35},{35,3},{4,36},{36... | collective-permute-start | bytes 3293192 | tf_op jit(solution)/shard_map/ppermute | solution.py:226
  48.7 15.0 %collective-permute-start.17 = (bf16[2048,128]{1,0:T(8,128)(2,1)}, bf16[2048,128]{1,0:T(8,128)(2,1)S(1)}, u32[]{:S(2)}, u32[]{:S(2)}) collective-permute-start(bf16[2048,128]{1,0:T(8,128)(2,1)} %get-tuple-element.104), channel_id=1, source_target_pairs={{0,6},{2,4},{4,2},{6,0},{1,7},{3,5},{5,3},{7,1},{8,14},{10,12},{12... | collective-permute-start | bytes 1572872 | tf_op jit(solution)/shard_map/ppermute | solution.py:226
  50.4 13.4 %collective-permute-start.15 = (bf16[2048,128]{1,0:T(8,128)(2,1)}, bf16[2048,128]{1,0:T(8,128)(2,1)S(1)}, u32[]{:S(2)}, u32[]{:S(2)}) collective-permute-start(bf16[2048,128]{1,0:T(8,128)(2,1)} %get-tuple-element.104), channel_id=1, source_target_pairs={{0,2},{2,0},{4,6},{6,4},{1,3},{3,1},{5,7},{7,5},{8,10},{10,8},{12,... | collective-permute-start | bytes 1572872 | tf_op jit(solution)/shard_map/ppermute | solution.py:226
  50.4 14.6 %collective-permute-start.16 = (bf16[2048,128]{1,0:T(8,128)(2,1)}, bf16[2048,128]{1,0:T(8,128)(2,1)S(1)}, u32[]{:S(2)}, u32[]{:S(2)}) collective-permute-start(bf16[2048,128]{1,0:T(8,128)(2,1)} %get-tuple-element.103), channel_id=1, source_target_pairs={{0,24},{8,16},{16,8},{24,0},{1,25},{9,17},{17,9},{25,1},{2,26},{10... | collective-permute-start | bytes 1572872 | tf_op jit(solution)/shard_map/ppermute | solution.py:226
  53.2 12.9 %collective-permute-start.14 = (bf16[2048,128]{1,0:T(8,128)(2,1)}, bf16[2048,128]{1,0:T(8,128)(2,1)S(1)}, u32[]{:S(2)}, u32[]{:S(2)}) collective-permute-start(bf16[2048,128]{1,0:T(8,128)(2,1)} %get-tuple-element.103), channel_id=1, source_target_pairs={{0,8},{8,0},{16,24},{24,16},{1,9},{9,1},{17,25},{25,17},{2,10},{10... | collective-permute-start | bytes 1572872 | tf_op jit(solution)/shard_map/ppermute | solution.py:226
  66.2 5.5 %collective-permute-start.23 = (bf16[8192,128]{1,0:T(8,128)(2,1)S(1)}, bf16[8192,128]{1,0:T(8,128)(2,1)S(1)}, u32[]{:S(2)}, u32[]{:S(2)}) collective-permute-start(bf16[8192,128]{1,0:T(8,128)(2,1)S(1)} %get-tuple-element.128), channel_id=1, source_target_pairs={{0,32},{32,0},{1,33},{33,1},{2,34},{34,2},{3,35},{35,3},{4,36},{36... | collective-permute-start | bytes 6291464 | tf_op jit(solution)/shard_map/ppermute | solution.py:226
  68.0 9.1 %collective-permute-start.19 = (bf16[1024,128]{1,0:T(8,128)(2,1)S(1)}, bf16[1024,128]{1,0:T(8,128)(2,1)S(1)}, u32[]{:S(2)}, u32[]{:S(2)}) collective-permute-start(bf16[1024,128]{1,0:T(8,128)(2,1)S(1)} %get-tuple-element.124), channel_id=1, source_target_pairs={{0,24},{8,16},{16,8},{24,0},{1,25},{9,17},{17,9},{25,1},{2,26},{10... | collective-permute-start | bytes 786440 | tf_op jit(solution)/shard_map/ppermute | solution.py:226
  69.2 8.7 %collective-permute-start.20 = (bf16[1024,128]{1,0:T(8,128)(2,1)S(1)}, bf16[1024,128]{1,0:T(8,128)(2,1)S(1)}, u32[]{:S(2)}, u32[]{:S(2)}) collective-permute-start(bf16[1024,128]{1,0:T(8,128)(2,1)S(1)} %get-tuple-element.125), channel_id=1, source_target_pairs={{0,6},{2,4},{4,2},{6,0},{1,7},{3,5},{5,3},{7,1},{8,14},{10,12},{12... | collective-permute-start | bytes 786440 | tf_op jit(solution)/shard_map/ppermute | solution.py:226
  70.2 7.8 %collective-permute-start.21 = (bf16[1024,128]{1,0:T(8,128)(2,1)S(1)}, bf16[1024,128]{1,0:T(8,128)(2,1)S(1)}, u32[]{:S(2)}, u32[]{:S(2)}) collective-permute-start(bf16[1024,128]{1,0:T(8,128)(2,1)S(1)} %get-tuple-element.126), channel_id=1, source_target_pairs={{0,8},{8,0},{16,24},{24,16},{1,9},{9,1},{17,25},{25,17},{2,10},{10... | collective-permute-start | bytes 786440 | tf_op jit(solution)/shard_map/ppermute | solution.py:226
  70.2 7.8 %collective-permute-start.22 = (bf16[1024,128]{1,0:T(8,128)(2,1)S(1)}, bf16[1024,128]{1,0:T(8,128)(2,1)S(1)}, u32[]{:S(2)}, u32[]{:S(2)}) collective-permute-start(bf16[1024,128]{1,0:T(8,128)(2,1)S(1)} %get-tuple-element.127), channel_id=1, source_target_pairs={{0,2},{2,0},{4,6},{6,4},{1,3},{3,1},{5,7},{7,5},{8,10},{10,8},{12,... | collective-permute-start | bytes 786440 | tf_op jit(solution)/shard_map/ppermute | solution.py:226
  78.0 2.4 %collective-permute-start.24 = (bf16[1024,128]{1,0:T(8,128)(2,1)S(1)}, bf16[1024,128]{1,0:T(8,128)(2,1)S(1)}, u32[]{:S(2)}, u32[]{:S(2)}) collective-permute-start(bf16[1024,128]{1,0:T(8,128)(2,1)S(1)} %collective-permute-done.19.refs_0_), channel_id=1, source_target_pairs={{0,32},{32,0},{1,33},{33,1},{2,34},{34,2},{3,35},{35,3},{4,36},{36... | collective-permute-start | bytes 786440 | tf_op jit(solution)/shard_map/ppermute | solution.py:226
  79.2 1.5 %collective-permute-start.25 = (bf16[1024,128]{1,0:T(8,128)(2,1)S(1)}, bf16[1024,128]{1,0:T(8,128)(2,1)S(1)}, u32[]{:S(2)}, u32[]{:S(2)}) collective-permute-start(bf16[1024,128]{1,0:T(8,128)(2,1)S(1)} %collective-permute-done.20.refs_1_), channel_id=1, source_target_pairs={{0,32},{32,0},{1,33},{33,1},{2,34},{34,2},{3,35},{35,3},{4,36},{36... | collective-permute-start | bytes 786440 | tf_op jit(solution)/shard_map/ppermute | solution.py:226
  79.3 1.8 %collective-permute-start.26 = (bf16[1024,128]{1,0:T(8,128)(2,1)S(1)}, bf16[1024,128]{1,0:T(8,128)(2,1)S(1)}, u32[]{:S(2)}, u32[]{:S(2)}) collective-permute-start(bf16[1024,128]{1,0:T(8,128)(2,1)S(1)} %collective-permute-done.21.refs_2_), channel_id=1, source_target_pairs={{0,32},{32,0},{1,33},{33,1},{2,34},{34,2},{3,35},{35,3},{4,36},{36... | collective-permute-start | bytes 786440 | tf_op jit(solution)/shard_map/ppermute | solution.py:226
  79.7 1.8 %collective-permute-start.27 = (bf16[1024,128]{1,0:T(8,128)(2,1)S(1)}, bf16[1024,128]{1,0:T(8,128)(2,1)S(1)}, u32[]{:S(2)}, u32[]{:S(2)}) collective-permute-start(bf16[1024,128]{1,0:T(8,128)(2,1)S(1)} %collective-permute-done.22.refs_3_), channel_id=1, source_target_pairs={{0,32},{32,0},{1,33},{33,1},{2,34},{34,2},{3,35},{35,3},{4,36},{36... | collective-permute-start | bytes 786440 | tf_op jit(solution)/shard_map/ppermute | solution.py:226

commit v6 on v5

--- a/solution.py
+++ b/solution.py
@@ -118,17 +118,13 @@
 
 
 def join_kernel(*refs):
-    rows, mine_0, mine_1, everything = refs[8:]
-    for h, mine in ((0, mine_0), (1, mine_1)):
+    for h in range(2):
         for k in range(4):
-            value = refs[4 * h + k][...]
-            mine[512 * k : 512 * k + 512] = value
-            everything[2048 * h + 512 * k : 2048 * h + 512 * k + 512] = value
-    everything[4096:4288] = rows[...].reshape(192, 128)
+            refs[8 + h][512 * k : 512 * k + 512] = refs[4 * h + k][...]
 
 
 def blocks_kernel(rows_own, other, blocks):
-    rows_sibling = other[4096:4288].reshape(4, 48, 128)
+    rows_sibling = other[...]
     for side, rows in ((0, rows_own[...]), (1, rows_sibling)):
         for h in range(2):
             for zl in range(4):
@@ -208,7 +204,7 @@
 
 
 def pick_first(refs, side, d, h, inner):
-    return refs[side], 2048 * h + 512 * inner
+    return refs[2 * side + h], 512 * inner
 
 
 def pick_near(refs, side, d, h, inner):
@@ -287,18 +283,20 @@
     halves = half_0, half_1
 
     first, second = ("x", "y"), ("y", "x")
-    parts = [[halves[h]] + [hop(halves[h], first[h], k) for k in (1, 2, 3)] for h in range(2)]
-    parts = lax.optimization_barrier(parts)
-    mine_0, mine_1, everything = pl.pallas_call(
+    pieces = {(h, k): hop(halves[h], first[h], k) for k in (1, 3, 2) for h in range(2)}
+    pieces = lax.optimization_barrier([pieces[h, k] for k in (1, 3, 2) for h in range(2)])
+    parts = [[halves[h], pieces[h], pieces[4 + h], pieces[2 + h]] for h in range(2)]
+    mine_0, mine_1 = pl.pallas_call(
         join_kernel,
-        out_shape=(pltpu.VMEM((2048, 128), HALF),) * 2 + (pltpu.VMEM((4288, 128), HALF),),
-        in_specs=[VMEM] * 9,
-        out_specs=(VMEM,) * 3,
-        compiler_params=limit(6),
-    )(*[inside(p) for p in parts[0] + parts[1]], inside(rows_own))
+        out_shape=(pltpu.VMEM((2048, 128), HALF),) * 2,
+        in_specs=[VMEM] * 8,
+        out_specs=(VMEM,) * 2,
+        compiler_params=limit(4),
+    )(*[inside(p) for p in parts[0] + parts[1]])
     mine = mine_0, mine_1
     near = [hop(mine[h], second[h], k) for k in (1, 3) for h in range(2)]
-    other = hop(everything, "core", 1)
+    other = [hop(v, "core", 1) for v in mine]
+    rows_other = hop(rows_own, "core", 1)
     base, mine_0 = lax.optimization_barrier((base_rows, mine_0))
     base = pl.pallas_call(
         stash_kernel,
@@ -315,7 +313,7 @@
         in_specs=[VMEM] * 2,
         out_specs=VMEM,
         compiler_params=limit(4),
-    )(inside(rows_own), inside(other))
+    )(inside(rows_own), inside(rows_other))
     states = pl.pallas_call(
         state_kernel,
         out_shape=(sa, sb, sa, sa, sb, sb),
@@ -346,7 +344,7 @@
             cost_estimate=cost(1024),
         )(place, inside(blocks), inside(base), *[inside(v) for v in pieces], *before)
 
-    merged = merge((0,), pick_first, [everything, other], None)
+    merged = merge((0,), pick_first, [*mine, *other], None)
     near, merged, states = lax.optimization_barrier((near, merged, states))
     half = shape((1024, 128), HALF)
     *relayed, everything = pl.pallas_call(

time: 84.4 us -> 83.4 us (0.988)
  Pallas kernels: 19.5 us -> 17.8 us
    pallas_call x1, Pallas kernels: 1.62 us -> 0.07 us  [per_device(): pl.pallas_call(join_kernel, out_shape=(pltpu.VMEM((2048, 128), HALF),) *...]
    ppermute x28 -> x30, waiting for transfers between devices: 24.5 us -> 24 us  [hop(): return lax.ppermute(value, axis, [(i, i ^ k) for i in range(n)])]
    ppermute x28 -> x30, starting transfers between devices: 39.1 us -> 39.5 us  [hop(): return lax.ppermute(value, axis, [(i, i ^ k) for i in range(n)])]
  transfers between devices with their start and end apart: 28 -> 30, of which waited for: 20 -> 19; matrix products, arithmetic and copies ran while one was open for 0% -> 0% of each run, Pallas kernels for 14% -> 14%
where the time goes in v6:
time: 83.4 us; the launch traced here: 83.2 us
  starting transfers between devices  39.5 us (47%)
  waiting for transfers between devices  24 us (29%)
  Pallas kernels  17.8 us (21%)
  between operations  0.93 us (1%)
    ppermute x30, starting transfers between devices, hop(): return lax.ppermute(value, axis, [(i, i ^ k) for i in range(n)])  39.5 us
    ppermute x30, waiting for transfers between devices, hop(): return lax.ppermute(value, axis, [(i, i ^ k) for i in range(n)])  24 us
    pallas_call x3, Pallas kernels, merge(): pl.pallas_call(functools.partial(next_merge_kernel if before else merge_k...  9.51 us
    pallas_call x1, Pallas kernels, per_device(): pl.pallas_call(stash_kernel, out_shape=pltpu.VMEM((4, 2, 2, 48, 4096), HA...  2.92 us
    pallas_call x1, Pallas kernels, per_device(): pl.pallas_call(pack_kernel, out_shape=[pltpu.VMEM((4, 176, 128), f32), pl...  1.9 us
    pallas_call x1, Pallas kernels, per_device(): pl.pallas_call(state_kernel, out_shape=(sa, sb, sa, sa, sb, sb), in_specs...  1.77 us
  transfers between devices with their start and end apart: 30, of which 19 were waited for; matrix products, arithmetic and copies ran while one was open for 0% of the time, Pallas kernels for 14%

profile of v6, /device:TPU:1, one launch (start us, length us, event | category | flops | bytes accessed | tf_op | source)
XLA Modules:
  0.0 83.2 jit_solution(1939699383483569222)
XLA Ops:
  0.6 0.1 pad_add_fusion
  0.7 1.9 %shard_map.144 = (f32[4,176,128]{2,1,0:T(8,128)S(1)}, bf16[4,176,128]{2,1,0:T(8,128)(2,1)S(1)}, f32[2,64,128]{2,1,0:T(8,128)S(1)}, f32[2,48,64]{2,1,0:T(8,128)S(...) custom-call(s32[2]{0:T(128)S(1)} %get-tuple-element.130.place, ...), custom_call_target="tpu_custom_call" | custom-call | tf_op jit(solution)/shard_map/pallas_call | solution.py:239
  2.6 3.3 %collective-permute-start = (bf16[4,176,128]{2,1,0:T(8,128)(2,1)S(1)}, bf16[4,176,128]{2,1,0:T(8,128)(2,1)S(1)}, u32[]{:S(2)}, u32[]{:S(2)}) collective-permute-start(bf16[4,176,128]{2,1,0:T(8,128)(2,1)S(1)} %get-tuple-element.69), channel_id=1, source_target_pairs={{0,32},{32,0},{1,33},{33,1},{2,34},{34,2},{3,35},{35,3},{4,36},{36... | collective-permute-start | bytes 540680 | tf_op jit(solution)/shard_map/ppermute | solution.py:222
  6.0 1.0 %collective-permute-done.given = bf16[4,176,128]{2,1,0:T(8,128)(2,1)S(1)} collective-permute-done((bf16[4,176,128]{2,1,0:T(8,128)(2,1)S(1)}, bf16[4,176,128]{2,1,0:T(8,128)(2,1)S(1)}, u32[]{:S(2)}, u32[]{:S(2)}) %collective-permute-start) | collective-permute-done | bytes 180256 | tf_op jit(solution)/shard_map/ppermute | solution.py:222
  7.0 0.6 shard_map.145
  7.6 0.1 collective-permute-start.1
  7.7 2.9 %collective-permute-start.2 = (bf16[176,128]{1,0:T(8,128)(2,1)S(1)}, bf16[176,128]{1,0:T(8,128)(2,1)S(1)}, u32[]{:S(2)}, u32[]{:S(2)}) collective-permute-start(bf16[176,128]{1,0:T(8,128)(2,1)S(1)} %get-tuple-element.72), channel_id=1, source_target_pairs={{0,128},{64,192},{128,0},{192,64},{1,129},{65,193},{129,1},{193,65... | collective-permute-start | bytes 135176 | tf_op jit(solution)/shard_map/ppermute | solution.py:222
  10.6 0.7 collective-permute-start.3
  11.2 0.0 collective-permute-done.1.got_1
  11.2 0.8 collective-permute-done.2.got_2
  12.0 3.3 %collective-permute-done.3.got_3 = bf16[176,128]{1,0:T(8,128)(2,1)S(1)} collective-permute-done((bf16[176,128]{1,0:T(8,128)(2,1)S(1)}, bf16[176,128]{1,0:T(8,128)(2,1)S(1)}, u32[]{:S(2)}, u32[]{:S(2)}) %collective-permute-start.3) | collective-permute-done | bytes 45088 | tf_op jit(solution)/shard_map/ppermute | solution.py:222
  15.3 0.2 shard_map.146
  15.5 4.3 %collective-permute-start.4 = (bf16[128,128]{1,0:T(8,128)(2,1)S(1)}, bf16[128,128]{1,0:T(8,128)(2,1)S(1)}, u32[]{:S(2)}, u32[]{:S(2)}) collective-permute-start(bf16[128,128]{1,0:T(8,128)(2,1)S(1)} %get-tuple-element.84), channel_id=1, source_target_pairs={{0,1},{1,0},{2,3},{3,2},{4,5},{5,4},{6,7},{7,6},{8,9},{9,8},{10,11... | collective-permute-start | bytes 98312 | tf_op jit(solution)/shard_map/ppermute | solution.py:222
  19.8 2.4 %collective-permute-done.4.across = bf16[128,128]{1,0:T(8,128)(2,1)S(1)} collective-permute-done((bf16[128,128]{1,0:T(8,128)(2,1)S(1)}, bf16[128,128]{1,0:T(8,128)(2,1)S(1)}, u32[]{:S(2)}, u32[]{:S(2)}) %collective-permute-start.4) | collective-permute-done | bytes 32800 | tf_op jit(solution)/shard_map/ppermute | solution.py:222
  22.2 0.8 collective-permute-start.7
  23.0 0.1 collective-permute-start.6
  23.1 2.6 %collective-permute-start.5 = (bf16[304,128]{1,0:T(8,128)(2,1)S(1)}, bf16[304,128]{1,0:T(8,128)(2,1)S(1)}, u32[]{:S(2)}, u32[]{:S(2)}) collective-permute-start(bf16[304,128]{1,0:T(8,128)(2,1)S(1)} %shard_map.147.refs_0_), channel_id=1, source_target_pairs={{0,64},{64,0},{128,192},{192,128},{1,65},{65,1},{129,193},{193,129... | collective-permute-start | bytes 233480 | tf_op jit(solution)/shard_map/ppermute | solution.py:222
  25.8 1.7 %collective-permute-done.7.refs_3_ = bf16[304,128]{1,0:T(8,128)(2,1)S(1)} collective-permute-done((bf16[304,128]{1,0:T(8,128)(2,1)S(1)}, bf16[304,128]{1,0:T(8,128)(2,1)S(1)}, u32[]{:S(2)}, u32[]{:S(2)}) %collective-permute-start.7) | collective-permute-done | bytes 77856 | tf_op jit(solution)/shard_map/ppermute | solution.py:222
  27.4 2.0 %collective-permute-done.6.refs_2_ = bf16[304,128]{1,0:T(8,128)(2,1)S(1)} collective-permute-done((bf16[304,128]{1,0:T(8,128)(2,1)S(1)}, bf16[304,128]{1,0:T(8,128)(2,1)S(1)}, u32[]{:S(2)}, u32[]{:S(2)}) %collective-permute-start.6) | collective-permute-done | bytes 77856 | tf_op jit(solution)/shard_map/ppermute | solution.py:222
  29.4 0.6 shard_map.148
  30.0 2.7 %collective-permute-start.13 = (bf16[512,128]{1,0:T(8,128)(2,1)S(1)}, bf16[512,128]{1,0:T(8,128)(2,1)S(1)}, u32[]{:S(2)}, u32[]{:S(2)}) collective-permute-start(bf16[512,128]{1,0:T(8,128)(2,1)S(1)} %bitcast.13), channel_id=1, source_target_pairs={{0,16},{8,24},{16,0},{24,8},{1,17},{9,25},{17,1},{25,9},{2,18},{10... | collective-permute-start | bytes 393224 | tf_op jit(solution)/shard_map/ppermute | solution.py:222
  32.7 0.8 collective-permute-start.11
  33.5 2.7 %collective-permute-start.12 = (bf16[512,128]{1,0:T(8,128)(2,1)S(1)}, bf16[512,128]{1,0:T(8,128)(2,1)S(1)}, u32[]{:S(2)}, u32[]{:S(2)}) collective-permute-start(bf16[512,128]{1,0:T(8,128)(2,1)S(1)} %bitcast.9), channel_id=1, source_target_pairs={{0,4},{2,6},{4,0},{6,2},{1,5},{3,7},{5,1},{7,3},{8,12},{10,14},{12... | collective-permute-start | bytes 393224 | tf_op jit(solution)/shard_map/ppermute | solution.py:222
  36.2 0.9 %collective-permute-start.10 = (bf16[512,128]{1,0:T(8,128)(2,1)S(1)}, bf16[512,128]{1,0:T(8,128)(2,1)S(1)}, u32[]{:S(2)}, u32[]{:S(2)}) collective-permute-start(bf16[512,128]{1,0:T(8,128)(2,1)S(1)} %bitcast.10), channel_id=1, source_target_pairs={{0,6},{2,4},{4,2},{6,0},{1,7},{3,5},{5,3},{7,1},{8,14},{10,12},{12... | collective-permute-start | bytes 393224 | tf_op jit(solution)/shard_map/ppermute | solution.py:222
  37.1 0.6 collective-permute-done.11.refs_7_
  37.7 1.4 %collective-permute-done.12.refs_2_ = bf16[512,128]{1,0:T(8,128)(2,1)S(1)} collective-permute-done((bf16[512,128]{1,0:T(8,128)(2,1)S(1)}, bf16[512,128]{1,0:T(8,128)(2,1)S(1)}, u32[]{:S(2)}, u32[]{:S(2)}) %collective-permute-start.12) | collective-permute-done | bytes 131104 | tf_op jit(solution)/shard_map/ppermute | solution.py:222
  39.1 2.5 %collective-permute-done.10.refs_3_ = bf16[512,128]{1,0:T(8,128)(2,1)S(1)} collective-permute-done((bf16[512,128]{1,0:T(8,128)(2,1)S(1)}, bf16[512,128]{1,0:T(8,128)(2,1)S(1)}, u32[]{:S(2)}, u32[]{:S(2)}) %collective-permute-start.10) | collective-permute-done | bytes 131104 | tf_op jit(solution)/shard_map/ppermute | solution.py:222
  41.5 0.1 shard_map.149
  41.6 5.8 %collective-permute-start.20 = (bf16[2048,128]{1,0:T(8,128)(2,1)S(1)}, bf16[2048,128]{1,0:T(8,128)(2,1)S(1)}, u32[]{:S(2)}, u32[]{:S(2)}) collective-permute-start(bf16[2048,128]{1,0:T(8,128)(2,1)S(1)} %get-tuple-element.98.refs_1_), channel_id=1, source_target_pairs={{0,32},{32,0},{1,33},{33,1},{2,34},{34,2},{3,35},{35,3},{4,36},{36... | collective-permute-start | bytes 1572872 | tf_op jit(solution)/shard_map/ppermute | solution.py:222
  47.4 0.1 collective-permute-start.18
  47.5 1.7 %collective-permute-start.17 = (bf16[2048,128]{1,0:T(8,128)(2,1)S(1)}, bf16[2048,128]{1,0:T(8,128)(2,1)S(1)}, u32[]{:S(2)}, u32[]{:S(2)}) collective-permute-start(bf16[2048,128]{1,0:T(8,128)(2,1)S(1)} %get-tuple-element.98.refs_1_), channel_id=1, source_target_pairs={{0,6},{2,4},{4,2},{6,0},{1,7},{3,5},{5,3},{7,1},{8,14},{10,12},{12... | collective-permute-start | bytes 1572872 | tf_op jit(solution)/shard_map/ppermute | solution.py:222
  49.2 0.7 collective-permute-start.19
  49.9 2.0 %collective-permute-start.16 = (bf16[2048,128]{1,0:T(8,128)(2,1)S(1)}, bf16[2048,128]{1,0:T(8,128)(2,1)S(1)}, u32[]{:S(2)}, u32[]{:S(2)}) collective-permute-start(bf16[2048,128]{1,0:T(8,128)(2,1)S(1)} %get-tuple-element.97.refs_0_), channel_id=1, source_target_pairs={{0,24},{8,16},{16,8},{24,0},{1,25},{9,17},{17,9},{25,1},{2,26},{10... | collective-permute-start | bytes 1572872 | tf_op jit(solution)/shard_map/ppermute | solution.py:222
  51.9 0.8 copy-done
  52.7 1.1 %collective-permute-start.14 = (bf16[2048,128]{1,0:T(8,128)(2,1)S(1)}, bf16[2048,128]{1,0:T(8,128)(2,1)S(1)}, u32[]{:S(2)}, u32[]{:S(2)}) collective-permute-start(bf16[2048,128]{1,0:T(8,128)(2,1)S(1)} %get-tuple-element.97.refs_0_), channel_id=1, source_target_pairs={{0,8},{8,0},{16,24},{24,16},{1,9},{9,1},{17,25},{25,17},{2,10},{10... | collective-permute-start | bytes 1572872 | tf_op jit(solution)/shard_map/ppermute | solution.py:222
  53.8 0.1 pad_add_fusion.2.place
  53.9 1.8 %shard_map.153 = (f32[2,64,128]{2,1,0:T(8,128)}, f32[2,48,64]{2,1,0:T(8,128)}, f32[2,64,128]{2,1,0:T(8,128)}, f32[2,64,128]{2,1,0:T(8,128)}, f32[2,48,64]{2,1,0:T(8,128)}, /*index=5*/f32[2,48,64]{2,1,0:T(8,128)}) custom-call(f32[176,128]{1,0:T(8,128)S(1)} %get-tuple-element.101.total, f32[2,64,128]{2,1,0:T(8,128)} %refs_0_.3, f32[2,48,64]{2,1,0:T(8,128)} %refs_1_.3, ...), custom_call_target="tpu_custom_call" | custom-call | bytes 1024 | tf_op jit(solution)/shard_map/pallas_call | solution.py:317
  55.6 0.1 shard_map.150.blocks
  55.7 0.0 copy-start.1
  55.8 2.9 %shard_map.151.base = bf16[4,2,2,48,4096]{4,3,2,1,0:T(8,128)(2,1)S(1)} custom-call(bf16[4,2,2,48,4096]{4,3,2,1,0:T(8,128)(2,1)} %bitcast.18), custom_call_target="tpu_custom_call" | custom-call | bytes 1024 | tf_op jit(solution)/shard_map/pallas_call | solution.py:301
  58.7 3.1 %shard_map.152.refs_5_ = bf16[4,2,2,48,4096]{4,3,2,1,0:T(8,128)(2,1)} custom-call(s32[3]{0:T(128)S(1)} %pad_add_fusion.2.place, bf16[2,2,192,256]{3,2,1,0:T(8,128)(2,1)S(1)} %shard_map.150.blocks, bf16[4,2,2,48,4096]{4,3,2,1,0:T(8,128)(2,1)S(1)} %shard_map.151.base, bf16[2048,128]{1,0:T(8,128)(2,1)S(1)} %get-tuple-element.97.refs_0_, ...), custom_call_target="tpu_custom_call" | custom-call | bytes 1024 | tf_op jit(solution)/shard_map/pallas_call | solution.py:332
  61.8 0.0 collective-permute-done.17.down_1.refs_3_
  61.8 1.7 %collective-permute-done.15.up_1.refs_1_ = bf16[2048,128]{1,0:T(8,128)(2,1)S(1)} collective-permute-done((bf16[2048,128]{1,0:T(8,128)(2,1)S(1)}, bf16[2048,128]{1,0:T(8,128)(2,1)S(1)}, u32[]{:S(2)}, u32[]{:S(2)}) %collective-permute-start.15) | collective-permute-done | bytes 524320 | tf_op jit(solution)/shard_map/ppermute | solution.py:222
  63.5 1.1 %collective-permute-done.16.down_0.refs_2_ = bf16[2048,128]{1,0:T(8,128)(2,1)S(1)} collective-permute-done((bf16[2048,128]{1,0:T(8,128)(2,1)S(1)}, bf16[2048,128]{1,0:T(8,128)(2,1)S(1)}, u32[]{:S(2)}, u32[]{:S(2)}) %collective-permute-start.16) | collective-permute-done | bytes 524320 | tf_op jit(solution)/shard_map/ppermute | solution.py:222
  64.6 1.2 %collective-permute-done.14.up_0.refs_0_ = bf16[2048,128]{1,0:T(8,128)(2,1)S(1)} collective-permute-done((bf16[2048,128]{1,0:T(8,128)(2,1)S(1)}, bf16[2048,128]{1,0:T(8,128)(2,1)S(1)}, u32[]{:S(2)}, u32[]{:S(2)}) %collective-permute-start.14) | collective-permute-done | bytes 524320 | tf_op jit(solution)/shard_map/ppermute | solution.py:222
  65.9 0.2 shard_map.154
  66.1 1.3 %collective-permute-start.25 = (bf16[8192,128]{1,0:T(8,128)(2,1)S(1)}, bf16[8192,128]{1,0:T(8,128)(2,1)S(1)}, u32[]{:S(2)}, u32[]{:S(2)}) collective-permute-start(bf16[8192,128]{1,0:T(8,128)(2,1)S(1)} %get-tuple-element.122), channel_id=1, source_target_pairs={{0,32},{32,0},{1,33},{33,1},{2,34},{34,2},{3,35},{35,3},{4,36},{36... | collective-permute-start | bytes 6291464 | tf_op jit(solution)/shard_map/ppermute | solution.py:222
  67.4 0.7 collective-permute-start.21
  68.1 0.9 %collective-permute-start.22 = (bf16[1024,128]{1,0:T(8,128)(2,1)S(1)}, bf16[1024,128]{1,0:T(8,128)(2,1)S(1)}, u32[]{:S(2)}, u32[]{:S(2)}) collective-permute-start(bf16[1024,128]{1,0:T(8,128)(2,1)S(1)} %get-tuple-element.119), channel_id=1, source_target_pairs={{0,6},{2,4},{4,2},{6,0},{1,7},{3,5},{5,3},{7,1},{8,14},{10,12},{12... | collective-permute-start | bytes 786440 | tf_op jit(solution)/shard_map/ppermute | solution.py:222
  69.0 0.5 collective-permute-start.23
  69.5 0.9 %collective-permute-start.24 = (bf16[1024,128]{1,0:T(8,128)(2,1)S(1)}, bf16[1024,128]{1,0:T(8,128)(2,1)S(1)}, u32[]{:S(2)}, u32[]{:S(2)}) collective-permute-start(bf16[1024,128]{1,0:T(8,128)(2,1)S(1)} %get-tuple-element.121), channel_id=1, source_target_pairs={{0,2},{2,0},{4,6},{6,4},{1,3},{3,1},{5,7},{7,5},{8,10},{10,8},{12,... | collective-permute-start | bytes 786440 | tf_op jit(solution)/shard_map/ppermute | solution.py:222
  70.4 0.8 collective-permute-done.25.refs_4_
  71.1 3.9 %shard_map.155.refs_8_ = bf16[4,2,2,48,4096]{4,3,2,1,0:T(8,128)(2,1)} custom-call(s32[3]{0:T(128)S(1)} %pad_add_fusion.2.place, bf16[2,2,192,256]{3,2,1,0:T(8,128)(2,1)S(1)} %shard_map.150.blocks, bf16[4,2,2,48,4096]{4,3,2,1,0:T(8,128)(2,1)S(1)} %shard_map.151.base, ...), custom_call_target="tpu_custom_call", output_to_operand_aliasing={{}: (8, {})} | custom-call | bytes 1024 | tf_op jit(solution)/shard_map/pallas_call | solution.py:332
  75.0 1.4 %collective-permute-done.21.refs_0_ = bf16[1024,128]{1,0:T(8,128)(2,1)S(1)} collective-permute-done((bf16[1024,128]{1,0:T(8,128)(2,1)S(1)}, bf16[1024,128]{1,0:T(8,128)(2,1)S(1)}, u32[]{:S(2)}, u32[]{:S(2)}) %collective-permute-start.21) | collective-permute-done | bytes 262176 | tf_op jit(solution)/shard_map/ppermute | solution.py:222
  76.4 0.4 collective-permute-done.22.refs_1_
  76.8 1.4 %collective-permute-start.26 = (bf16[1024,128]{1,0:T(8,128)(2,1)S(1)}, bf16[1024,128]{1,0:T(8,128)(2,1)S(1)}, u32[]{:S(2)}, u32[]{:S(2)}) collective-permute-start(bf16[1024,128]{1,0:T(8,128)(2,1)S(1)} %collective-permute-done.21.refs_0_), channel_id=1, source_target_pairs={{0,32},{32,0},{1,33},{33,1},{2,34},{34,2},{3,35},{35,3},{4,36},{36... | collective-permute-start | bytes 786440 | tf_op jit(solution)/shard_map/ppermute | solution.py:222
  78.3 0.0 collective-permute-start.27
  78.3 0.5 collective-permute-start.28
  78.8 0.0 collective-permute-start.29
  78.8 0.6 collective-permute-done.26.refs_4_
  79.4 0.4 collective-permute-done.27.refs_5_
  79.8 0.4 collective-permute-done.28.refs_6_
  80.2 0.4 collective-permute-done.29.refs_7_
  80.5 2.5 %shard_map.156 = bf16[4,2,2,48,4096]{4,3,2,1,0:T(8,128)(2,1)} custom-call(s32[3]{0:T(128)S(1)} %pad_add_fusion.2.place, bf16[2,2,192,256]{3,2,1,0:T(8,128)(2,1)S(1)} %shard_map.150.blocks, bf16[4,2,2,48,4096]{4,3,2,1,0:T(8,128)(2,1)S(1)} %shard_map.151.base, bf16[1024,128]{1,0:T(8,128)(2,1)S(1)} %collective-permute-done.21.refs_0_, ...), custom_call_target="tpu_custom_call", output_to_operand_aliasing={{}: (11, {})} | custom-call | bytes 1024 | tf_op jit(solution)/shard_map/pallas_call | solution.py:332
  (15 shorter events, 0.0 us)
Async XLA Ops:
  2.6 4.4 %collective-permute-start = (bf16[4,176,128]{2,1,0:T(8,128)(2,1)S(1)}, bf16[4,176,128]{2,1,0:T(8,128)(2,1)S(1)}, u32[]{:S(2)}, u32[]{:S(2)}) collective-permute-start(bf16[4,176,128]{2,1,0:T(8,128)(2,1)S(1)} %get-tuple-element.69), channel_id=1, source_target_pairs={{0,32},{32,0},{1,33},{33,1},{2,34},{34,2},{3,35},{35,3},{4,36},{36... | collective-permute-start | bytes 540680 | tf_op jit(solution)/shard_map/ppermute | solution.py:222
  7.6 3.6 %collective-permute-start.1 = (bf16[176,128]{1,0:T(8,128)(2,1)S(1)}, bf16[176,128]{1,0:T(8,128)(2,1)S(1)}, u32[]{:S(2)}, u32[]{:S(2)}) collective-permute-start(bf16[176,128]{1,0:T(8,128)(2,1)S(1)} %get-tuple-element.71), channel_id=1, source_target_pairs={{0,64},{64,0},{128,192},{192,128},{1,65},{65,1},{129,193},{193,129... | collective-permute-start | bytes 135176 | tf_op jit(solution)/shard_map/ppermute | solution.py:222
  7.7 4.3 %collective-permute-start.2 = (bf16[176,128]{1,0:T(8,128)(2,1)S(1)}, bf16[176,128]{1,0:T(8,128)(2,1)S(1)}, u32[]{:S(2)}, u32[]{:S(2)}) collective-permute-start(bf16[176,128]{1,0:T(8,128)(2,1)S(1)} %get-tuple-element.72), channel_id=1, source_target_pairs={{0,128},{64,192},{128,0},{192,64},{1,129},{65,193},{129,1},{193,65... | collective-permute-start | bytes 135176 | tf_op jit(solution)/shard_map/ppermute | solution.py:222
  10.6 4.7 %collective-permute-start.3 = (bf16[176,128]{1,0:T(8,128)(2,1)S(1)}, bf16[176,128]{1,0:T(8,128)(2,1)S(1)}, u32[]{:S(2)}, u32[]{:S(2)}) collective-permute-start(bf16[176,128]{1,0:T(8,128)(2,1)S(1)} %get-tuple-element.73), channel_id=1, source_target_pairs={{0,192},{64,128},{128,64},{192,0},{1,193},{65,129},{129,65},{193,1... | collective-permute-start | bytes 135176 | tf_op jit(solution)/shard_map/ppermute | solution.py:222
  15.5 6.7 %collective-permute-start.4 = (bf16[128,128]{1,0:T(8,128)(2,1)S(1)}, bf16[128,128]{1,0:T(8,128)(2,1)S(1)}, u32[]{:S(2)}, u32[]{:S(2)}) collective-permute-start(bf16[128,128]{1,0:T(8,128)(2,1)S(1)} %get-tuple-element.84), channel_id=1, source_target_pairs={{0,1},{1,0},{2,3},{3,2},{4,5},{5,4},{6,7},{7,6},{8,9},{9,8},{10,11... | collective-permute-start | bytes 98312 | tf_op jit(solution)/shard_map/ppermute | solution.py:222
  22.2 5.2 %collective-permute-start.7 = (bf16[304,128]{1,0:T(8,128)(2,1)S(1)}, bf16[304,128]{1,0:T(8,128)(2,1)S(1)}, u32[]{:S(2)}, u32[]{:S(2)}) collective-permute-start(bf16[304,128]{1,0:T(8,128)(2,1)S(1)} %shard_map.147.refs_0_), channel_id=1, source_target_pairs={{0,192},{64,128},{128,64},{192,0},{1,193},{65,129},{129,65},{193,1... | collective-permute-start | bytes 233480 | tf_op jit(solution)/shard_map/ppermute | solution.py:222
  23.0 6.4 %collective-permute-start.6 = (bf16[304,128]{1,0:T(8,128)(2,1)S(1)}, bf16[304,128]{1,0:T(8,128)(2,1)S(1)}, u32[]{:S(2)}, u32[]{:S(2)}) collective-permute-start(bf16[304,128]{1,0:T(8,128)(2,1)S(1)} %shard_map.147.refs_0_), channel_id=1, source_target_pairs={{0,128},{64,192},{128,0},{192,64},{1,129},{65,193},{129,1},{193,65... | collective-permute-start | bytes 233480 | tf_op jit(solution)/shard_map/ppermute | solution.py:222
  23.1 6.3 %collective-permute-start.5 = (bf16[304,128]{1,0:T(8,128)(2,1)S(1)}, bf16[304,128]{1,0:T(8,128)(2,1)S(1)}, u32[]{:S(2)}, u32[]{:S(2)}) collective-permute-start(bf16[304,128]{1,0:T(8,128)(2,1)S(1)} %shard_map.147.refs_0_), channel_id=1, source_target_pairs={{0,64},{64,0},{128,192},{192,128},{1,65},{65,1},{129,193},{193,129... | collective-permute-start | bytes 233480 | tf_op jit(solution)/shard_map/ppermute | solution.py:222
  30.0 7.1 %collective-permute-start.13 = (bf16[512,128]{1,0:T(8,128)(2,1)S(1)}, bf16[512,128]{1,0:T(8,128)(2,1)S(1)}, u32[]{:S(2)}, u32[]{:S(2)}) collective-permute-start(bf16[512,128]{1,0:T(8,128)(2,1)S(1)} %bitcast.13), channel_id=1, source_target_pairs={{0,16},{8,24},{16,0},{24,8},{1,17},{9,25},{17,1},{25,9},{2,18},{10... | collective-permute-start | bytes 393224 | tf_op jit(solution)/shard_map/ppermute | solution.py:222
  32.7 5.0 %collective-permute-start.11 = (bf16[512,128]{1,0:T(8,128)(2,1)S(1)}, bf16[512,128]{1,0:T(8,128)(2,1)S(1)}, u32[]{:S(2)}, u32[]{:S(2)}) collective-permute-start(bf16[512,128]{1,0:T(8,128)(2,1)S(1)} %bitcast.14), channel_id=1, source_target_pairs={{0,24},{8,16},{16,8},{24,0},{1,25},{9,17},{17,9},{25,1},{2,26},{10... | collective-permute-start | bytes 393224 | tf_op jit(solution)/shard_map/ppermute | solution.py:222
  33.4 4.3 %collective-permute-start.9 = (bf16[512,128]{1,0:T(8,128)(2,1)S(1)}, bf16[512,128]{1,0:T(8,128)(2,1)S(1)}, u32[]{:S(2)}, u32[]{:S(2)}) collective-permute-start(bf16[512,128]{1,0:T(8,128)(2,1)S(1)} %bitcast.15), channel_id=1, source_target_pairs={{0,8},{8,0},{16,24},{24,16},{1,9},{9,1},{17,25},{25,17},{2,10},{10... | collective-permute-start | bytes 393224 | tf_op jit(solution)/shard_map/ppermute | solution.py:222
  33.5 5.6 %collective-permute-start.12 = (bf16[512,128]{1,0:T(8,128)(2,1)S(1)}, bf16[512,128]{1,0:T(8,128)(2,1)S(1)}, u32[]{:S(2)}, u32[]{:S(2)}) collective-permute-start(bf16[512,128]{1,0:T(8,128)(2,1)S(1)} %bitcast.9), channel_id=1, source_target_pairs={{0,4},{2,6},{4,0},{6,2},{1,5},{3,7},{5,1},{7,3},{8,12},{10,14},{12... | collective-permute-start | bytes 393224 | tf_op jit(solution)/shard_map/ppermute | solution.py:222
  36.2 5.3 %collective-permute-start.10 = (bf16[512,128]{1,0:T(8,128)(2,1)S(1)}, bf16[512,128]{1,0:T(8,128)(2,1)S(1)}, u32[]{:S(2)}, u32[]{:S(2)}) collective-permute-start(bf16[512,128]{1,0:T(8,128)(2,1)S(1)} %bitcast.10), channel_id=1, source_target_pairs={{0,6},{2,4},{4,2},{6,0},{1,7},{3,5},{5,3},{7,1},{8,14},{10,12},{12... | collective-permute-start | bytes 393224 | tf_op jit(solution)/shard_map/ppermute | solution.py:222
  37.1 4.5 %collective-permute-start.8 = (bf16[512,128]{1,0:T(8,128)(2,1)S(1)}, bf16[512,128]{1,0:T(8,128)(2,1)S(1)}, u32[]{:S(2)}, u32[]{:S(2)}) collective-permute-start(bf16[512,128]{1,0:T(8,128)(2,1)S(1)} %bitcast.11), channel_id=1, source_target_pairs={{0,2},{2,0},{4,6},{6,4},{1,3},{3,1},{5,7},{7,5},{8,10},{10,8},{12,... | collective-permute-start | bytes 393224 | tf_op jit(solution)/shard_map/ppermute | solution.py:222
  41.6 10.3 %collective-permute-start.20 = (bf16[2048,128]{1,0:T(8,128)(2,1)S(1)}, bf16[2048,128]{1,0:T(8,128)(2,1)S(1)}, u32[]{:S(2)}, u32[]{:S(2)}) collective-permute-start(bf16[2048,128]{1,0:T(8,128)(2,1)S(1)} %get-tuple-element.98.refs_1_), channel_id=1, source_target_pairs={{0,32},{32,0},{1,33},{33,1},{2,34},{34,2},{3,35},{35,3},{4,36},{36... | collective-permute-start | bytes 1572872 | tf_op jit(solution)/shard_map/ppermute | solution.py:222
  47.4 2.5 %collective-permute-start.18 = (bf16[4,48,128]{2,1,0:T(8,128)(2,1)S(1)}, bf16[4,48,128]{2,1,0:T(8,128)(2,1)S(1)}, u32[]{:S(2)}, u32[]{:S(2)}) collective-permute-start(bf16[4,48,128]{2,1,0:T(8,128)(2,1)S(1)} %get-tuple-element.99.rows_own), channel_id=1, source_target_pairs={{0,32},{32,0},{1,33},{33,1},{2,34},{34,2},{3,35},{35,3},{4,36},{36... | collective-permute-start | bytes 147464 | tf_op jit(solution)/shard_map/ppermute | solution.py:222
  47.5 14.3 %collective-permute-start.17 = (bf16[2048,128]{1,0:T(8,128)(2,1)S(1)}, bf16[2048,128]{1,0:T(8,128)(2,1)S(1)}, u32[]{:S(2)}, u32[]{:S(2)}) collective-permute-start(bf16[2048,128]{1,0:T(8,128)(2,1)S(1)} %get-tuple-element.98.refs_1_), channel_id=1, source_target_pairs={{0,6},{2,4},{4,2},{6,0},{1,7},{3,5},{5,3},{7,1},{8,14},{10,12},{12... | collective-permute-start | bytes 1572872 | tf_op jit(solution)/shard_map/ppermute | solution.py:222
  49.2 9.4 %collective-permute-start.19 = (bf16[2048,128]{1,0:T(8,128)(2,1)S(1)}, bf16[2048,128]{1,0:T(8,128)(2,1)}, u32[]{:S(2)}, u32[]{:S(2)}) collective-permute-start(bf16[2048,128]{1,0:T(8,128)(2,1)S(1)} %get-tuple-element.97.refs_0_), channel_id=1, source_target_pairs={{0,32},{32,0},{1,33},{33,1},{2,34},{34,2},{3,35},{35,3},{4,36},{36... | collective-permute-start | bytes 1572872 | tf_op jit(solution)/shard_map/ppermute | solution.py:222
  49.9 13.6 %collective-permute-start.15 = (bf16[2048,128]{1,0:T(8,128)(2,1)S(1)}, bf16[2048,128]{1,0:T(8,128)(2,1)S(1)}, u32[]{:S(2)}, u32[]{:S(2)}) collective-permute-start(bf16[2048,128]{1,0:T(8,128)(2,1)S(1)} %get-tuple-element.98.refs_1_), channel_id=1, source_target_pairs={{0,2},{2,0},{4,6},{6,4},{1,3},{3,1},{5,7},{7,5},{8,10},{10,8},{12,... | collective-permute-start | bytes 1572872 | tf_op jit(solution)/shard_map/ppermute | solution.py:222
  49.9 14.7 %collective-permute-start.16 = (bf16[2048,128]{1,0:T(8,128)(2,1)S(1)}, bf16[2048,128]{1,0:T(8,128)(2,1)S(1)}, u32[]{:S(2)}, u32[]{:S(2)}) collective-permute-start(bf16[2048,128]{1,0:T(8,128)(2,1)S(1)} %get-tuple-element.97.refs_0_), channel_id=1, source_target_pairs={{0,24},{8,16},{16,8},{24,0},{1,25},{9,17},{17,9},{25,1},{2,26},{10... | collective-permute-start | bytes 1572872 | tf_op jit(solution)/shard_map/ppermute | solution.py:222
  51.9 0.8 copy-start
  52.7 13.2 %collective-permute-start.14 = (bf16[2048,128]{1,0:T(8,128)(2,1)S(1)}, bf16[2048,128]{1,0:T(8,128)(2,1)S(1)}, u32[]{:S(2)}, u32[]{:S(2)}) collective-permute-start(bf16[2048,128]{1,0:T(8,128)(2,1)S(1)} %get-tuple-element.97.refs_0_), channel_id=1, source_target_pairs={{0,8},{8,0},{16,24},{24,16},{1,9},{9,1},{17,25},{25,17},{2,10},{10... | collective-permute-start | bytes 1572872 | tf_op jit(solution)/shard_map/ppermute | solution.py:222
  55.7 3.0 %copy-start.1 = (bf16[2048,128]{1,0:T(8,128)(2,1)S(1)}, bf16[2048,128]{1,0:T(8,128)(2,1)}, u32[]{:S(2)}) copy-start(bf16[2048,128]{1,0:T(8,128)(2,1)} %copy-done) | copy-start | bytes 1572868
  66.1 5.1 %collective-permute-start.25 = (bf16[8192,128]{1,0:T(8,128)(2,1)S(1)}, bf16[8192,128]{1,0:T(8,128)(2,1)S(1)}, u32[]{:S(2)}, u32[]{:S(2)}) collective-permute-start(bf16[8192,128]{1,0:T(8,128)(2,1)S(1)} %get-tuple-element.122), channel_id=1, source_target_pairs={{0,32},{32,0},{1,33},{33,1},{2,34},{34,2},{3,35},{35,3},{4,36},{36... | collective-permute-start | bytes 6291464 | tf_op jit(solution)/shard_map/ppermute | solution.py:222
  67.4 9.1 %collective-permute-start.21 = (bf16[1024,128]{1,0:T(8,128)(2,1)S(1)}, bf16[1024,128]{1,0:T(8,128)(2,1)S(1)}, u32[]{:S(2)}, u32[]{:S(2)}) collective-permute-start(bf16[1024,128]{1,0:T(8,128)(2,1)S(1)} %get-tuple-element.118), channel_id=1, source_target_pairs={{0,24},{8,16},{16,8},{24,0},{1,25},{9,17},{17,9},{25,1},{2,26},{10... | collective-permute-start | bytes 786440 | tf_op jit(solution)/shard_map/ppermute | solution.py:222
  68.1 8.7 %collective-permute-start.22 = (bf16[1024,128]{1,0:T(8,128)(2,1)S(1)}, bf16[1024,128]{1,0:T(8,128)(2,1)S(1)}, u32[]{:S(2)}, u32[]{:S(2)}) collective-permute-start(bf16[1024,128]{1,0:T(8,128)(2,1)S(1)} %get-tuple-element.119), channel_id=1, source_target_pairs={{0,6},{2,4},{4,2},{6,0},{1,7},{3,5},{5,3},{7,1},{8,14},{10,12},{12... | collective-permute-start | bytes 786440 | tf_op jit(solution)/shard_map/ppermute | solution.py:222
  69.0 7.8 %collective-permute-start.23 = (bf16[1024,128]{1,0:T(8,128)(2,1)S(1)}, bf16[1024,128]{1,0:T(8,128)(2,1)S(1)}, u32[]{:S(2)}, u32[]{:S(2)}) collective-permute-start(bf16[1024,128]{1,0:T(8,128)(2,1)S(1)} %get-tuple-element.120), channel_id=1, source_target_pairs={{0,8},{8,0},{16,24},{24,16},{1,9},{9,1},{17,25},{25,17},{2,10},{10... | collective-permute-start | bytes 786440 | tf_op jit(solution)/shard_map/ppermute | solution.py:222
  69.5 7.3 %collective-permute-start.24 = (bf16[1024,128]{1,0:T(8,128)(2,1)S(1)}, bf16[1024,128]{1,0:T(8,128)(2,1)S(1)}, u32[]{:S(2)}, u32[]{:S(2)}) collective-permute-start(bf16[1024,128]{1,0:T(8,128)(2,1)S(1)} %get-tuple-element.121), channel_id=1, source_target_pairs={{0,2},{2,0},{4,6},{6,4},{1,3},{3,1},{5,7},{7,5},{8,10},{10,8},{12,... | collective-permute-start | bytes 786440 | tf_op jit(solution)/shard_map/ppermute | solution.py:222
  76.8 2.6 %collective-permute-start.26 = (bf16[1024,128]{1,0:T(8,128)(2,1)S(1)}, bf16[1024,128]{1,0:T(8,128)(2,1)S(1)}, u32[]{:S(2)}, u32[]{:S(2)}) collective-permute-start(bf16[1024,128]{1,0:T(8,128)(2,1)S(1)} %collective-permute-done.21.refs_0_), channel_id=1, source_target_pairs={{0,32},{32,0},{1,33},{33,1},{2,34},{34,2},{3,35},{35,3},{4,36},{36... | collective-permute-start | bytes 786440 | tf_op jit(solution)/shard_map/ppermute | solution.py:222
  78.3 1.5 %collective-permute-start.27 = (bf16[1024,128]{1,0:T(8,128)(2,1)S(1)}, bf16[1024,128]{1,0:T(8,128)(2,1)S(1)}, u32[]{:S(2)}, u32[]{:S(2)}) collective-permute-start(bf16[1024,128]{1,0:T(8,128)(2,1)S(1)} %collective-permute-done.22.refs_1_), channel_id=1, source_target_pairs={{0,32},{32,0},{1,33},{33,1},{2,34},{34,2},{3,35},{35,3},{4,36},{36... | collective-permute-start | bytes 786440 | tf_op jit(solution)/shard_map/ppermute | solution.py:222
  78.3 1.9 %collective-permute-start.28 = (bf16[1024,128]{1,0:T(8,128)(2,1)S(1)}, bf16[1024,128]{1,0:T(8,128)(2,1)S(1)}, u32[]{:S(2)}, u32[]{:S(2)}) collective-permute-start(bf16[1024,128]{1,0:T(8,128)(2,1)S(1)} %collective-permute-done.23.refs_2_), channel_id=1, source_target_pairs={{0,32},{32,0},{1,33},{33,1},{2,34},{34,2},{3,35},{35,3},{4,36},{36... | collective-permute-start | bytes 786440 | tf_op jit(solution)/shard_map/ppermute | solution.py:222
  78.8 1.8 %collective-permute-start.29 = (bf16[1024,128]{1,0:T(8,128)(2,1)S(1)}, bf16[1024,128]{1,0:T(8,128)(2,1)S(1)}, u32[]{:S(2)}, u32[]{:S(2)}) collective-permute-start(bf16[1024,128]{1,0:T(8,128)(2,1)S(1)} %collective-permute-done.24.refs_3_), channel_id=1, source_target_pairs={{0,32},{32,0},{1,33},{33,1},{2,34},{34,2},{3,35},{35,3},{4,36},{36... | collective-permute-start | bytes 786440 | tf_op jit(solution)/shard_map/ppermute | solution.py:222

commit v7 on v6

--- a/solution.py
+++ b/solution.py
@@ -137,13 +137,11 @@
                 blocks[side, h, 48 * zl : 48 * zl + 48, :] = jnp.concatenate(parts, axis=-1)
 
 
-def relay_kernel(up_0, up_1, down_0, down_1, half_0, half_1, half_2, half_3, everything):
+def relay_kernel(up_0, up_1, down_0, down_1, half_0, half_1, half_2, half_3):
     half_0[...] = up_0[0:1024]
     half_1[...] = up_1[0:1024]
     half_2[...] = down_0[1024:2048]
     half_3[...] = down_1[1024:2048]
-    for k, piece in enumerate((up_0, up_1, down_0, down_1)):
-        everything[2048 * k : 2048 * k + 2048] = piece[...]
 
 
 def stash_kernel(base, kept, sems):
@@ -210,7 +208,7 @@
 def pick_near(refs, side, d, h, inner):
     if side == 0:
         return refs[2 * d + h], 512 * inner
-    return refs[4], 2048 * (2 * d + h) + 512 * inner
+    return refs[4 + 2 * d + h], 512 * inner
 
 
 def pick_far(refs, side, d, h, inner):
@@ -347,16 +345,16 @@
     merged = merge((0,), pick_first, [*mine, *other], None)
     near, merged, states = lax.optimization_barrier((near, merged, states))
     half = shape((1024, 128), HALF)
-    *relayed, everything = pl.pallas_call(
+    relayed = pl.pallas_call(
         relay_kernel,
-        out_shape=(half,) * 4 + (shape((8192, 128), HALF),),
+        out_shape=(half,) * 4,
         in_specs=[VMEM] * 4,
-        out_specs=(VMEM,) * 5,
+        out_specs=(VMEM,) * 4,
         compiler_params=limit(8),
     )(*near)
     far = [hop(relayed[2 * s + h], second[h], 3 - 2 * s) for s in range(2) for h in range(2)]
-    near_other = hop(everything, "core", 1)
-    merged = merge((1, 3), pick_near, [*near, near_other], merged)
+    near_other = [hop(v, "core", 1) for v in near]
+    merged = merge((1, 3), pick_near, [*near, *near_other], merged)
     far, merged = lax.optimization_barrier((far, merged))
     far_other = [hop(v, "core", 1) for v in far]
     merged = merge((2,), pick_far, far + far_other, merged)

time: 83.4 us -> 84.5 us (1.013)
  starting transfers between devices: 39.5 us -> 41.4 us
    ppermute x30 -> x33, starting transfers between devices: 39.5 us -> 41.4 us  [hop(): return lax.ppermute(value, axis, [(i, i ^ k) for i in range(n)])]
    ppermute x30 -> x33, waiting for transfers between devices: 24 us -> 23.3 us  [hop(): return lax.ppermute(value, axis, [(i, i ^ k) for i in range(n)])]
  transfers between devices with their start and end apart: 30 -> 33, of which waited for: 19 -> 20; matrix products, arithmetic and copies ran while one was open for 0% -> 0% of each run, Pallas kernels for 14% -> 14%
where the time goes in v7:
time: 84.5 us; the launch traced here: 84.3 us
  starting transfers between devices  41.4 us (49%)
  waiting for transfers between devices  23.3 us (28%)
  Pallas kernels  17.7 us (21%)
  between operations  0.93 us (1%)
    ppermute x33, starting transfers between devices, hop(): return lax.ppermute(value, axis, [(i, i ^ k) for i in range(n)])  41.4 us
    ppermute x33, waiting for transfers between devices, hop(): return lax.ppermute(value, axis, [(i, i ^ k) for i in range(n)])  23.3 us
    pallas_call x3, Pallas kernels, merge(): pl.pallas_call(functools.partial(next_merge_kernel if before else merge_k...  9.52 us
    pallas_call x1, Pallas kernels, per_device(): pl.pallas_call(stash_kernel, out_shape=pltpu.VMEM((4, 2, 2, 48, 4096), HA...  2.92 us
    pallas_call x1, Pallas kernels, per_device(): pl.pallas_call(pack_kernel, out_shape=[pltpu.VMEM((4, 176, 128), f32), pl...  1.9 us
    pallas_call x1, Pallas kernels, per_device(): pl.pallas_call(state_kernel, out_shape=(sa, sb, sa, sa, sb, sb), in_specs...  1.77 us
  transfers between devices with their start and end apart: 33, of which 20 were waited for; matrix products, arithmetic and copies ran while one was open for 0% of the time, Pallas kernels for 14%

profile of v7, /device:TPU:1, one launch (start us, length us, event | category | flops | bytes accessed | tf_op | source)
XLA Modules:
  0.0 84.3 jit_solution(2760363902633318349)
XLA Ops:
  0.6 0.1 pad_add_fusion
  0.7 1.9 %shard_map.144 = (f32[4,176,128]{2,1,0:T(8,128)S(1)}, bf16[4,176,128]{2,1,0:T(8,128)(2,1)S(1)}, f32[2,64,128]{2,1,0:T(8,128)S(1)}, f32[2,48,64]{2,1,0:T(8,128)S(...) custom-call(s32[2]{0:T(128)S(1)} %get-tuple-element.128.place, ...), custom_call_target="tpu_custom_call" | custom-call | tf_op jit(solution)/shard_map/pallas_call | solution.py:237
  2.6 3.3 %collective-permute-start = (bf16[4,176,128]{2,1,0:T(8,128)(2,1)S(1)}, bf16[4,176,128]{2,1,0:T(8,128)(2,1)S(1)}, u32[]{:S(2)}, u32[]{:S(2)}) collective-permute-start(bf16[4,176,128]{2,1,0:T(8,128)(2,1)S(1)} %get-tuple-element.68), channel_id=1, source_target_pairs={{0,32},{32,0},{1,33},{33,1},{2,34},{34,2},{3,35},{35,3},{4,36},{36... | collective-permute-start | bytes 540680 | tf_op jit(solution)/shard_map/ppermute | solution.py:220
  6.0 1.0 %collective-permute-done.given = bf16[4,176,128]{2,1,0:T(8,128)(2,1)S(1)} collective-permute-done((bf16[4,176,128]{2,1,0:T(8,128)(2,1)S(1)}, bf16[4,176,128]{2,1,0:T(8,128)(2,1)S(1)}, u32[]{:S(2)}, u32[]{:S(2)}) %collective-permute-start) | collective-permute-done | bytes 180256 | tf_op jit(solution)/shard_map/ppermute | solution.py:220
  7.0 0.6 shard_map.145
  7.6 0.1 collective-permute-start.1
  7.7 2.9 %collective-permute-start.2 = (bf16[176,128]{1,0:T(8,128)(2,1)S(1)}, bf16[176,128]{1,0:T(8,128)(2,1)S(1)}, u32[]{:S(2)}, u32[]{:S(2)}) collective-permute-start(bf16[176,128]{1,0:T(8,128)(2,1)S(1)} %get-tuple-element.71), channel_id=1, source_target_pairs={{0,128},{64,192},{128,0},{192,64},{1,129},{65,193},{129,1},{193,65... | collective-permute-start | bytes 135176 | tf_op jit(solution)/shard_map/ppermute | solution.py:220
  10.6 0.7 collective-permute-start.3
  11.2 0.8 collective-permute-done.2.got_2
  12.0 3.3 %collective-permute-done.3.got_3 = bf16[176,128]{1,0:T(8,128)(2,1)S(1)} collective-permute-done((bf16[176,128]{1,0:T(8,128)(2,1)S(1)}, bf16[176,128]{1,0:T(8,128)(2,1)S(1)}, u32[]{:S(2)}, u32[]{:S(2)}) %collective-permute-start.3) | collective-permute-done | bytes 45088 | tf_op jit(solution)/shard_map/ppermute | solution.py:220
  15.3 0.2 shard_map.146
  15.5 4.3 %collective-permute-start.4 = (bf16[128,128]{1,0:T(8,128)(2,1)S(1)}, bf16[128,128]{1,0:T(8,128)(2,1)S(1)}, u32[]{:S(2)}, u32[]{:S(2)}) collective-permute-start(bf16[128,128]{1,0:T(8,128)(2,1)S(1)} %get-tuple-element.83), channel_id=1, source_target_pairs={{0,1},{1,0},{2,3},{3,2},{4,5},{5,4},{6,7},{7,6},{8,9},{9,8},{10,11... | collective-permute-start | bytes 98312 | tf_op jit(solution)/shard_map/ppermute | solution.py:220
  19.8 2.4 %collective-permute-done.4.across = bf16[128,128]{1,0:T(8,128)(2,1)S(1)} collective-permute-done((bf16[128,128]{1,0:T(8,128)(2,1)S(1)}, bf16[128,128]{1,0:T(8,128)(2,1)S(1)}, u32[]{:S(2)}, u32[]{:S(2)}) %collective-permute-start.4) | collective-permute-done | bytes 32800 | tf_op jit(solution)/shard_map/ppermute | solution.py:220
  22.2 0.8 collective-permute-start.7
  23.0 0.1 collective-permute-start.6
  23.1 2.6 %collective-permute-start.5 = (bf16[304,128]{1,0:T(8,128)(2,1)S(1)}, bf16[304,128]{1,0:T(8,128)(2,1)S(1)}, u32[]{:S(2)}, u32[]{:S(2)}) collective-permute-start(bf16[304,128]{1,0:T(8,128)(2,1)S(1)} %shard_map.147.refs_0_), channel_id=1, source_target_pairs={{0,64},{64,0},{128,192},{192,128},{1,65},{65,1},{129,193},{193,129... | collective-permute-start | bytes 233480 | tf_op jit(solution)/shard_map/ppermute | solution.py:220
  25.8 1.7 %collective-permute-done.7.refs_3_ = bf16[304,128]{1,0:T(8,128)(2,1)S(1)} collective-permute-done((bf16[304,128]{1,0:T(8,128)(2,1)S(1)}, bf16[304,128]{1,0:T(8,128)(2,1)S(1)}, u32[]{:S(2)}, u32[]{:S(2)}) %collective-permute-start.7) | collective-permute-done | bytes 77856 | tf_op jit(solution)/shard_map/ppermute | solution.py:220
  27.4 2.0 %collective-permute-done.6.refs_2_ = bf16[304,128]{1,0:T(8,128)(2,1)S(1)} collective-permute-done((bf16[304,128]{1,0:T(8,128)(2,1)S(1)}, bf16[304,128]{1,0:T(8,128)(2,1)S(1)}, u32[]{:S(2)}, u32[]{:S(2)}) %collective-permute-start.6) | collective-permute-done | bytes 77856 | tf_op jit(solution)/shard_map/ppermute | solution.py:220
  29.4 0.6 shard_map.148
  30.0 2.7 %collective-permute-start.13 = (bf16[512,128]{1,0:T(8,128)(2,1)S(1)}, bf16[512,128]{1,0:T(8,128)(2,1)S(1)}, u32[]{:S(2)}, u32[]{:S(2)}) collective-permute-start(bf16[512,128]{1,0:T(8,128)(2,1)S(1)} %bitcast.13), channel_id=1, source_target_pairs={{0,16},{8,24},{16,0},{24,8},{1,17},{9,25},{17,1},{25,9},{2,18},{10... | collective-permute-start | bytes 393224 | tf_op jit(solution)/shard_map/ppermute | solution.py:220
  32.7 0.8 collective-permute-start.11
  33.5 2.7 %collective-permute-start.12 = (bf16[512,128]{1,0:T(8,128)(2,1)S(1)}, bf16[512,128]{1,0:T(8,128)(2,1)S(1)}, u32[]{:S(2)}, u32[]{:S(2)}) collective-permute-start(bf16[512,128]{1,0:T(8,128)(2,1)S(1)} %bitcast.9), channel_id=1, source_target_pairs={{0,4},{2,6},{4,0},{6,2},{1,5},{3,7},{5,1},{7,3},{8,12},{10,14},{12... | collective-permute-start | bytes 393224 | tf_op jit(solution)/shard_map/ppermute | solution.py:220
  36.2 0.9 %collective-permute-start.10 = (bf16[512,128]{1,0:T(8,128)(2,1)S(1)}, bf16[512,128]{1,0:T(8,128)(2,1)S(1)}, u32[]{:S(2)}, u32[]{:S(2)}) collective-permute-start(bf16[512,128]{1,0:T(8,128)(2,1)S(1)} %bitcast.10), channel_id=1, source_target_pairs={{0,6},{2,4},{4,2},{6,0},{1,7},{3,5},{5,3},{7,1},{8,14},{10,12},{12... | collective-permute-start | bytes 393224 | tf_op jit(solution)/shard_map/ppermute | solution.py:220
  37.1 0.6 collective-permute-done.11.refs_7_
  37.7 1.4 %collective-permute-done.12.refs_2_ = bf16[512,128]{1,0:T(8,128)(2,1)S(1)} collective-permute-done((bf16[512,128]{1,0:T(8,128)(2,1)S(1)}, bf16[512,128]{1,0:T(8,128)(2,1)S(1)}, u32[]{:S(2)}, u32[]{:S(2)}) %collective-permute-start.12) | collective-permute-done | bytes 131104 | tf_op jit(solution)/shard_map/ppermute | solution.py:220
  39.1 2.5 %collective-permute-done.10.refs_3_ = bf16[512,128]{1,0:T(8,128)(2,1)S(1)} collective-permute-done((bf16[512,128]{1,0:T(8,128)(2,1)S(1)}, bf16[512,128]{1,0:T(8,128)(2,1)S(1)}, u32[]{:S(2)}, u32[]{:S(2)}) %collective-permute-start.10) | collective-permute-done | bytes 131104 | tf_op jit(solution)/shard_map/ppermute | solution.py:220
  41.5 0.1 shard_map.149
  41.6 5.8 %collective-permute-start.20 = (bf16[2048,128]{1,0:T(8,128)(2,1)S(1)}, bf16[2048,128]{1,0:T(8,128)(2,1)S(1)}, u32[]{:S(2)}, u32[]{:S(2)}) collective-permute-start(bf16[2048,128]{1,0:T(8,128)(2,1)S(1)} %get-tuple-element.97.refs_1_), channel_id=1, source_target_pairs={{0,32},{32,0},{1,33},{33,1},{2,34},{34,2},{3,35},{35,3},{4,36},{36... | collective-permute-start | bytes 1572872 | tf_op jit(solution)/shard_map/ppermute | solution.py:220
  47.4 0.1 collective-permute-start.18
  47.5 1.7 %collective-permute-start.17 = (bf16[2048,128]{1,0:T(8,128)(2,1)S(1)}, bf16[2048,128]{1,0:T(8,128)(2,1)S(1)}, u32[]{:S(2)}, u32[]{:S(2)}) collective-permute-start(bf16[2048,128]{1,0:T(8,128)(2,1)S(1)} %get-tuple-element.97.refs_1_), channel_id=1, source_target_pairs={{0,6},{2,4},{4,2},{6,0},{1,7},{3,5},{5,3},{7,1},{8,14},{10,12},{12... | collective-permute-start | bytes 1572872 | tf_op jit(solution)/shard_map/ppermute | solution.py:220
  49.2 0.7 collective-permute-start.19
  49.9 2.0 %collective-permute-start.16 = (bf16[2048,128]{1,0:T(8,128)(2,1)S(1)}, bf16[2048,128]{1,0:T(8,128)(2,1)S(1)}, u32[]{:S(2)}, u32[]{:S(2)}) collective-permute-start(bf16[2048,128]{1,0:T(8,128)(2,1)S(1)} %get-tuple-element.96.refs_0_), channel_id=1, source_target_pairs={{0,24},{8,16},{16,8},{24,0},{1,25},{9,17},{17,9},{25,1},{2,26},{10... | collective-permute-start | bytes 1572872 | tf_op jit(solution)/shard_map/ppermute | solution.py:220
  51.9 0.8 copy-done
  52.7 1.1 %collective-permute-start.14 = (bf16[2048,128]{1,0:T(8,128)(2,1)S(1)}, bf16[2048,128]{1,0:T(8,128)(2,1)S(1)}, u32[]{:S(2)}, u32[]{:S(2)}) collective-permute-start(bf16[2048,128]{1,0:T(8,128)(2,1)S(1)} %get-tuple-element.96.refs_0_), channel_id=1, source_target_pairs={{0,8},{8,0},{16,24},{24,16},{1,9},{9,1},{17,25},{25,17},{2,10},{10... | collective-permute-start | bytes 1572872 | tf_op jit(solution)/shard_map/ppermute | solution.py:220
  53.8 0.1 pad_add_fusion.2.place
  53.9 1.8 %shard_map.153 = (f32[2,64,128]{2,1,0:T(8,128)}, f32[2,48,64]{2,1,0:T(8,128)}, f32[2,64,128]{2,1,0:T(8,128)}, f32[2,64,128]{2,1,0:T(8,128)}, f32[2,48,64]{2,1,0:T(8,128)}, /*index=5*/f32[2,48,64]{2,1,0:T(8,128)}) custom-call(f32[176,128]{1,0:T(8,128)S(1)} %get-tuple-element.100.total, f32[2,64,128]{2,1,0:T(8,128)} %refs_0_.3, f32[2,48,64]{2,1,0:T(8,128)} %refs_1_.3, ...), custom_call_target="tpu_custom_call" | custom-call | bytes 1024 | tf_op jit(solution)/shard_map/pallas_call | solution.py:315
  55.6 0.1 shard_map.150.blocks
  55.7 0.0 copy-start.1
  55.8 2.9 %shard_map.151.base = bf16[4,2,2,48,4096]{4,3,2,1,0:T(8,128)(2,1)S(1)} custom-call(bf16[4,2,2,48,4096]{4,3,2,1,0:T(8,128)(2,1)} %bitcast.18), custom_call_target="tpu_custom_call" | custom-call | bytes 1024 | tf_op jit(solution)/shard_map/pallas_call | solution.py:299
  58.7 3.1 %shard_map.152.refs_8_ = bf16[4,2,2,48,4096]{4,3,2,1,0:T(8,128)(2,1)} custom-call(s32[3]{0:T(128)S(1)} %pad_add_fusion.2.place, bf16[2,2,192,256]{3,2,1,0:T(8,128)(2,1)S(1)} %shard_map.150.blocks, bf16[4,2,2,48,4096]{4,3,2,1,0:T(8,128)(2,1)S(1)} %shard_map.151.base, bf16[2048,128]{1,0:T(8,128)(2,1)S(1)} %get-tuple-element.96.refs_0_, ...), custom_call_target="tpu_custom_call" | custom-call | bytes 1024 | tf_op jit(solution)/shard_map/pallas_call | solution.py:330
  61.8 0.0 collective-permute-done.17.down_1.refs_3_
  61.8 1.7 %collective-permute-done.15.up_1.refs_1_ = bf16[2048,128]{1,0:T(8,128)(2,1)S(1)} collective-permute-done((bf16[2048,128]{1,0:T(8,128)(2,1)S(1)}, bf16[2048,128]{1,0:T(8,128)(2,1)S(1)}, u32[]{:S(2)}, u32[]{:S(2)}) %collective-permute-start.15) | collective-permute-done | bytes 524320 | tf_op jit(solution)/shard_map/ppermute | solution.py:220
  63.5 1.1 %collective-permute-done.16.down_0.refs_2_ = bf16[2048,128]{1,0:T(8,128)(2,1)S(1)} collective-permute-done((bf16[2048,128]{1,0:T(8,128)(2,1)S(1)}, bf16[2048,128]{1,0:T(8,128)(2,1)S(1)}, u32[]{:S(2)}, u32[]{:S(2)}) %collective-permute-start.16) | collective-permute-done | bytes 524320 | tf_op jit(solution)/shard_map/ppermute | solution.py:220
  64.6 1.2 %collective-permute-done.14.up_0.refs_0_ = bf16[2048,128]{1,0:T(8,128)(2,1)S(1)} collective-permute-done((bf16[2048,128]{1,0:T(8,128)(2,1)S(1)}, bf16[2048,128]{1,0:T(8,128)(2,1)S(1)}, u32[]{:S(2)}, u32[]{:S(2)}) %collective-permute-start.14) | collective-permute-done | bytes 524320 | tf_op jit(solution)/shard_map/ppermute | solution.py:220
  65.9 1.2 %collective-permute-start.25 = (bf16[2048,128]{1,0:T(8,128)(2,1)S(1)}, bf16[2048,128]{1,0:T(8,128)(2,1)S(1)}, u32[]{:S(2)}, u32[]{:S(2)}) collective-permute-start(bf16[2048,128]{1,0:T(8,128)(2,1)S(1)} %collective-permute-done.14.up_0.refs_0_), channel_id=1, source_target_pairs={{0,32},{32,0},{1,33},{33,1},{2,34},{34,2},{3,35},{35,3},{4,36},{36... | collective-permute-start | bytes 1572872 | tf_op jit(solution)/shard_map/ppermute | solution.py:220
  67.1 0.0 collective-permute-start.26
  67.1 0.5 collective-permute-start.27
  67.6 0.1 shard_map.154
  67.6 0.8 collective-permute-start.21
  68.4 0.2 collective-permute-done.25.refs_4_
  68.6 0.9 %collective-permute-start.22 = (bf16[1024,128]{1,0:T(8,128)(2,1)S(1)}, bf16[1024,128]{1,0:T(8,128)(2,1)S(1)}, u32[]{:S(2)}, u32[]{:S(2)}) collective-permute-start(bf16[1024,128]{1,0:T(8,128)(2,1)S(1)} %get-tuple-element.118), channel_id=1, source_target_pairs={{0,6},{2,4},{4,2},{6,0},{1,7},{3,5},{5,3},{7,1},{8,14},{10,12},{12... | collective-permute-start | bytes 786440 | tf_op jit(solution)/shard_map/ppermute | solution.py:220
  69.5 1.1 %collective-permute-start.23 = (bf16[1024,128]{1,0:T(8,128)(2,1)S(1)}, bf16[1024,128]{1,0:T(8,128)(2,1)S(1)}, u32[]{:S(2)}, u32[]{:S(2)}) collective-permute-start(bf16[1024,128]{1,0:T(8,128)(2,1)S(1)} %get-tuple-element.119), channel_id=1, source_target_pairs={{0,8},{8,0},{16,24},{24,16},{1,9},{9,1},{17,25},{25,17},{2,10},{10... | collective-permute-start | bytes 786440 | tf_op jit(solution)/shard_map/ppermute | solution.py:220
  70.6 1.3 %collective-permute-start.24 = (bf16[1024,128]{1,0:T(8,128)(2,1)S(1)}, bf16[1024,128]{1,0:T(8,128)(2,1)S(1)}, u32[]{:S(2)}, u32[]{:S(2)}) collective-permute-start(bf16[1024,128]{1,0:T(8,128)(2,1)S(1)} %get-tuple-element.120), channel_id=1, source_target_pairs={{0,2},{2,0},{4,6},{6,4},{1,3},{3,1},{5,7},{7,5},{8,10},{10,8},{12,... | collective-permute-start | bytes 786440 | tf_op jit(solution)/shard_map/ppermute | solution.py:220
  71.9 3.9 %shard_map.155.refs_8_ = bf16[4,2,2,48,4096]{4,3,2,1,0:T(8,128)(2,1)} custom-call(s32[3]{0:T(128)S(1)} %pad_add_fusion.2.place, bf16[2,2,192,256]{3,2,1,0:T(8,128)(2,1)S(1)} %shard_map.150.blocks, bf16[4,2,2,48,4096]{4,3,2,1,0:T(8,128)(2,1)S(1)} %shard_map.151.base, ...), custom_call_target="tpu_custom_call", output_to_operand_aliasing={{}: (11, {})} | custom-call | bytes 1024 | tf_op jit(solution)/shard_map/pallas_call | solution.py:330
  75.8 0.5 collective-permute-done.21.refs_0_
  76.3 0.7 collective-permute-done.22.refs_1_
  77.0 0.4 collective-permute-done.24.refs_3_
  77.5 1.8 %collective-permute-start.29 = (bf16[1024,128]{1,0:T(8,128)(2,1)S(1)}, bf16[1024,128]{1,0:T(8,128)(2,1)S(1)}, u32[]{:S(2)}, u32[]{:S(2)}) collective-permute-start(bf16[1024,128]{1,0:T(8,128)(2,1)S(1)} %collective-permute-done.21.refs_0_), channel_id=1, source_target_pairs={{0,32},{32,0},{1,33},{33,1},{2,34},{34,2},{3,35},{35,3},{4,36},{36... | collective-permute-start | bytes 786440 | tf_op jit(solution)/shard_map/ppermute | solution.py:220
  79.3 0.5 collective-permute-start.31
  79.8 0.6 collective-permute-done.29.refs_4_
  80.5 0.4 collective-permute-done.30.refs_5_
  80.9 0.4 collective-permute-done.31.refs_6_
  81.2 0.4 collective-permute-done.32.refs_7_
  81.6 2.5 %shard_map.156 = bf16[4,2,2,48,4096]{4,3,2,1,0:T(8,128)(2,1)} custom-call(s32[3]{0:T(128)S(1)} %pad_add_fusion.2.place, bf16[2,2,192,256]{3,2,1,0:T(8,128)(2,1)S(1)} %shard_map.150.blocks, bf16[4,2,2,48,4096]{4,3,2,1,0:T(8,128)(2,1)S(1)} %shard_map.151.base, bf16[1024,128]{1,0:T(8,128)(2,1)S(1)} %collective-permute-done.21.refs_0_, ...), custom_call_target="tpu_custom_call", output_to_operand_aliasing={{}: (11, {})} | custom-call | bytes 1024 | tf_op jit(solution)/shard_map/pallas_call | solution.py:330
  (21 shorter events, 0.1 us)
Async XLA Ops:
  2.6 4.4 %collective-permute-start = (bf16[4,176,128]{2,1,0:T(8,128)(2,1)S(1)}, bf16[4,176,128]{2,1,0:T(8,128)(2,1)S(1)}, u32[]{:S(2)}, u32[]{:S(2)}) collective-permute-start(bf16[4,176,128]{2,1,0:T(8,128)(2,1)S(1)} %get-tuple-element.68), channel_id=1, source_target_pairs={{0,32},{32,0},{1,33},{33,1},{2,34},{34,2},{3,35},{35,3},{4,36},{36... | collective-permute-start | bytes 540680 | tf_op jit(solution)/shard_map/ppermute | solution.py:220
  7.6 3.6 %collective-permute-start.1 = (bf16[176,128]{1,0:T(8,128)(2,1)S(1)}, bf16[176,128]{1,0:T(8,128)(2,1)S(1)}, u32[]{:S(2)}, u32[]{:S(2)}) collective-permute-start(bf16[176,128]{1,0:T(8,128)(2,1)S(1)} %get-tuple-element.70), channel_id=1, source_target_pairs={{0,64},{64,0},{128,192},{192,128},{1,65},{65,1},{129,193},{193,129... | collective-permute-start | bytes 135176 | tf_op jit(solution)/shard_map/ppermute | solution.py:220
  7.7 4.3 %collective-permute-start.2 = (bf16[176,128]{1,0:T(8,128)(2,1)S(1)}, bf16[176,128]{1,0:T(8,128)(2,1)S(1)}, u32[]{:S(2)}, u32[]{:S(2)}) collective-permute-start(bf16[176,128]{1,0:T(8,128)(2,1)S(1)} %get-tuple-element.71), channel_id=1, source_target_pairs={{0,128},{64,192},{128,0},{192,64},{1,129},{65,193},{129,1},{193,65... | collective-permute-start | bytes 135176 | tf_op jit(solution)/shard_map/ppermute | solution.py:220
  10.6 4.7 %collective-permute-start.3 = (bf16[176,128]{1,0:T(8,128)(2,1)S(1)}, bf16[176,128]{1,0:T(8,128)(2,1)S(1)}, u32[]{:S(2)}, u32[]{:S(2)}) collective-permute-start(bf16[176,128]{1,0:T(8,128)(2,1)S(1)} %get-tuple-element.72), channel_id=1, source_target_pairs={{0,192},{64,128},{128,64},{192,0},{1,193},{65,129},{129,65},{193,1... | collective-permute-start | bytes 135176 | tf_op jit(solution)/shard_map/ppermute | solution.py:220
  15.5 6.7 %collective-permute-start.4 = (bf16[128,128]{1,0:T(8,128)(2,1)S(1)}, bf16[128,128]{1,0:T(8,128)(2,1)S(1)}, u32[]{:S(2)}, u32[]{:S(2)}) collective-permute-start(bf16[128,128]{1,0:T(8,128)(2,1)S(1)} %get-tuple-element.83), channel_id=1, source_target_pairs={{0,1},{1,0},{2,3},{3,2},{4,5},{5,4},{6,7},{7,6},{8,9},{9,8},{10,11... | collective-permute-start | bytes 98312 | tf_op jit(solution)/shard_map/ppermute | solution.py:220
  22.2 5.2 %collective-permute-start.7 = (bf16[304,128]{1,0:T(8,128)(2,1)S(1)}, bf16[304,128]{1,0:T(8,128)(2,1)S(1)}, u32[]{:S(2)}, u32[]{:S(2)}) collective-permute-start(bf16[304,128]{1,0:T(8,128)(2,1)S(1)} %shard_map.147.refs_0_), channel_id=1, source_target_pairs={{0,192},{64,128},{128,64},{192,0},{1,193},{65,129},{129,65},{193,1... | collective-permute-start | bytes 233480 | tf_op jit(solution)/shard_map/ppermute | solution.py:220
  23.0 6.4 %collective-permute-start.6 = (bf16[304,128]{1,0:T(8,128)(2,1)S(1)}, bf16[304,128]{1,0:T(8,128)(2,1)S(1)}, u32[]{:S(2)}, u32[]{:S(2)}) collective-permute-start(bf16[304,128]{1,0:T(8,128)(2,1)S(1)} %shard_map.147.refs_0_), channel_id=1, source_target_pairs={{0,128},{64,192},{128,0},{192,64},{1,129},{65,193},{129,1},{193,65... | collective-permute-start | bytes 233480 | tf_op jit(solution)/shard_map/ppermute | solution.py:220
  23.1 6.3 %collective-permute-start.5 = (bf16[304,128]{1,0:T(8,128)(2,1)S(1)}, bf16[304,128]{1,0:T(8,128)(2,1)S(1)}, u32[]{:S(2)}, u32[]{:S(2)}) collective-permute-start(bf16[304,128]{1,0:T(8,128)(2,1)S(1)} %shard_map.147.refs_0_), channel_id=1, source_target_pairs={{0,64},{64,0},{128,192},{192,128},{1,65},{65,1},{129,193},{193,129... | collective-permute-start | bytes 233480 | tf_op jit(solution)/shard_map/ppermute | solution.py:220
  30.0 7.1 %collective-permute-start.13 = (bf16[512,128]{1,0:T(8,128)(2,1)S(1)}, bf16[512,128]{1,0:T(8,128)(2,1)S(1)}, u32[]{:S(2)}, u32[]{:S(2)}) collective-permute-start(bf16[512,128]{1,0:T(8,128)(2,1)S(1)} %bitcast.13), channel_id=1, source_target_pairs={{0,16},{8,24},{16,0},{24,8},{1,17},{9,25},{17,1},{25,9},{2,18},{10... | collective-permute-start | bytes 393224 | tf_op jit(solution)/shard_map/ppermute | solution.py:220
  32.7 5.0 %collective-permute-start.11 = (bf16[512,128]{1,0:T(8,128)(2,1)S(1)}, bf16[512,128]{1,0:T(8,128)(2,1)S(1)}, u32[]{:S(2)}, u32[]{:S(2)}) collective-permute-start(bf16[512,128]{1,0:T(8,128)(2,1)S(1)} %bitcast.14), channel_id=1, source_target_pairs={{0,24},{8,16},{16,8},{24,0},{1,25},{9,17},{17,9},{25,1},{2,26},{10... | collective-permute-start | bytes 393224 | tf_op jit(solution)/shard_map/ppermute | solution.py:220
  33.4 4.3 %collective-permute-start.9 = (bf16[512,128]{1,0:T(8,128)(2,1)S(1)}, bf16[512,128]{1,0:T(8,128)(2,1)S(1)}, u32[]{:S(2)}, u32[]{:S(2)}) collective-permute-start(bf16[512,128]{1,0:T(8,128)(2,1)S(1)} %bitcast.15), channel_id=1, source_target_pairs={{0,8},{8,0},{16,24},{24,16},{1,9},{9,1},{17,25},{25,17},{2,10},{10... | collective-permute-start | bytes 393224 | tf_op jit(solution)/shard_map/ppermute | solution.py:220
  33.5 5.6 %collective-permute-start.12 = (bf16[512,128]{1,0:T(8,128)(2,1)S(1)}, bf16[512,128]{1,0:T(8,128)(2,1)S(1)}, u32[]{:S(2)}, u32[]{:S(2)}) collective-permute-start(bf16[512,128]{1,0:T(8,128)(2,1)S(1)} %bitcast.9), channel_id=1, source_target_pairs={{0,4},{2,6},{4,0},{6,2},{1,5},{3,7},{5,1},{7,3},{8,12},{10,14},{12... | collective-permute-start | bytes 393224 | tf_op jit(solution)/shard_map/ppermute | solution.py:220
  36.2 5.3 %collective-permute-start.10 = (bf16[512,128]{1,0:T(8,128)(2,1)S(1)}, bf16[512,128]{1,0:T(8,128)(2,1)S(1)}, u32[]{:S(2)}, u32[]{:S(2)}) collective-permute-start(bf16[512,128]{1,0:T(8,128)(2,1)S(1)} %bitcast.10), channel_id=1, source_target_pairs={{0,6},{2,4},{4,2},{6,0},{1,7},{3,5},{5,3},{7,1},{8,14},{10,12},{12... | collective-permute-start | bytes 393224 | tf_op jit(solution)/shard_map/ppermute | solution.py:220
  37.1 4.5 %collective-permute-start.8 = (bf16[512,128]{1,0:T(8,128)(2,1)S(1)}, bf16[512,128]{1,0:T(8,128)(2,1)S(1)}, u32[]{:S(2)}, u32[]{:S(2)}) collective-permute-start(bf16[512,128]{1,0:T(8,128)(2,1)S(1)} %bitcast.11), channel_id=1, source_target_pairs={{0,2},{2,0},{4,6},{6,4},{1,3},{3,1},{5,7},{7,5},{8,10},{10,8},{12,... | collective-permute-start | bytes 393224 | tf_op jit(solution)/shard_map/ppermute | solution.py:220
  41.6 10.3 %collective-permute-start.20 = (bf16[2048,128]{1,0:T(8,128)(2,1)S(1)}, bf16[2048,128]{1,0:T(8,128)(2,1)S(1)}, u32[]{:S(2)}, u32[]{:S(2)}) collective-permute-start(bf16[2048,128]{1,0:T(8,128)(2,1)S(1)} %get-tuple-element.97.refs_1_), channel_id=1, source_target_pairs={{0,32},{32,0},{1,33},{33,1},{2,34},{34,2},{3,35},{35,3},{4,36},{36... | collective-permute-start | bytes 1572872 | tf_op jit(solution)/shard_map/ppermute | solution.py:220
  47.4 2.5 %collective-permute-start.18 = (bf16[4,48,128]{2,1,0:T(8,128)(2,1)S(1)}, bf16[4,48,128]{2,1,0:T(8,128)(2,1)S(1)}, u32[]{:S(2)}, u32[]{:S(2)}) collective-permute-start(bf16[4,48,128]{2,1,0:T(8,128)(2,1)S(1)} %get-tuple-element.98.rows_own), channel_id=1, source_target_pairs={{0,32},{32,0},{1,33},{33,1},{2,34},{34,2},{3,35},{35,3},{4,36},{36... | collective-permute-start | bytes 147464 | tf_op jit(solution)/shard_map/ppermute | solution.py:220
  47.5 14.3 %collective-permute-start.17 = (bf16[2048,128]{1,0:T(8,128)(2,1)S(1)}, bf16[2048,128]{1,0:T(8,128)(2,1)S(1)}, u32[]{:S(2)}, u32[]{:S(2)}) collective-permute-start(bf16[2048,128]{1,0:T(8,128)(2,1)S(1)} %get-tuple-element.97.refs_1_), channel_id=1, source_target_pairs={{0,6},{2,4},{4,2},{6,0},{1,7},{3,5},{5,3},{7,1},{8,14},{10,12},{12... | collective-permute-start | bytes 1572872 | tf_op jit(solution)/shard_map/ppermute | solution.py:220
  49.2 9.4 %collective-permute-start.19 = (bf16[2048,128]{1,0:T(8,128)(2,1)S(1)}, bf16[2048,128]{1,0:T(8,128)(2,1)}, u32[]{:S(2)}, u32[]{:S(2)}) collective-permute-start(bf16[2048,128]{1,0:T(8,128)(2,1)S(1)} %get-tuple-element.96.refs_0_), channel_id=1, source_target_pairs={{0,32},{32,0},{1,33},{33,1},{2,34},{34,2},{3,35},{35,3},{4,36},{36... | collective-permute-start | bytes 1572872 | tf_op jit(solution)/shard_map/ppermute | solution.py:220
  49.9 13.6 %collective-permute-start.15 = (bf16[2048,128]{1,0:T(8,128)(2,1)S(1)}, bf16[2048,128]{1,0:T(8,128)(2,1)S(1)}, u32[]{:S(2)}, u32[]{:S(2)}) collective-permute-start(bf16[2048,128]{1,0:T(8,128)(2,1)S(1)} %get-tuple-element.97.refs_1_), channel_id=1, source_target_pairs={{0,2},{2,0},{4,6},{6,4},{1,3},{3,1},{5,7},{7,5},{8,10},{10,8},{12,... | collective-permute-start | bytes 1572872 | tf_op jit(solution)/shard_map/ppermute | solution.py:220
  49.9 14.7 %collective-permute-start.16 = (bf16[2048,128]{1,0:T(8,128)(2,1)S(1)}, bf16[2048,128]{1,0:T(8,128)(2,1)S(1)}, u32[]{:S(2)}, u32[]{:S(2)}) collective-permute-start(bf16[2048,128]{1,0:T(8,128)(2,1)S(1)} %get-tuple-element.96.refs_0_), channel_id=1, source_target_pairs={{0,24},{8,16},{16,8},{24,0},{1,25},{9,17},{17,9},{25,1},{2,26},{10... | collective-permute-start | bytes 1572872 | tf_op jit(solution)/shard_map/ppermute | solution.py:220
  51.9 0.8 copy-start
  52.7 13.2 %collective-permute-start.14 = (bf16[2048,128]{1,0:T(8,128)(2,1)S(1)}, bf16[2048,128]{1,0:T(8,128)(2,1)S(1)}, u32[]{:S(2)}, u32[]{:S(2)}) collective-permute-start(bf16[2048,128]{1,0:T(8,128)(2,1)S(1)} %get-tuple-element.96.refs_0_), channel_id=1, source_target_pairs={{0,8},{8,0},{16,24},{24,16},{1,9},{9,1},{17,25},{25,17},{2,10},{10... | collective-permute-start | bytes 1572872 | tf_op jit(solution)/shard_map/ppermute | solution.py:220
  55.7 3.0 %copy-start.1 = (bf16[2048,128]{1,0:T(8,128)(2,1)S(1)}, bf16[2048,128]{1,0:T(8,128)(2,1)}, u32[]{:S(2)}) copy-start(bf16[2048,128]{1,0:T(8,128)(2,1)} %copy-done) | copy-start | bytes 1572868
  65.9 2.7 %collective-permute-start.25 = (bf16[2048,128]{1,0:T(8,128)(2,1)S(1)}, bf16[2048,128]{1,0:T(8,128)(2,1)S(1)}, u32[]{:S(2)}, u32[]{:S(2)}) collective-permute-start(bf16[2048,128]{1,0:T(8,128)(2,1)S(1)} %collective-permute-done.14.up_0.refs_0_), channel_id=1, source_target_pairs={{0,32},{32,0},{1,33},{33,1},{2,34},{34,2},{3,35},{35,3},{4,36},{36... | collective-permute-start | bytes 1572872 | tf_op jit(solution)/shard_map/ppermute | solution.py:220
  67.1 2.5 %collective-permute-start.26 = (bf16[2048,128]{1,0:T(8,128)(2,1)S(1)}, bf16[2048,128]{1,0:T(8,128)(2,1)S(1)}, u32[]{:S(2)}, u32[]{:S(2)}) collective-permute-start(bf16[2048,128]{1,0:T(8,128)(2,1)S(1)} %collective-permute-done.15.up_1.refs_1_), channel_id=1, source_target_pairs={{0,32},{32,0},{1,33},{33,1},{2,34},{34,2},{3,35},{35,3},{4,36},{36... | collective-permute-start | bytes 1572872 | tf_op jit(solution)/shard_map/ppermute | solution.py:220
  67.1 3.5 %collective-permute-start.27 = (bf16[2048,128]{1,0:T(8,128)(2,1)S(1)}, bf16[2048,128]{1,0:T(8,128)(2,1)S(1)}, u32[]{:S(2)}, u32[]{:S(2)}) collective-permute-start(bf16[2048,128]{1,0:T(8,128)(2,1)S(1)} %collective-permute-done.16.down_0.refs_2_), channel_id=1, source_target_pairs={{0,32},{32,0},{1,33},{33,1},{2,34},{34,2},{3,35},{35,3},{4,36},{36... | collective-permute-start | bytes 1572872 | tf_op jit(solution)/shard_map/ppermute | solution.py:220
  67.6 4.3 %collective-permute-start.28 = (bf16[2048,128]{1,0:T(8,128)(2,1)S(1)}, bf16[2048,128]{1,0:T(8,128)(2,1)S(1)}, u32[]{:S(2)}, u32[]{:S(2)}) collective-permute-start(bf16[2048,128]{1,0:T(8,128)(2,1)S(1)} %collective-permute-done.17.down_1.refs_3_), channel_id=1, source_target_pairs={{0,32},{32,0},{1,33},{33,1},{2,34},{34,2},{3,35},{35,3},{4,36},{36... | collective-permute-start | bytes 1572872 | tf_op jit(solution)/shard_map/ppermute | solution.py:220
  67.6 8.7 %collective-permute-start.21 = (bf16[1024,128]{1,0:T(8,128)(2,1)S(1)}, bf16[1024,128]{1,0:T(8,128)(2,1)S(1)}, u32[]{:S(2)}, u32[]{:S(2)}) collective-permute-start(bf16[1024,128]{1,0:T(8,128)(2,1)S(1)} %get-tuple-element.117), channel_id=1, source_target_pairs={{0,24},{8,16},{16,8},{24,0},{1,25},{9,17},{17,9},{25,1},{2,26},{10... | collective-permute-start | bytes 786440 | tf_op jit(solution)/shard_map/ppermute | solution.py:220
  68.6 8.4 %collective-permute-start.22 = (bf16[1024,128]{1,0:T(8,128)(2,1)S(1)}, bf16[1024,128]{1,0:T(8,128)(2,1)S(1)}, u32[]{:S(2)}, u32[]{:S(2)}) collective-permute-start(bf16[1024,128]{1,0:T(8,128)(2,1)S(1)} %get-tuple-element.118), channel_id=1, source_target_pairs={{0,6},{2,4},{4,2},{6,0},{1,7},{3,5},{5,3},{7,1},{8,14},{10,12},{12... | collective-permute-start | bytes 786440 | tf_op jit(solution)/shard_map/ppermute | solution.py:220
  69.5 7.5 %collective-permute-start.23 = (bf16[1024,128]{1,0:T(8,128)(2,1)S(1)}, bf16[1024,128]{1,0:T(8,128)(2,1)S(1)}, u32[]{:S(2)}, u32[]{:S(2)}) collective-permute-start(bf16[1024,128]{1,0:T(8,128)(2,1)S(1)} %get-tuple-element.119), channel_id=1, source_target_pairs={{0,8},{8,0},{16,24},{24,16},{1,9},{9,1},{17,25},{25,17},{2,10},{10... | collective-permute-start | bytes 786440 | tf_op jit(solution)/shard_map/ppermute | solution.py:220
  70.6 6.9 %collective-permute-start.24 = (bf16[1024,128]{1,0:T(8,128)(2,1)S(1)}, bf16[1024,128]{1,0:T(8,128)(2,1)S(1)}, u32[]{:S(2)}, u32[]{:S(2)}) collective-permute-start(bf16[1024,128]{1,0:T(8,128)(2,1)S(1)} %get-tuple-element.120), channel_id=1, source_target_pairs={{0,2},{2,0},{4,6},{6,4},{1,3},{3,1},{5,7},{7,5},{8,10},{10,8},{12,... | collective-permute-start | bytes 786440 | tf_op jit(solution)/shard_map/ppermute | solution.py:220
  77.5 3.0 %collective-permute-start.29 = (bf16[1024,128]{1,0:T(8,128)(2,1)S(1)}, bf16[1024,128]{1,0:T(8,128)(2,1)S(1)}, u32[]{:S(2)}, u32[]{:S(2)}) collective-permute-start(bf16[1024,128]{1,0:T(8,128)(2,1)S(1)} %collective-permute-done.21.refs_0_), channel_id=1, source_target_pairs={{0,32},{32,0},{1,33},{33,1},{2,34},{34,2},{3,35},{35,3},{4,36},{36... | collective-permute-start | bytes 786440 | tf_op jit(solution)/shard_map/ppermute | solution.py:220
  79.3 1.5 %collective-permute-start.30 = (bf16[1024,128]{1,0:T(8,128)(2,1)S(1)}, bf16[1024,128]{1,0:T(8,128)(2,1)S(1)}, u32[]{:S(2)}, u32[]{:S(2)}) collective-permute-start(bf16[1024,128]{1,0:T(8,128)(2,1)S(1)} %collective-permute-done.22.refs_1_), channel_id=1, source_target_pairs={{0,32},{32,0},{1,33},{33,1},{2,34},{34,2},{3,35},{35,3},{4,36},{36... | collective-permute-start | bytes 786440 | tf_op jit(solution)/shard_map/ppermute | solution.py:220
  79.3 1.9 %collective-permute-start.31 = (bf16[1024,128]{1,0:T(8,128)(2,1)S(1)}, bf16[1024,128]{1,0:T(8,128)(2,1)S(1)}, u32[]{:S(2)}, u32[]{:S(2)}) collective-permute-start(bf16[1024,128]{1,0:T(8,128)(2,1)S(1)} %collective-permute-done.23.refs_2_), channel_id=1, source_target_pairs={{0,32},{32,0},{1,33},{33,1},{2,34},{34,2},{3,35},{35,3},{4,36},{36... | collective-permute-start | bytes 786440 | tf_op jit(solution)/shard_map/ppermute | solution.py:220
  79.8 1.8 %collective-permute-start.32 = (bf16[1024,128]{1,0:T(8,128)(2,1)S(1)}, bf16[1024,128]{1,0:T(8,128)(2,1)S(1)}, u32[]{:S(2)}, u32[]{:S(2)}) collective-permute-start(bf16[1024,128]{1,0:T(8,128)(2,1)S(1)} %collective-permute-done.24.refs_3_), channel_id=1, source_target_pairs={{0,32},{32,0},{1,33},{33,1},{2,34},{34,2},{3,35},{35,3},{4,36},{36... | collective-permute-start | bytes 786440 | tf_op jit(solution)/shard_map/ppermute | solution.py:220
